TPU v7x, 32 devices: a whole 2x2x4 slice. The times are simulated.
32 devices in a mesh: groups: 2 (over y), sector: 4 (over z), blk: 2 (over x), op: 2 (over core).
Axes of the slice: x: 2, y: 2, z: 4, core: 2. Of those that a mesh axis runs over, the one named last changes fastest.
Arguments:
- psi: bfloat16 [384, 128, 128], P(('groups', 'sector', 'blk')), parts along dimension 0, may hold values from -6 to 6
- left_ops: bfloat16 [128, 2, 128, 128], P(('groups', 'op'), 'blk'), parts along dimension 0, may hold values from -0.0625 to 0.0625
- right_ops: bfloat16 [128, 2, 128, 128], P(('groups', 'op')), parts along dimension 0, may hold values from -0.5 to 0.5
- left_qn: int32 [384], P(('groups', 'sector', 'blk')), parts along dimension 0, may hold values from 0 to 1
- right_qn: int32 [384], P(('groups', 'sector', 'blk')), parts along dimension 0, may hold values from 0 to 1
- pair_slot: int32 [128, 192], P(('groups', 'op'), ('sector', 'blk')), parts along dimension 0, may hold values from 0 to 15
- slot_target: int32 [8, 2, 16], P(('groups', 'sector'), 'blk'), parts along dimension 0, may hold values from 0 to 23
Outputs:
- sigma: float32 [384, 128, 128], P(('groups', 'sector', 'blk')), parts along dimension 0
There are 2 independent parts, one for each index of `groups`. A program takes and returns all parts, laid end to end along the dimension named above; each array names one. Nothing has to cross between parts.
Inputs may be any that keep to these rules, and one draw needn't show every extreme that they name: `pair_slot`: slot c leads to the owner of row c // 4; all pairs of one source device with equal slot have one target.
All inputs are finite; a program needn't handle non-finite values.
Results may differ from a plain program's by a relative error of at most 0.0029.
Values may be sent and summed in bfloat16 or wider, within the bound.
No kernel may reach another device: no remote copies, remote signals or barrier semaphores. Data moves between devices by JAX's collectives and lax.ppermute only.
A program may use at most 64 MiB of HBM per device.

v0:
```python
import jax
import jax.numpy as jnp
from jax import lax
from jax.sharding import PartitionSpec as P

CAP = 4


def shards(psi, left_ops, right_ops, left_qn, right_qn, pair_slot, slot_target):
    sec = psi.shape[0]
    width = psi.shape[1]
    right_count = right_ops.shape[1]
    owners = slot_target.shape[2] // CAP
    gathered = lax.all_gather(left_ops, "blk", axis=1, tiled=True)
    left_count = gathered.shape[1]
    right_match = (right_qn[:, None] == jnp.arange(right_count)[None, :]).astype(jnp.bfloat16)
    left_match = (left_qn[:, None] == jnp.arange(left_count)[None, :]).astype(jnp.bfloat16)

    def one_operator(buffer, inputs):
        left_k, right_k, slots = inputs
        chosen_right = jnp.einsum(
            "sq,qab->sab", right_match, right_k, preferred_element_type=jnp.float32
        ).astype(jnp.bfloat16)
        half_k = jnp.einsum(
            "sab,scb->sac", psi, chosen_right, preferred_element_type=jnp.float32
        ).astype(jnp.bfloat16)
        chosen_left = jnp.einsum(
            "sq,qab->sab", left_match, left_k, preferred_element_type=jnp.float32
        ).astype(jnp.bfloat16)
        term = jnp.einsum("sab,sbc->sac", chosen_left, half_k, preferred_element_type=jnp.float32)
        return (buffer + jax.ops.segment_sum(term, slots, num_segments=owners * CAP), None)

    start = jnp.zeros((owners * CAP, width, width), jnp.float32)
    buffer, unused = lax.scan(one_operator, start, (gathered, right_ops, pair_slot))
    outgoing = buffer.reshape(owners, CAP, width, width)
    target_ids = slot_target[0, 0].reshape(owners, CAP)
    half_cap = CAP // 2
    reduced = lax.psum_scatter(outgoing, "op", scatter_dimension=1, tiled=True)
    my_ids = lax.dynamic_slice_in_dim(target_ids, lax.axis_index("op") * half_cap, half_cap, 1)
    arrived, arrived_ids = (
        lax.all_to_all(reduced, "sector", split_axis=0, concat_axis=0, tiled=True),
        lax.all_to_all(my_ids, "sector", split_axis=0, concat_axis=0, tiled=True),
    )
    local_sigma = jax.ops.segment_sum(
        arrived.reshape(-1, width, width), arrived_ids.reshape(-1), num_segments=sec
    )
    return lax.psum(local_sigma, "op")


def solution(mesh):
    in_specs = (
        P(("groups", "sector", "blk"), None, None),
        P(("groups", "op"), "blk", None, None),
        P(("groups", "op"), None, None, None),
        P(("groups", "sector", "blk")),
        P(("groups", "sector", "blk")),
        P(("groups", "op"), ("sector", "blk")),
        P(("groups", "sector"), "blk", None),
    )
    out_specs = P(("groups", "sector", "blk"), None, None)
    return jax.shard_map(shards, mesh=mesh, in_specs=in_specs, out_specs=out_specs, check_vma=False)
```

profile of v0, /device:TPU:0, one launch (start us, length us, event | category | flops | bytes accessed | tf_op | source)
XLA Modules:
  0.0 395.3 jit_solution(3355287239055552774)
XLA Ops:
  8.1 36.7 %all-gather.2.cloned.1.call-done = bf16[32,2,128,128]{3,2,0,1:T(8,128)(2,1)} async-done(((bf16[32,1,128,128]{3,2,0,1:T(8,128)(2,1)}), bf16[32,2,128,128]{3,2,0,1:T(8,128)(2,1)}) %all-gather.2.cloned.1.call-update) | async-done | bytes 2097168 | tf_op jit(solution)/shard_map/all_gather | solution.py:14
  44.9 276.7 %while.11 = (s32[]{:T(128)}, f32[16,128,128]{2,1,0:T(8,128)S(1)}, s32[32,24]{1,0:T(8,128)S(1)}, bf16[32,2,128,128]{3,2,0,1:T(8,128)(2,1)}, bf16[32,2,128,128]{3,...) while((s32[]{:T(128)}, f32[16,128,128]{2,1,0:T(8,128)S(1)}, ...), condition=%wide.region_2.3_spmd.clone, body=%wide.region_0.2_spmd.clone.sunk | while | flops 206045376 | bytes 10617417 | solution.py:34
  50.9 2.6 scatter_fusion
  76.8 2.6 scatter_fusion
  85.5 2.6 scatter_fusion
  94.1 2.6 scatter_fusion
  102.8 2.6 scatter_fusion
  120.1 2.6 scatter_fusion
  137.4 2.6 scatter_fusion
  146.0 2.6 scatter_fusion
  154.7 2.6 scatter_fusion
  163.3 2.6 scatter_fusion
  172.0 2.6 scatter_fusion
  180.6 2.6 scatter_fusion
  189.3 2.6 scatter_fusion
  197.9 2.6 scatter_fusion
  206.6 2.6 scatter_fusion
  215.2 2.6 scatter_fusion
  223.8 2.6 scatter_fusion
  232.5 2.6 scatter_fusion
  249.8 2.6 scatter_fusion
  267.1 2.6 scatter_fusion
  275.7 2.6 scatter_fusion
  284.4 2.6 scatter_fusion
  293.0 2.6 scatter_fusion
  301.7 2.6 scatter_fusion
  324.4 4.6 %all-to-all-start = ((s32[4,1,2]{2,1,0:T(1,128)}), s32[4,1,2]{2,1,0:T(1,128)S(1)}, u32[]{:S(2)}, u32[]{:S(2)}) async-start(s32[4,1,2]{2,1,0:T(1,128)} %bitcast.17), calls=%async_computation | async-start | bytes 4096 | tf_op jit(solution)/shard_map/all_to_all | solution.py:42
  330.4 12.0 %all-reduce.6.cloned.1.call-done = f32[4,4,128,128]{3,2,1,0:T(8,128)} async-done(((f32[4,4,128,128]{3,2,1,0:T(8,128)}), f32[4,4,128,128]{3,2,1,0:T(8,128)}) %all-reduce.6.cloned.1.call-update) | async-done | bytes 1048592
  344.3 4.9 %all-to-all-start.1 = ((f32[4,2,128,128]{3,2,1,0:T(8,128)}), f32[4,2,128,128]{3,2,1,0:T(8,128)S(1)}, u32[]{:S(2)}, u32[]{:S(2)}) async-start(f32[4,2,128,128]{3,2,1,0:T(8,128)} %constant_dynamic-slice_fusion.3), calls=%async_computation.1 | async-start | bytes 1048576 | tf_op jit(solution)/shard_map/all_to_all | solution.py:41
  349.8 14.3 %all-to-all-done.1 = f32[4,2,128,128]{3,2,1,0:T(8,128)S(1)} async-done(((f32[4,2,128,128]{3,2,1,0:T(8,128)}), f32[4,2,128,128]{3,2,1,0:T(8,128)S(1)}, u32[]{:S(2)}, u32[]{:S(2)}) %all-to-all-start.1) | async-done | bytes 524320 | tf_op jit(solution)/shard_map/all_to_all | solution.py:41
  366.5 19.6 %all-reduce.4.cloned.1.call-done = f32[24,128,128]{2,1,0:T(8,128)} async-done(((f32[24,128,128]{2,1,0:T(8,128)}), f32[24,128,128]{2,1,0:T(8,128)}) %all-reduce.4.cloned.1.call-update) | async-done | bytes 1572880 | tf_op jit(solution)/shard_map/psum | solution.py:47
  386.1 2.7 copy.62
  (231 shorter events, 222.2 us)
Async XLA Ops:
  6.5 38.3 %copy-start.2 = (s32[24]{0:T(128)S(1)}, s32[24]{0:T(128)}, u32[]{:S(2)}) copy-start(s32[24]{0:T(128)} %param.12) | copy-start | bytes 292
  6.5 38.3 %copy-start.3 = (s32[24]{0:T(128)S(1)}, s32[24]{0:T(128)}, u32[]{:S(2)}) copy-start(s32[24]{0:T(128)} %param.13) | copy-start | bytes 292
  6.5 38.2 %all-gather.2.cloned.1.call-start = ((), (), s32[]{:S(2)}) async-start(), calls=%async_computation.2 | async-start | bytes 3145728 | tf_op jit(solution)/shard_map/all_gather | solution.py:14
  7.3 335.1 %all-reduce.6.cloned.1.call-start = ((), (), s32[]{:S(2)}) async-start(), calls=%async_computation.4 | async-start | bytes 2097152
  44.9 278.2 %copy-start.4 = (s32[1,1,16]{2,1,0:T(1,128)S(1)}, s32[1,1,16]{2,1,0:T(1,128)}, u32[]{:S(2)}) copy-start(s32[1,1,16]{2,1,0:T(1,128)} %param.15) | copy-start | bytes 196
  44.9 284.2 %copy-start.5 = (u32[32]{0:T(128)S(1)}, u32[32]{0:T(128)}, u32[]{:S(2)}) copy-start(u32[32]{0:T(128)} %constant.31) | copy-start | bytes 388
  321.6 1.0 copy-start
  324.4 19.8 %all-to-all-start = ((s32[4,1,2]{2,1,0:T(1,128)}), s32[4,1,2]{2,1,0:T(1,128)S(1)}, u32[]{:S(2)}, u32[]{:S(2)}) async-start(s32[4,1,2]{2,1,0:T(1,128)} %bitcast.17), calls=%async_computation | async-start | bytes 4096 | tf_op jit(solution)/shard_map/all_to_all | solution.py:42
  344.3 19.8 %all-to-all-start.1 = ((f32[4,2,128,128]{3,2,1,0:T(8,128)}), f32[4,2,128,128]{3,2,1,0:T(8,128)S(1)}, u32[]{:S(2)}, u32[]{:S(2)}) async-start(f32[4,2,128,128]{3,2,1,0:T(8,128)} %constant_dynamic-slice_fusion.3), calls=%async_computation.1 | async-start | bytes 1048576 | tf_op jit(solution)/shard_map/all_to_all | solution.py:41
  349.1 36.9 %all-reduce.4.cloned.1.call-start = ((), (), s32[]{:S(2)}) async-start(), calls=%async_computation.3 | async-start | bytes 3145728 | tf_op jit(solution)/shard_map/psum | solution.py:47
  365.3 1.1 copy-start.1
Sparse Core Ops, SparseCore 0:
  8.9 35.8 all-gather.1
  322.7 19.5 all-reduce.5
  366.6 19.4 all-reduce.3
where the time goes:
time: 399 us; the launch traced here: 395 us
  matrix products  136 us (34%)
  other arithmetic  86.3 us (22%)
  waiting for transfers between devices  83.3 us (21%)
  local copies, waits for them, and re-layouts  64.6 us (16%)
  between operations  13.9 us (3%)
  starting transfers between devices  9.53 us (2%)
    scatter-add x32, other arithmetic, one_operator(): jax.ops.segment_sum(term, slots, num_segments=owners * CAP)  84.1 us
    dot_general x32, matrix products, one_operator(): jnp.einsum('sab,sbc->sac', chosen_left, half_k, preferred_element_type=jn...  82.2 us
    dynamic_slice x64, local copies, waits for them, and re-layouts, shards(): lax.scan(one_operator, start, (gathered, right_ops, pair_slot))  54.5 us
    dot_general x32, matrix products, one_operator(): jnp.einsum('sq,qab->sab', right_match, right_k, preferred_element_type=jn...  41.2 us
    all_gather x1, waiting for transfers between devices, shards(): gathered = lax.all_gather(left_ops, 'blk', axis=1, tiled=True)  36.7 us
    psum x1, waiting for transfers between devices, shards(): return lax.psum(local_sigma, 'op')  19.6 us
    all_to_all x1, waiting for transfers between devices, shards(): lax.all_to_all(reduced, 'sector', split_axis=0, concat_axis=0, tiled=True)  14.3 us
    dot_general x32, matrix products, one_operator(): jnp.einsum('sq,qab->sab', left_match, left_k, preferred_element_type=jnp....  12.9 us
  transfers between devices with their start and end apart: 5, of which 4 were waited for; matrix products, arithmetic and copies ran while one was open for 1% of the time, Pallas kernels for 0%

commit v1 on v0

v1 whole, which is shorter than its diff:
```python
import functools

import jax
import jax.numpy as jnp
from jax import lax
from jax.experimental import pallas as pl
from jax.experimental.pallas import tpu as pltpu
from jax.sharding import PartitionSpec as P

CAP = 4
GROUP = 4
BLOCK_K = 16
NT = (((1,), (1,)), ((), ()))


def pick(left_qn, order, wanted):
    count = left_qn.shape[0]

    def step(s, n):
        order[n] = s
        return n + (left_qn[s] == wanted).astype(jnp.int32)

    n = lax.fori_loop(0, count, step, jnp.int32(0))
    for extra in range(GROUP - 1):
        order[n + extra] = jnp.int32(count)
    return lax.div(n + GROUP - 1, jnp.int32(GROUP))


def accumulate(wanted, left_qn, right_qn, slots, psi, right, left, half, total, order):
    sectors, width = psi.shape[0], psi.shape[1]
    operators, right_count = right.shape[0], right.shape[1]
    zero = jnp.zeros((width, width), jnp.bfloat16)

    def one_group(g, unused):
        members = [order[g * GROUP + j] for j in range(GROUP)]
        places = [jnp.minimum(s, sectors - 1) for s in members]
        quanta = [jnp.where(s < sectors, right_qn[at], -1) for s, at in zip(members, places)]
        sources = []
        for p in range(GROUP // 2):
            rows = []
            for e in (2 * p, 2 * p + 1):
                block = psi[places[e]]
                rows.append(
                    jnp.concatenate([jnp.where(quanta[e] == r, block, zero) for r in range(right_count)], axis=1)
                )
            sources.append(jnp.concatenate(rows, axis=0))
        for first in range(0, operators, BLOCK_K):
            stream = jnp.concatenate(
                [right[first : first + BLOCK_K, r].reshape(BLOCK_K * width, width) for r in range(right_count)], axis=1
            )
            for p in range(GROUP // 2):
                product = lax.dot_general(stream, sources[p], NT, preferred_element_type=jnp.float32)
                half[:, p] = product.astype(jnp.bfloat16).reshape(BLOCK_K, width, 2 * width)
            for k in range(BLOCK_K):
                block = left[first + k]
                weights = jnp.concatenate(
                    [jnp.concatenate([block, zero], axis=1), jnp.concatenate([zero, block], axis=1)], axis=0
                )
                term = lax.dot_general(
                    half[k].reshape(GROUP // 2 * width, 2 * width), weights, NT, preferred_element_type=jnp.float32
                )
                for j in range(GROUP):
                    p, e = j // 2, j % 2
                    total[slots[first + k, places[j]]] += term[
                        p * width : (p + 1) * width, e * width : (e + 1) * width
                    ]
        return unused

    lax.fori_loop(0, pick(left_qn, order, wanted), one_group, 0)


def own_kernel(left_local, left_qn, right_qn, slots, psi, right, left, total, half, order):
    total[...] = jnp.zeros_like(total)
    mine = lax.axis_index("blk")
    for l in range(left_local):
        accumulate(
            mine * left_local + l, left_qn, right_qn, slots, psi, right, left.at[:, l], half, total, order
        )


def other_kernel(left_qn, right_qn, slots, psi, right, start, lefts, *rest):
    outs, (half, total, order) = rest[:-3], rest[-3:]
    shifts, left_local = lefts.shape[0], lefts.shape[2]
    total[...] = start[...]
    mine = lax.axis_index("blk")

    def one_shift(d, unused):
        owner = lax.rem(mine + d + 1, jnp.int32(shifts + 1))
        for l in range(left_local):
            accumulate(
                owner * left_local + l, left_qn, right_qn, slots, psi, right, lefts.at[d, :, l], half, total, order
            )
        return unused

    lax.fori_loop(0, shifts, one_shift, 0)
    row = lax.axis_index("sector")
    for d, out in enumerate(outs):
        owner = lax.rem(row + d, jnp.int32(len(outs)))
        for m in range(CAP):
            out[m] = total[owner * CAP + m].astype(jnp.bfloat16)


def assemble_kernel(rows, targets, *rest):
    mine, theirs, out = rest[:rows], rest[rows : 2 * rows], rest[-1]
    out[...] = jnp.zeros_like(out)
    row = lax.axis_index("sector")
    for d in range(rows):
        source = lax.rem(row + rows - d, jnp.int32(rows))
        for m in range(CAP):
            block = mine[d][m].astype(jnp.float32) + theirs[d][m].astype(jnp.float32)
            out[targets[source, row * CAP + m]] += block.T


def shards(sizes, psi, left_ops, right_ops, left_qn, right_qn, pair_slot, slot_target):
    rows, blocks, halves = sizes
    sectors, width = psi.shape[0], psi.shape[1]
    operators, left_local = left_ops.shape[0], left_ops.shape[1]
    slot_count = rows * CAP
    smem = pl.BlockSpec(memory_space=pltpu.SMEM)
    vmem = pl.BlockSpec(memory_space=pltpu.VMEM)
    slot_shape = (slot_count, width, width)
    half_shape = pltpu.VMEM((BLOCK_K, GROUP // 2, width, 2 * width), jnp.bfloat16)
    order_shape = pltpu.SMEM((sectors + GROUP,), jnp.int32)
    cost = pl.CostEstimate(
        flops=4 * operators * sectors * width**3, bytes_accessed=8 * 2**20, transcendentals=0
    )
    params = pltpu.CompilerParams(vmem_limit_bytes=40 * 2**20)

    targets = lax.all_gather(slot_target[0, 0], "sector")
    shift_blk = [
        lax.ppermute(left_ops, "blk", [((b + d) % blocks, b) for b in range(blocks)]) for d in range(1, blocks)
    ]
    started = pl.pallas_call(
        functools.partial(own_kernel, left_local),
        out_shape=jax.ShapeDtypeStruct(slot_shape, jnp.float32),
        in_specs=[smem] * 3 + [vmem] * 3,
        out_specs=vmem,
        scratch_shapes=[half_shape, order_shape],
        compiler_params=params,
        cost_estimate=cost,
        name="own_left",
    )(left_qn, right_qn, pair_slot, psi, right_ops, left_ops)
    partial = pl.pallas_call(
        other_kernel,
        out_shape=[jax.ShapeDtypeStruct((CAP, width, width), jnp.bfloat16)] * rows,
        in_specs=[smem] * 3 + [vmem] * 4,
        out_specs=[vmem] * rows,
        scratch_shapes=[half_shape, pltpu.VMEM(slot_shape, jnp.float32), order_shape],
        compiler_params=params,
        cost_estimate=cost,
        name="other_left",
    )(left_qn, right_qn, pair_slot, psi, right_ops, started, jnp.stack(shift_blk))
    mine = [partial[0]] + [
        lax.ppermute(partial[d], "sector", [(i, (i + d) % rows) for i in range(rows)]) for d in range(1, rows)
    ]
    theirs = [lax.ppermute(block, "op", [(h, halves - 1 - h) for h in range(halves)]) for block in mine]
    return pl.pallas_call(
        functools.partial(assemble_kernel, rows),
        out_shape=jax.ShapeDtypeStruct((sectors, width, width), jnp.float32),
        in_specs=[smem] + [vmem] * (2 * rows),
        out_specs=vmem,
        compiler_params=params,
        name="assemble",
    )(targets, *mine, *theirs)


def solution(mesh):
    in_specs = (
        P(("groups", "sector", "blk"), None, None),
        P(("groups", "op"), "blk", None, None),
        P(("groups", "op"), None, None, None),
        P(("groups", "sector", "blk")),
        P(("groups", "sector", "blk")),
        P(("groups", "op"), ("sector", "blk")),
        P(("groups", "sector"), "blk", None),
    )
    out_specs = P(("groups", "sector", "blk"), None, None)
    sizes = tuple(mesh.shape[name] for name in ("sector", "blk", "op"))
    return jax.shard_map(
        functools.partial(shards, sizes), mesh=mesh, in_specs=in_specs, out_specs=out_specs, check_vma=False
    )
```

time: 399 us -> 64.2 us (0.16)
  matrix products: 136 us -> 0 us
  other arithmetic: 86.3 us -> 0 us
  waiting for transfers between devices: 83.3 us -> 16 us
  local copies, waits for them, and re-layouts: 64.6 us -> 6.04 us
  Pallas kernels: 0 us -> 22.9 us
  between operations: 13.9 us -> 0.05 us
  blocking collectives: 0 us -> 10.3 us
    dot_general x96 -> x0, matrix products: 136 us -> none  [the longest x32 82.2 us: one_operator(): jnp.einsum('sab,sbc->sac', chosen_left, half_k, preferred_element_type=jn...]
    scatter-add x33 -> x0, other arithmetic: 85.2 us -> none  [the longest x32 84.1 us: one_operator(): jax.ops.segment_sum(term, slots, num_segments=owners * CAP)]
    dynamic_slice x65 -> x0, local copies, waits for them, and re-layouts: 55.2 us -> none  [the longest x64 54.5 us: shards(): lax.scan(one_operator, start, (gathered, right_ops, pair_slot))]
    all_gather x1 -> x0, waiting for transfers between devices: 36.7 us -> none  [shards(): gathered = lax.all_gather(left_ops, 'blk', axis=1, tiled=True)]
    pallas_call x0 -> x3, Pallas kernels: none -> 22.9 us  [the longest x1 11.5 us: shards(): pl.pallas_call(other_kernel, out_shape=[jax.ShapeDtypeStruct((CAP, width,...]
    psum x1 -> x0, waiting for transfers between devices: 19.6 us -> none  [shards(): return lax.psum(local_sigma, 'op')]
    ppermute x0 -> x8, waiting for transfers between devices: none -> 16 us  [the longest x1 8.08 us: shards(): lax.ppermute(left_ops, 'blk', [((b + d) % blocks, b) for b in range(block...]
    all_to_all x2 -> x0, waiting for transfers between devices: 14.3 us -> none  [the longest x1 14.3 us: shards(): lax.all_to_all(reduced, 'sector', split_axis=0, concat_axis=0, tiled=True)]
  transfers between devices with their start and end apart: 5 -> 8, of which waited for: 4 -> 4; matrix products, arithmetic and copies ran while one was open for 1% -> 1% of each run, Pallas kernels for 0% -> 15%
where the time goes in v1:
time: 64.2 us; the launch traced here: 63.1 us
  Pallas kernels  22.9 us (36%)
  waiting for transfers between devices  16 us (25%)
  blocking collectives  10.3 us (16%)
  starting transfers between devices  7.78 us (12%)
  local copies, waits for them, and re-layouts  6.04 us (9%)
    pallas_call x1, Pallas kernels, shards(): pl.pallas_call(other_kernel, out_shape=[jax.ShapeDtypeStruct((CAP, width,...  11.5 us
    all_gather x1, blocking collectives, shards(): targets = lax.all_gather(slot_target[0, 0], 'sector')  10.3 us
    pallas_call x1, Pallas kernels, shards(): pl.pallas_call(functools.partial(own_kernel, left_local), out_shape=jax.S...  9.23 us
    ppermute x1, waiting for transfers between devices, shards(): lax.ppermute(left_ops, 'blk', [((b + d) % blocks, b) for b in range(block...  8.08 us
    ppermute x3, waiting for transfers between devices, shards(): lax.ppermute(partial[d], 'sector', [(i, (i + d) % rows) for i in range(ro...  7.91 us
    unnamed x13, local copies, waits for them, and re-layouts  6.04 us
    ppermute x3, starting transfers between devices, shards(): lax.ppermute(partial[d], 'sector', [(i, (i + d) % rows) for i in range(ro...  4.46 us
    ppermute x1, starting transfers between devices, shards(): lax.ppermute(left_ops, 'blk', [((b + d) % blocks, b) for b in range(block...  2.94 us
  transfers between devices with their start and end apart: 8, of which 4 were waited for; matrix products, arithmetic and copies ran while one was open for 1% of the time, Pallas kernels for 15%

profile of v1, /device:TPU:0, one launch (start us, length us, event | category | flops | bytes accessed | tf_op | source)
XLA Modules:
  0.0 63.1 jit_solution(5328310669528968734)
XLA Ops:
  0.0 2.9 %collective-permute-start = (bf16[32,1,128,128]{3,2,0,1:T(8,128)(2,1)}, bf16[32,1,128,128]{3,2,0,1:T(8,128)(2,1)S(1)}, u32[]{:S(2)}, u32[]{:S(2)}) collective-permute-start(bf16[32,1,128,128]{3,2,0,1:T(8,128)(2,1)} %bitcast.4), channel_id=1, source_target_pairs={{2,0},{0,2},{3,1},{1,3},{6,4},{4,6},{7,5},{5,7},{10,8},{8,10},{11,... | collective-permute-start | bytes 3145736 | tf_op jit(solution)/shard_map/ppermute | solution.py:131
  2.9 0.8 %copy.13.slots = s32[32,24]{1,0:T(8,128)S(1)} copy(s32[32,24]{0,1:T(8,128)} %param.12) | data formatting | bytes 6144 | tf_op args[5]
  3.7 0.0 copy-start
  3.7 1.6 %copy-done = bf16[32,2,128,128]{3,2,1,0:T(8,128)(2,1)S(1)} copy-done((bf16[32,2,128,128]{3,2,1,0:T(8,128)(2,1)S(1)}, bf16[32,2,128,128]{3,2,1,0:T(8,128)(2,1)}, u32[]{:S(2)}) %copy-start) | copy-done | bytes 2097176
  5.3 0.0 copy-start.1
  5.3 1.2 %copy-done.1 = bf16[32,1,128,128]{3,2,1,0:T(8,128)(2,1)S(1)} copy-done((bf16[32,1,128,128]{3,2,1,0:T(8,128)(2,1)S(1)}, bf16[32,1,128,128]{3,2,1,0:T(8,128)(2,1)}, u32[]{:S(2)}) %copy-start.1) | copy-done | bytes 1048600
  6.5 0.0 copy-start.2
  6.5 1.1 %copy-done.2 = bf16[24,128,128]{2,1,0:T(8,128)(2,1)S(1)} copy-done((bf16[24,128,128]{2,1,0:T(8,128)(2,1)S(1)}, bf16[24,128,128]{2,1,0:T(8,128)(2,1)}, u32[]{:S(2)}) %copy-start.2) | copy-done | bytes 786456
  7.7 0.7 %copy-done.3 = s32[24]{0:T(128)S(1)} copy-done((s32[24]{0:T(128)S(1)}, s32[24]{0:T(128)}, u32[]{:S(2)}) %copy-start.3) | copy-done | bytes 120
  8.3 0.0 copy-start.4
  8.3 0.7 %copy-done.4 = s32[24]{0:T(128)S(1)} copy-done((s32[24]{0:T(128)S(1)}, s32[24]{0:T(128)}, u32[]{:S(2)}) %copy-start.4) | copy-done | bytes 120
  9.0 9.2 %own_left.1.start = f32[16,128,128]{2,1,0:T(8,128)S(1)} custom-call(s32[24]{0:T(128)S(1)} %copy-done.3, s32[24]{0:T(128)S(1)} %copy-done.4, s32[32,24]{1,0:T(8,128)S(1)} %copy.13.slots, bf16[24,128,128]{2,1,0:T(8,128)(2,1)S(1)} %copy-done.2, bf16[32,2,128,128]{3,2,1,0:T(8,128)(2,1)S(1)} %copy-done, bf16[32,1,128,128]{3,2,1,0:T(8,128)(2,1)S(1)} %copy-done.1), custom_call_target="tpu_custom_call" | custom-call | flops 6442450944 | bytes 8388608 | tf_op jit(solution)/shard_map/own_left/pallas_call | solution.py:133
  18.2 8.1 %collective-permute-done = bf16[32,1,128,128]{3,2,0,1:T(8,128)(2,1)S(1)} collective-permute-done((bf16[32,1,128,128]{3,2,0,1:T(8,128)(2,1)}, bf16[32,1,128,128]{3,2,0,1:T(8,128)(2,1)S(1)}, u32[]{:S(2)}, u32[]{:S(2)}) %collective-permute-start) | collective-permute-done | bytes 1048608 | tf_op jit(solution)/shard_map/ppermute | solution.py:131
  26.3 0.0 copy-start.5
  26.3 11.5 %other_left.1 = (bf16[4,128,128]{2,1,0:T(8,128)(2,1)S(1)}, bf16[4,128,128]{2,1,0:T(8,128)(2,1)S(1)}, bf16[4,128,128]{2,1,0:T(8,128)(2,1)S(1)}, bf16[4,128,128]{2,1,0:T(8,128)(2,1)S(1)}) custom-call(s32[24]{0:T(128)S(1)} %copy-done.3, s32[24]{0:T(128)S(1)} %copy-done.4, s32[32,24]{1,0:T(8,128)S(1)} %copy.13.slots, bf16[24,128,128]{2,1,0:T(8,128)(2,1)S(1)} %copy-done.2, ...), custom_call_target="tpu_custom_call" | custom-call | flops 6442450944 | bytes 8388608 | tf_op jit(solution)/shard_map/other_left/pallas_call | solution.py:143
  37.9 0.1 collective-permute-start.1
  37.9 4.4 %collective-permute-start.2 = (bf16[4,128,128]{2,1,0:T(8,128)(2,1)S(1)}, bf16[4,128,128]{2,1,0:T(8,128)(2,1)S(1)}, u32[]{:S(2)}, u32[]{:S(2)}) collective-permute-start(bf16[4,128,128]{2,1,0:T(8,128)(2,1)S(1)} %get-tuple-element.11), channel_id=1, source_target_pairs={{0,8},{4,12},{8,0},{12,4},{1,9},{5,13},{9,1},{13,5},{2,10},{6,14},... | collective-permute-start | bytes 393224 | tf_op jit(solution)/shard_map/ppermute | solution.py:154
  42.3 0.0 collective-permute-start.3
  42.3 0.0 collective-permute-start.4
  42.3 4.0 %collective-permute-done.1.rest_1_ = bf16[4,128,128]{2,1,0:T(8,128)(2,1)S(1)} collective-permute-done((bf16[4,128,128]{2,1,0:T(8,128)(2,1)S(1)}, bf16[4,128,128]{2,1,0:T(8,128)(2,1)S(1)}, u32[]{:S(2)}, u32[]{:S(2)}) %collective-permute-start.1) | collective-permute-done | bytes 131104 | tf_op jit(solution)/shard_map/ppermute | solution.py:154
  46.3 0.0 collective-permute-start.5
  46.3 3.8 %collective-permute-done.2.rest_2_ = bf16[4,128,128]{2,1,0:T(8,128)(2,1)S(1)} collective-permute-done((bf16[4,128,128]{2,1,0:T(8,128)(2,1)S(1)}, bf16[4,128,128]{2,1,0:T(8,128)(2,1)S(1)}, u32[]{:S(2)}, u32[]{:S(2)}) %collective-permute-start.2) | collective-permute-done | bytes 131104 | tf_op jit(solution)/shard_map/ppermute | solution.py:154
  50.1 0.0 collective-permute-start.6
  50.1 0.1 collective-permute-done.3.rest_3_
  50.3 0.4 collective-permute-start.7
  50.6 0.0 copy-done.5
  50.6 10.3 %all-gather = s32[4,1,16]{2,1,0:T(1,128)S(1)} all-gather(s32[1,1,16]{2,1,0:T(1,128)S(1)} %copy-done.5), channel_id=2, replica_groups=mesh['groups'=2,'sector'=4,'blk'=2,'op'=2] {'sector'}, dimensions={0}, use_global_device_ids=true | all-gather | bytes 320 | tf_op jit(solution)/shard_map/all_gather | solution.py:129
  60.9 0.0 collective-permute-done.4.rest_4_
  60.9 0.0 collective-permute-done.5.rest_5_
  60.9 0.0 collective-permute-done.6.rest_6_
  60.9 0.0 collective-permute-done.7.rest_7_
  60.9 2.1 %assemble.1 = f32[24,128,128]{2,1,0:T(8,128)} custom-call(s32[4,16]{1,0:T(4,128)S(1)} %bitcast.3, bf16[4,128,128]{2,1,0:T(8,128)(2,1)S(1)} %get-tuple-element.9.rest_0_, bf16[4,128,128]{2,1,0:T(8,128)(2,1)S(1)} %collective-permute-done.1.rest_1_, bf16[4,128,128]{2,1,0:T(8,128)(2,1)S(1)} %collective-permute-done.2.rest_2_, ...), custom_call_target="tpu_custom_call" | custom-call | tf_op jit(solution)/shard_map/assemble/pallas_call | solution.py:157
  (1 shorter events, 0.0 us)
Async XLA Ops:
  0.0 26.3 %collective-permute-start = (bf16[32,1,128,128]{3,2,0,1:T(8,128)(2,1)}, bf16[32,1,128,128]{3,2,0,1:T(8,128)(2,1)S(1)}, u32[]{:S(2)}, u32[]{:S(2)}) collective-permute-start(bf16[32,1,128,128]{3,2,0,1:T(8,128)(2,1)} %bitcast.4), channel_id=1, source_target_pairs={{2,0},{0,2},{3,1},{1,3},{6,4},{4,6},{7,5},{5,7},{10,8},{8,10},{11,... | collective-permute-start | bytes 3145736 | tf_op jit(solution)/shard_map/ppermute | solution.py:131
  3.7 1.6 %copy-start = (bf16[32,2,128,128]{3,2,1,0:T(8,128)(2,1)S(1)}, bf16[32,2,128,128]{3,2,1,0:T(8,128)(2,1)}, u32[]{:S(2)}) copy-start(bf16[32,2,128,128]{3,2,1,0:T(8,128)(2,1)} %right.3) | copy-start | bytes 6291460
  5.3 1.2 %copy-start.1 = (bf16[32,1,128,128]{3,2,1,0:T(8,128)(2,1)S(1)}, bf16[32,1,128,128]{3,2,1,0:T(8,128)(2,1)}, u32[]{:S(2)}) copy-start(bf16[32,1,128,128]{3,2,1,0:T(8,128)(2,1)} %left.1) | copy-start | bytes 3145732
  6.5 1.1 %copy-start.2 = (bf16[24,128,128]{2,1,0:T(8,128)(2,1)S(1)}, bf16[24,128,128]{2,1,0:T(8,128)(2,1)}, u32[]{:S(2)}) copy-start(bf16[24,128,128]{2,1,0:T(8,128)(2,1)} %psi.3) | copy-start | bytes 2359300
  7.7 0.7 %copy-start.3 = (s32[24]{0:T(128)S(1)}, s32[24]{0:T(128)}, u32[]{:S(2)}) copy-start(s32[24]{0:T(128)} %left_qn.3) | copy-start | bytes 292
  8.3 0.7 %copy-start.4 = (s32[24]{0:T(128)S(1)}, s32[24]{0:T(128)}, u32[]{:S(2)}) copy-start(s32[24]{0:T(128)} %right_qn.3) | copy-start | bytes 292
  26.3 24.3 %copy-start.5 = (s32[1,1,16]{2,1,0:T(1,128)S(1)}, s32[1,1,16]{2,1,0:T(1,128)}, u32[]{:S(2)}) copy-start(s32[1,1,16]{2,1,0:T(1,128)} %param.13) | copy-start | bytes 196
  37.9 8.5 %collective-permute-start.1 = (bf16[4,128,128]{2,1,0:T(8,128)(2,1)S(1)}, bf16[4,128,128]{2,1,0:T(8,128)(2,1)S(1)}, u32[]{:S(2)}, u32[]{:S(2)}) collective-permute-start(bf16[4,128,128]{2,1,0:T(8,128)(2,1)S(1)} %get-tuple-element.10), channel_id=1, source_target_pairs={{0,4},{4,8},{8,12},{12,0},{1,5},{5,9},{9,13},{13,1},{2,6},{6,10},{... | collective-permute-start | bytes 393224 | tf_op jit(solution)/shard_map/ppermute | solution.py:154
  37.9 12.2 %collective-permute-start.2 = (bf16[4,128,128]{2,1,0:T(8,128)(2,1)S(1)}, bf16[4,128,128]{2,1,0:T(8,128)(2,1)S(1)}, u32[]{:S(2)}, u32[]{:S(2)}) collective-permute-start(bf16[4,128,128]{2,1,0:T(8,128)(2,1)S(1)} %get-tuple-element.11), channel_id=1, source_target_pairs={{0,8},{4,12},{8,0},{12,4},{1,9},{5,13},{9,1},{13,5},{2,10},{6,14},... | collective-permute-start | bytes 393224 | tf_op jit(solution)/shard_map/ppermute | solution.py:154
  42.3 7.9 %collective-permute-start.3 = (bf16[4,128,128]{2,1,0:T(8,128)(2,1)S(1)}, bf16[4,128,128]{2,1,0:T(8,128)(2,1)S(1)}, u32[]{:S(2)}, u32[]{:S(2)}) collective-permute-start(bf16[4,128,128]{2,1,0:T(8,128)(2,1)S(1)} %get-tuple-element.12), channel_id=1, source_target_pairs={{0,12},{4,0},{8,4},{12,8},{1,13},{5,1},{9,5},{13,9},{2,14},{6,2},{... | collective-permute-start | bytes 393224 | tf_op jit(solution)/shard_map/ppermute | solution.py:154
  42.3 18.6 %collective-permute-start.4 = (bf16[4,128,128]{2,1,0:T(8,128)(2,1)S(1)}, bf16[4,128,128]{2,1,0:T(8,128)(2,1)S(1)}, u32[]{:S(2)}, u32[]{:S(2)}) collective-permute-start(bf16[4,128,128]{2,1,0:T(8,128)(2,1)S(1)} %get-tuple-element.9.rest_0_), channel_id=1, source_target_pairs={{0,1},{1,0},{2,3},{3,2},{4,5},{5,4},{6,7},{7,6},{8,9},{9,8},{10,11... | collective-permute-start | bytes 393224 | tf_op jit(solution)/shard_map/ppermute | solution.py:156
  46.3 14.6 %collective-permute-start.5 = (bf16[4,128,128]{2,1,0:T(8,128)(2,1)S(1)}, bf16[4,128,128]{2,1,0:T(8,128)(2,1)S(1)}, u32[]{:S(2)}, u32[]{:S(2)}) collective-permute-start(bf16[4,128,128]{2,1,0:T(8,128)(2,1)S(1)} %collective-permute-done.1.rest_1_), channel_id=1, source_target_pairs={{0,1},{1,0},{2,3},{3,2},{4,5},{5,4},{6,7},{7,6},{8,9},{9,8},{10,11... | collective-permute-start | bytes 393224 | tf_op jit(solution)/shard_map/ppermute | solution.py:156
  50.1 10.8 %collective-permute-start.6 = (bf16[4,128,128]{2,1,0:T(8,128)(2,1)S(1)}, bf16[4,128,128]{2,1,0:T(8,128)(2,1)S(1)}, u32[]{:S(2)}, u32[]{:S(2)}) collective-permute-start(bf16[4,128,128]{2,1,0:T(8,128)(2,1)S(1)} %collective-permute-done.2.rest_2_), channel_id=1, source_target_pairs={{0,1},{1,0},{2,3},{3,2},{4,5},{5,4},{6,7},{7,6},{8,9},{9,8},{10,11... | collective-permute-start | bytes 393224 | tf_op jit(solution)/shard_map/ppermute | solution.py:156
  50.3 10.7 %collective-permute-start.7 = (bf16[4,128,128]{2,1,0:T(8,128)(2,1)S(1)}, bf16[4,128,128]{2,1,0:T(8,128)(2,1)S(1)}, u32[]{:S(2)}, u32[]{:S(2)}) collective-permute-start(bf16[4,128,128]{2,1,0:T(8,128)(2,1)S(1)} %collective-permute-done.3.rest_3_), channel_id=1, source_target_pairs={{0,1},{1,0},{2,3},{3,2},{4,5},{5,4},{6,7},{7,6},{8,9},{9,8},{10,11... | collective-permute-start | bytes 393224 | tf_op jit(solution)/shard_map/ppermute | solution.py:156

commit v2 on v1

v2 whole, which is shorter than its diff:
```python
import functools

import jax
import jax.numpy as jnp
from jax import lax
from jax.experimental import pallas as pl
from jax.experimental.pallas import tpu as pltpu
from jax.sharding import PartitionSpec as P

CAP = 4
GROUP = 4
BLOCK_K = 8
TAIL = 16
NT = (((1,), (1,)), ((), ()))


def pick(left_qn, order, wanted):
    count = left_qn.shape[0]

    def step(s, n):
        order[n] = s
        return n + (left_qn[s] == wanted).astype(jnp.int32)

    n = lax.fori_loop(0, count, step, jnp.int32(0))
    for extra in range(GROUP - 1):
        order[n + extra] = jnp.int32(count)
    return lax.div(n + GROUP - 1, jnp.int32(GROUP))


def accumulate(groups, first, pieces, right_qn, slots, psi, right, half, total, order):
    sectors, width = psi.shape[0], psi.shape[1]
    right_count = right.shape[1]
    zero = jnp.zeros((width, width), jnp.bfloat16)

    def one_group(g, unused):
        members = [order[g * GROUP + j] for j in range(GROUP)]
        places = [jnp.minimum(s, sectors - 1) for s in members]
        quanta = [jnp.where(s < sectors, right_qn[at], -1) for s, at in zip(members, places)]
        sources = []
        for p in range(GROUP // 2):
            rows = []
            for e in (2 * p, 2 * p + 1):
                block = psi[places[e]]
                rows.append(
                    jnp.concatenate([jnp.where(quanta[e] == r, block, zero) for r in range(right_count)], axis=1)
                )
            sources.append(jnp.concatenate(rows, axis=0))

        def right_side(i):
            at = pl.ds(first + i * BLOCK_K, BLOCK_K)
            stream = jnp.concatenate(
                [right[at, r].reshape(BLOCK_K * width, width) for r in range(right_count)], axis=1
            )
            for p in range(GROUP // 2):
                product = lax.dot_general(stream, sources[p], NT, preferred_element_type=jnp.float32)
                half[i % 2, :, p] = product.astype(jnp.bfloat16).reshape(BLOCK_K, width, 2 * width)

        def left_side(i):
            for k in range(BLOCK_K):
                block = pieces[i][k]
                weights = jnp.concatenate(
                    [jnp.concatenate([block, zero], axis=1), jnp.concatenate([zero, block], axis=1)], axis=0
                )
                term = lax.dot_general(
                    half[i % 2, k].reshape(GROUP // 2 * width, 2 * width),
                    weights,
                    NT,
                    preferred_element_type=jnp.float32,
                )
                for j in range(GROUP):
                    p, e = j // 2, j % 2
                    total[slots[places[j], first + i * BLOCK_K + k]] += term[
                        p * width : (p + 1) * width, e * width : (e + 1) * width
                    ]

        right_side(0)
        for i in range(len(pieces)):
            if i + 1 < len(pieces):
                right_side(i + 1)
            left_side(i)
        return unused

    lax.fori_loop(0, groups, one_group, 0)


def split_pieces(left):
    return [left.at[pl.ds(at, BLOCK_K)] for at in range(0, left.shape[0], BLOCK_K)]


def own_kernel(
    left_qn_in, right_qn_in, slots_in, psi_in, right_in, left_in, total,
    left_qn, right_qn, slots, psi, right, left, half, order, sems,
):
    left_local = left.shape[1]
    middle = left.shape[0] // 2
    parts = [pl.ds(0, middle), pl.ds(middle, middle)]
    pairs = [(left_qn_in, left_qn), (right_qn_in, right_qn), (slots_in, slots), (psi_in, psi)]
    for part in parts:
        pairs += [(right_in.at[part], right.at[part]), (left_in.at[part], left.at[part])]
    copies = [pltpu.make_async_copy(src, dst, sems.at[i]) for i, (src, dst) in enumerate(pairs)]
    for copy in copies:
        copy.start()
    total[...] = jnp.zeros_like(total)
    mine = lax.axis_index("blk")
    for copy in copies[:-2]:
        copy.wait()
    for i in range(2):
        if i == 1:
            for copy in copies[-2:]:
                copy.wait()
        for l in range(left_local):
            groups = pick(left_qn, order, mine * left_local + l)
            pieces = split_pieces(left.at[parts[i], l])
            accumulate(groups, i * middle, pieces, right_qn, slots, psi, right, half, total, order)


def other_kernel(last, offset, left_qn, right_qn, slots, slot_target, psi, right, start, *rest):
    if last:
        lefts, outs, (half, total, order) = rest[:2], rest[2:-3], rest[-3:]
    else:
        lefts, (total, half, order) = rest[:2], rest[2:]
    shifts, left_local = lefts[0].shape[0], lefts[0].shape[2]
    operators = slots.shape[1]
    total[...] = start[...]
    mine, row = lax.axis_index("blk"), lax.axis_index("sector")
    first = lax.rem(row + offset, jnp.int32(2)) * (operators // 2)

    def one_shift(d, unused):
        owner = lax.rem(mine + d + 1, jnp.int32(shifts + 1))
        for l in range(left_local):
            groups = pick(left_qn, order, owner * left_local + l)
            pieces = [piece for left in lefts for piece in split_pieces(left.at[d, :, l])]
            accumulate(groups, first, pieces, right_qn, slots, psi, right, half, total, order)
        return unused

    lax.fori_loop(0, shifts, one_shift, 0)
    if not last:
        return
    width = total.shape[1]
    line = lax.broadcasted_iota(jnp.int32, (TAIL, width), 0)
    for d, out in enumerate(outs):
        owner = lax.rem(row + d, jnp.int32(len(outs)))
        ids = jnp.zeros((TAIL, width), jnp.int32)
        for m in range(CAP):
            out[m * width : (m + 1) * width, :] = total[owner * CAP + m].astype(jnp.bfloat16)
            ids = jnp.where(line == m, slot_target[0, 0, owner * CAP + m], ids)
        out[CAP * width :, :] = ids.astype(jnp.float32).astype(jnp.bfloat16)


def assemble_kernel(rows, *rest):
    mine, theirs, out = rest[:rows], rest[rows : 2 * rows], rest[-1]
    width = out.shape[1]
    out[...] = jnp.zeros_like(out)
    for d in range(rows):
        ids = mine[d][CAP * width :, :].astype(jnp.float32)
        for m in range(CAP):
            at = pl.ds(m * width, width)
            block = mine[d][at, :].astype(jnp.float32) + theirs[d][at, :].astype(jnp.float32)
            target = jnp.max(ids[m : m + 1, :]).astype(jnp.int32)
            out[target] += block.T


def shards(sizes, psi, left_ops, right_ops, left_qn, right_qn, pair_slot, slot_target):
    rows, blocks, halves = sizes
    sectors, width = psi.shape[0], psi.shape[1]
    operators, left_local = left_ops.shape[0], left_ops.shape[1]
    slot_count = rows * CAP
    slots = pair_slot.T
    smem = pl.BlockSpec(memory_space=pltpu.SMEM)
    vmem = pl.BlockSpec(memory_space=pltpu.VMEM)
    hbm = pl.BlockSpec(memory_space=pltpu.HBM)
    slot_shape = (slot_count, width, width)
    half_shape = pltpu.VMEM((2, BLOCK_K, GROUP // 2, width, 2 * width), jnp.bfloat16)
    order_shape = pltpu.SMEM((sectors + GROUP,), jnp.int32)
    params = pltpu.CompilerParams(vmem_limit_bytes=40 * 2**20)

    def cost(share):
        flops = int(16 * operators * sectors * width**3 * share)
        return pl.CostEstimate(flops=flops, bytes_accessed=4 * 2**20, transcendentals=0)

    first = lax.rem(lax.axis_index("sector"), 2) * (operators // 2)
    quarter = operators // 4
    swap = [(i, i ^ 1) for i in range(rows)]
    sent = [lax.dynamic_slice_in_dim(left_ops, first + i * quarter, quarter, 0) for i in range(2)]
    near = [
        [lax.ppermute(part, "blk", [((b + d) % blocks, b) for b in range(blocks)]) for d in range(1, blocks)]
        for part in sent
    ]
    far = [[lax.ppermute(part, "sector", swap) for part in parts] for parts in near]
    near, far = ([jnp.stack(parts) for parts in side] for side in (near, far))

    total = pl.pallas_call(
        own_kernel,
        out_shape=jax.ShapeDtypeStruct(slot_shape, jnp.float32),
        in_specs=[hbm] * 6,
        out_specs=vmem,
        scratch_shapes=[
            pltpu.SMEM(left_qn.shape, jnp.int32),
            pltpu.SMEM(right_qn.shape, jnp.int32),
            pltpu.SMEM(slots.shape, jnp.int32),
            pltpu.VMEM(psi.shape, psi.dtype),
            pltpu.VMEM(right_ops.shape, right_ops.dtype),
            pltpu.VMEM(left_ops.shape, left_ops.dtype),
            half_shape,
            order_shape,
            pltpu.SemaphoreType.DMA((8,)),
        ],
        compiler_params=pltpu.CompilerParams(vmem_limit_bytes=54 * 2**20),
        cost_estimate=cost(0.5),
        name="own_left",
    )(left_qn, right_qn, slots, psi, right_ops, left_ops)
    common = (left_qn, right_qn, slots, slot_target, psi, right_ops)
    total = pl.pallas_call(
        functools.partial(other_kernel, False, 0),
        out_shape=jax.ShapeDtypeStruct(slot_shape, jnp.float32),
        in_specs=[smem] * 4 + [vmem] * 5,
        out_specs=vmem,
        scratch_shapes=[half_shape, order_shape],
        compiler_params=params,
        cost_estimate=cost(0.25),
        name="other_left_near",
    )(*common, total, *near)
    partial = pl.pallas_call(
        functools.partial(other_kernel, True, 1),
        out_shape=[jax.ShapeDtypeStruct((CAP * width + TAIL, width), jnp.bfloat16)] * rows,
        in_specs=[smem] * 4 + [vmem] * 5,
        out_specs=[vmem] * rows,
        scratch_shapes=[half_shape, pltpu.VMEM(slot_shape, jnp.float32), order_shape],
        compiler_params=params,
        cost_estimate=cost(0.25),
        name="other_left_far",
    )(*common, total, *far)
    mine = [partial[0]] + [
        lax.ppermute(partial[d], "sector", [(i, (i + d) % rows) for i in range(rows)]) for d in range(1, rows)
    ]
    theirs = [lax.ppermute(block, "op", [(h, halves - 1 - h) for h in range(halves)]) for block in mine]
    return pl.pallas_call(
        functools.partial(assemble_kernel, rows),
        out_shape=jax.ShapeDtypeStruct((sectors, width, width), jnp.float32),
        in_specs=[vmem] * (2 * rows),
        out_specs=vmem,
        compiler_params=params,
        name="assemble",
    )(*mine, *theirs)


def solution(mesh):
    in_specs = (
        P(("groups", "sector", "blk"), None, None),
        P(("groups", "op"), "blk", None, None),
        P(("groups", "op"), None, None, None),
        P(("groups", "sector", "blk")),
        P(("groups", "sector", "blk")),
        P(("groups", "op"), ("sector", "blk")),
        P(("groups", "sector"), "blk", None),
    )
    out_specs = P(("groups", "sector", "blk"), None, None)
    sizes = tuple(mesh.shape[name] for name in ("sector", "blk", "op"))
    return jax.shard_map(
        functools.partial(shards, sizes), mesh=mesh, in_specs=in_specs, out_specs=out_specs, check_vma=False
    )
```

time: 64.2 us -> 55.7 us (0.87); the launches traced: 63.1 us -> 55.5 us
  blocking collectives: 10.3 us -> 0 us
  local copies, waits for them, and re-layouts: 6.04 us -> 2.31 us
  starting transfers between devices: 7.78 us -> 11.3 us
  Pallas kernels: 22.9 us -> 26.2 us
    all_gather x1 -> x0, blocking collectives: 10.3 us -> none  [shards(): targets = lax.all_gather(slot_target[0, 0], 'sector')]
    unnamed x13 -> x14, local copies, waits for them, and re-layouts: 6.04 us -> 1.25 us
    pallas_call x2 -> x3, Pallas kernels: 20.8 us -> 24.6 us  [the longest x1 14 us: shards(): pl.pallas_call(own_kernel, out_shape=jax.ShapeDtypeStruct(slot_shape, jnp...]
    ppermute x1 -> x4, waiting for transfers between devices: 8.08 us -> 4.76 us  [the longest x2 4.76 us: shards(): lax.ppermute(part, 'sector', swap)]
    ppermute x1 -> x4, starting transfers between devices: 2.94 us -> 5.16 us  [the longest x2 3.08 us: shards(): lax.ppermute(part, 'blk', [((b + d) % blocks, b) for b in range(blocks)])]
    ppermute x3, starting transfers between devices: 4.46 us -> 6.11 us  [shards(): lax.ppermute(partial[d], 'sector', [(i, (i + d) % rows) for i in range(ro...]
    ppermute x3, waiting for transfers between devices: 7.91 us -> 9.42 us  [shards(): lax.ppermute(partial[d], 'sector', [(i, (i + d) % rows) for i in range(ro...]
    ppermute x4, waiting for transfers between devices: 0.01 us -> 1.34 us  [shards(): lax.ppermute(block, 'op', [(h, halves - 1 - h) for h in range(halves)])]
  transfers between devices with their start and end apart: 8 -> 11, of which waited for: 4 -> 6; matrix products, arithmetic and copies ran while one was open for 1% -> 0% of each run, Pallas kernels for 15% -> 35%
where the time goes in v2:
time: 55.7 us; the launch traced here: 55.5 us
  Pallas kernels  26.2 us (47%)
  waiting for transfers between devices  15.5 us (28%)
  starting transfers between devices  11.3 us (20%)
  local copies, waits for them, and re-layouts  2.31 us (4%)
    pallas_call x1, Pallas kernels, shards(): pl.pallas_call(own_kernel, out_shape=jax.ShapeDtypeStruct(slot_shape, jnp...  14 us
    ppermute x3, waiting for transfers between devices, shards(): lax.ppermute(partial[d], 'sector', [(i, (i + d) % rows) for i in range(ro...  9.42 us
    ppermute x3, starting transfers between devices, shards(): lax.ppermute(partial[d], 'sector', [(i, (i + d) % rows) for i in range(ro...  6.11 us
    pallas_call x1, Pallas kernels, shards(): pl.pallas_call(functools.partial(other_kernel, False, 0), out_shape=jax.S...  5.33 us
    pallas_call x1, Pallas kernels, shards(): pl.pallas_call(functools.partial(other_kernel, True, 1), out_shape=[jax.S...  5.31 us
    ppermute x2, waiting for transfers between devices, shards(): lax.ppermute(part, 'sector', swap)  4.76 us
    ppermute x2, starting transfers between devices, shards(): lax.ppermute(part, 'blk', [((b + d) % blocks, b) for b in range(blocks)])  3.08 us
    ppermute x2, starting transfers between devices, shards(): lax.ppermute(part, 'sector', swap)  2.08 us
  transfers between devices with their start and end apart: 11, of which 6 were waited for; matrix products, arithmetic and copies ran while one was open for 0% of the time, Pallas kernels for 35%

profile of v2, /device:TPU:0, one launch (start us, length us, event | category | flops | bytes accessed | tf_op | source)
XLA Modules:
  0.0 55.5 jit_solution(15609925908122550815)
XLA Ops:
  0.0 1.1 %constant_dynamic-slice_fusion = (bf16[8,1,128,128]{3,2,0,1:T(8,128)(2,1)S(1)}, bf16[8,1,128,128]{3,2,0,1:T(8,128)(2,1)S(1)}) fusion(bf16[32,1,128,128]{3,2,0,1:T(8,128)(2,1)} %bitcast.17, s32[]{:T(128)S(6)} %select_n.7, s32[]{:T(128)S(6)} %select_n.6), kind=kLoop, calls=%fused_computation | loop fusion | bytes 1048584 | tf_op jit(solution)/shard_map/dynamic_slice | solution.py:184
  1.1 3.0 %collective-permute-start = (bf16[8,1,128,128]{3,2,0,1:T(8,128)(2,1)S(1)}, bf16[8,1,128,128]{3,2,0,1:T(8,128)(2,1)S(1)}, u32[]{:S(2)}, u32[]{:S(2)}) collective-permute-start(bf16[8,1,128,128]{3,2,0,1:T(8,128)(2,1)S(1)} %get-tuple-element.14), channel_id=1, source_target_pairs={{2,0},{0,2},{3,1},{1,3},{6,4},{4,6},{7,5},{5,7},{10,8},{8,10},{11,... | collective-permute-start | bytes 786440 | tf_op jit(solution)/shard_map/ppermute | solution.py:186
  4.1 0.1 collective-permute-start.1
  4.2 0.0 copy-start.4
  4.2 0.0 copy-start.5
  4.2 14.0 %own_left.1.start = f32[16,128,128]{2,1,0:T(8,128)} custom-call(s32[24]{0:T(128)} %left_qn.3, s32[24]{0:T(128)} %right_qn.3, s32[24,32]{1,0:T(8,128)} %bitcast.14, bf16[24,128,128]{2,1,0:T(8,128)(2,1)} %psi.3, bf16[32,2,128,128]{3,2,1,0:T(8,128)(2,1)} %right.3, bf16[32,1,128,128]{3,2,1,0:T(8,128)(2,1)} %left_in.1), custom_call_target="tpu_custom_call" | custom-call | flops 12884901888 | bytes 4194304 | tf_op jit(solution)/shard_map/own_left/pallas_call | solution.py:192
  18.2 0.0 collective-permute-done
  18.2 0.1 collective-permute-start.2
  18.3 0.0 collective-permute-done.1
  18.3 2.0 %collective-permute-start.3 = (bf16[8,1,128,128]{3,2,0,1:T(8,128)(2,1)S(1)}, bf16[8,1,128,128]{3,2,0,1:T(8,128)(2,1)S(1)}, u32[]{:S(2)}, u32[]{:S(2)}) collective-permute-start(bf16[8,1,128,128]{3,2,0,1:T(8,128)(2,1)S(1)} %collective-permute-done.1), channel_id=1, source_target_pairs={{0,4},{4,0},{8,12},{12,8},{1,5},{5,1},{9,13},{13,9},{2,6},{6,2},{1... | collective-permute-start | bytes 786440 | tf_op jit(solution)/shard_map/ppermute | solution.py:189
  20.3 0.0 copy-done
  20.3 0.0 copy-start.6
  20.3 1.2 %copy-done.6 = f32[16,128,128]{2,1,0:T(8,128)S(1)} copy-done((f32[16,128,128]{2,1,0:T(8,128)S(1)}, f32[16,128,128]{2,1,0:T(8,128)}, u32[]{:S(2)}) %copy-start.6) | copy-done | bytes 1048600
  21.6 5.3 %other_left_near.1.start = f32[16,128,128]{2,1,0:T(8,128)S(1)} custom-call(s32[24]{0:T(128)S(1)} %copy-done.3, s32[24]{0:T(128)S(1)} %copy-done.4, s32[24,32]{1,0:T(8,128)S(1)} %bitcast.15, s32[1,1,16]{2,1,0:T(1,128)S(1)} %copy-done.5, bf16[24,128,128]{2,1,0:T(8,128)(2,1)S(1)} %copy-done.1, bf16[32,2,128,128]{3,2,1,0:T(8,128)(2,1)S(1)} %copy-done, ...), custom_call_target="tpu_custom_call" | custom-call | flops 6442450944 | bytes 4194304 | tf_op jit(solution)/shard_map/other_left_near/pallas_call | solution.py:213
  26.9 0.6 %collective-permute-done.2 = bf16[8,1,128,128]{3,2,0,1:T(8,128)(2,1)S(1)} collective-permute-done((bf16[8,1,128,128]{3,2,0,1:T(8,128)(2,1)S(1)}, bf16[8,1,128,128]{3,2,0,1:T(8,128)(2,1)S(1)}, u32[]{:S(2)}, u32[]{:S(2)}) %collective-permute-start.2) | collective-permute-done | bytes 262176 | tf_op jit(solution)/shard_map/ppermute | solution.py:189
  27.5 4.2 %collective-permute-done.3 = bf16[8,1,128,128]{3,2,0,1:T(8,128)(2,1)S(1)} collective-permute-done((bf16[8,1,128,128]{3,2,0,1:T(8,128)(2,1)S(1)}, bf16[8,1,128,128]{3,2,0,1:T(8,128)(2,1)S(1)}, u32[]{:S(2)}, u32[]{:S(2)}) %collective-permute-start.3) | collective-permute-done | bytes 262176 | tf_op jit(solution)/shard_map/ppermute | solution.py:189
  31.7 5.3 %other_left_far.1 = (bf16[528,128]{1,0:T(8,128)(2,1)S(1)}, bf16[528,128]{1,0:T(8,128)(2,1)S(1)}, bf16[528,128]{1,0:T(8,128)(2,1)S(1)}, bf16[528,128]{1,0:T(8,128)(2,1)S(1)}) custom-call(s32[24]{0:T(128)S(1)} %copy-done.3, s32[24]{0:T(128)S(1)} %copy-done.4, s32[24,32]{1,0:T(8,128)S(1)} %bitcast.16, s32[1,1,16]{2,1,0:T(1,128)S(1)} %copy-done.5, ...), custom_call_target="tpu_custom_call" | custom-call | flops 6442450944 | bytes 4194304 | tf_op jit(solution)/shard_map/other_left_far/pallas_call | solution.py:223
  37.0 3.8 %collective-permute-start.6 = (bf16[528,128]{1,0:T(8,128)(2,1)S(1)}, bf16[528,128]{1,0:T(8,128)(2,1)S(1)}, u32[]{:S(2)}, u32[]{:S(2)}) collective-permute-start(bf16[528,128]{1,0:T(8,128)(2,1)S(1)} %get-tuple-element.12), channel_id=1, source_target_pairs={{0,12},{4,0},{8,4},{12,8},{1,13},{5,1},{9,5},{13,9},{2,14},{6,2},{... | collective-permute-start | bytes 405512 | tf_op jit(solution)/shard_map/ppermute | solution.py:234
  40.8 0.0 collective-permute-start.4
  40.8 2.3 %collective-permute-start.5 = (bf16[528,128]{1,0:T(8,128)(2,1)S(1)}, bf16[528,128]{1,0:T(8,128)(2,1)S(1)}, u32[]{:S(2)}, u32[]{:S(2)}) collective-permute-start(bf16[528,128]{1,0:T(8,128)(2,1)S(1)} %get-tuple-element.11), channel_id=1, source_target_pairs={{0,8},{4,12},{8,0},{12,4},{1,9},{5,13},{9,1},{13,5},{2,10},{6,14},... | collective-permute-start | bytes 405512 | tf_op jit(solution)/shard_map/ppermute | solution.py:234
  43.1 0.0 collective-permute-start.7
  43.1 1.8 %collective-permute-done.6.rest_3_ = bf16[528,128]{1,0:T(8,128)(2,1)S(1)} collective-permute-done((bf16[528,128]{1,0:T(8,128)(2,1)S(1)}, bf16[528,128]{1,0:T(8,128)(2,1)S(1)}, u32[]{:S(2)}, u32[]{:S(2)}) %collective-permute-start.6) | collective-permute-done | bytes 135200 | tf_op jit(solution)/shard_map/ppermute | solution.py:234
  44.9 0.0 collective-permute-start.10
  44.9 4.2 %collective-permute-done.4.rest_1_ = bf16[528,128]{1,0:T(8,128)(2,1)S(1)} collective-permute-done((bf16[528,128]{1,0:T(8,128)(2,1)S(1)}, bf16[528,128]{1,0:T(8,128)(2,1)S(1)}, u32[]{:S(2)}, u32[]{:S(2)}) %collective-permute-start.4) | collective-permute-done | bytes 135200 | tf_op jit(solution)/shard_map/ppermute | solution.py:234
  49.1 0.0 collective-permute-start.8
  49.1 3.4 %collective-permute-done.5.rest_2_ = bf16[528,128]{1,0:T(8,128)(2,1)S(1)} collective-permute-done((bf16[528,128]{1,0:T(8,128)(2,1)S(1)}, bf16[528,128]{1,0:T(8,128)(2,1)S(1)}, u32[]{:S(2)}, u32[]{:S(2)}) %collective-permute-start.5) | collective-permute-done | bytes 135200 | tf_op jit(solution)/shard_map/ppermute | solution.py:234
  52.5 0.0 collective-permute-start.9
  52.5 0.0 collective-permute-done.7.rest_4_
  52.5 0.0 collective-permute-done.10.rest_7_
  52.5 0.0 collective-permute-done.8.rest_5_
  52.5 1.3 %collective-permute-done.9.rest_6_ = bf16[528,128]{1,0:T(8,128)(2,1)S(1)} collective-permute-done((bf16[528,128]{1,0:T(8,128)(2,1)S(1)}, bf16[528,128]{1,0:T(8,128)(2,1)S(1)}, u32[]{:S(2)}, u32[]{:S(2)}) %collective-permute-start.9) | collective-permute-done | bytes 135200 | tf_op jit(solution)/shard_map/ppermute | solution.py:236
  53.9 1.6 %assemble.1 = f32[24,128,128]{2,1,0:T(8,128)} custom-call(bf16[528,128]{1,0:T(8,128)(2,1)S(1)} %get-tuple-element.9.rest_0_, bf16[528,128]{1,0:T(8,128)(2,1)S(1)} %collective-permute-done.4.rest_1_, bf16[528,128]{1,0:T(8,128)(2,1)S(1)} %collective-permute-done.5.rest_2_, bf16[528,128]{1,0:T(8,128)(2,1)S(1)} %collective-permute-done.6.rest_3_, ...), custom_call_target="tpu_custom_call" | custom-call | tf_op jit(solution)/shard_map/assemble/pallas_call | solution.py:237
  (9 shorter events, 0.0 us)
Async XLA Ops:
  1.1 17.1 %collective-permute-start = (bf16[8,1,128,128]{3,2,0,1:T(8,128)(2,1)S(1)}, bf16[8,1,128,128]{3,2,0,1:T(8,128)(2,1)S(1)}, u32[]{:S(2)}, u32[]{:S(2)}) collective-permute-start(bf16[8,1,128,128]{3,2,0,1:T(8,128)(2,1)S(1)} %get-tuple-element.14), channel_id=1, source_target_pairs={{2,0},{0,2},{3,1},{1,3},{6,4},{4,6},{7,5},{5,7},{10,8},{8,10},{11,... | collective-permute-start | bytes 786440 | tf_op jit(solution)/shard_map/ppermute | solution.py:186
  4.1 14.2 %collective-permute-start.1 = (bf16[8,1,128,128]{3,2,0,1:T(8,128)(2,1)S(1)}, bf16[8,1,128,128]{3,2,0,1:T(8,128)(2,1)S(1)}, u32[]{:S(2)}, u32[]{:S(2)}) collective-permute-start(bf16[8,1,128,128]{3,2,0,1:T(8,128)(2,1)S(1)} %get-tuple-element.13), channel_id=1, source_target_pairs={{2,0},{0,2},{3,1},{1,3},{6,4},{4,6},{7,5},{5,7},{10,8},{8,10},{11,... | collective-permute-start | bytes 786440 | tf_op jit(solution)/shard_map/ppermute | solution.py:186
  4.2 16.2 %copy-start = (bf16[32,2,128,128]{3,2,1,0:T(8,128)(2,1)S(1)}, bf16[32,2,128,128]{3,2,1,0:T(8,128)(2,1)}, u32[]{:S(2)}) copy-start(bf16[32,2,128,128]{3,2,1,0:T(8,128)(2,1)} %right.3) | copy-start | bytes 6291460
  4.2 16.2 %copy-start.1 = (bf16[24,128,128]{2,1,0:T(8,128)(2,1)S(1)}, bf16[24,128,128]{2,1,0:T(8,128)(2,1)}, u32[]{:S(2)}) copy-start(bf16[24,128,128]{2,1,0:T(8,128)(2,1)} %psi.3) | copy-start | bytes 2359300
  4.2 16.2 %copy-start.2 = (s32[32,24]{0,1:T(8,128)S(1)}, s32[32,24]{0,1:T(8,128)}, u32[]{:S(2)}) copy-start(s32[32,24]{0,1:T(8,128)} %param.12) | copy-start | bytes 9220
  4.2 16.2 %copy-start.3 = (s32[24]{0:T(128)S(1)}, s32[24]{0:T(128)}, u32[]{:S(2)}) copy-start(s32[24]{0:T(128)} %left_qn.3) | copy-start | bytes 292
  4.2 16.2 %copy-start.4 = (s32[24]{0:T(128)S(1)}, s32[24]{0:T(128)}, u32[]{:S(2)}) copy-start(s32[24]{0:T(128)} %right_qn.3) | copy-start | bytes 292
  4.2 16.2 %copy-start.5 = (s32[1,1,16]{2,1,0:T(1,128)S(1)}, s32[1,1,16]{2,1,0:T(1,128)}, u32[]{:S(2)}) copy-start(s32[1,1,16]{2,1,0:T(1,128)} %slot_target.3) | copy-start | bytes 196
  18.2 9.3 %collective-permute-start.2 = (bf16[8,1,128,128]{3,2,0,1:T(8,128)(2,1)S(1)}, bf16[8,1,128,128]{3,2,0,1:T(8,128)(2,1)S(1)}, u32[]{:S(2)}, u32[]{:S(2)}) collective-permute-start(bf16[8,1,128,128]{3,2,0,1:T(8,128)(2,1)S(1)} %collective-permute-done), channel_id=1, source_target_pairs={{0,4},{4,0},{8,12},{12,8},{1,5},{5,1},{9,13},{13,9},{2,6},{6,2},{1... | collective-permute-start | bytes 786440 | tf_op jit(solution)/shard_map/ppermute | solution.py:189
  18.3 13.4 %collective-permute-start.3 = (bf16[8,1,128,128]{3,2,0,1:T(8,128)(2,1)S(1)}, bf16[8,1,128,128]{3,2,0,1:T(8,128)(2,1)S(1)}, u32[]{:S(2)}, u32[]{:S(2)}) collective-permute-start(bf16[8,1,128,128]{3,2,0,1:T(8,128)(2,1)S(1)} %collective-permute-done.1), channel_id=1, source_target_pairs={{0,4},{4,0},{8,12},{12,8},{1,5},{5,1},{9,13},{13,9},{2,6},{6,2},{1... | collective-permute-start | bytes 786440 | tf_op jit(solution)/shard_map/ppermute | solution.py:189
  20.3 1.2 %copy-start.6 = (f32[16,128,128]{2,1,0:T(8,128)S(1)}, f32[16,128,128]{2,1,0:T(8,128)}, u32[]{:S(2)}) copy-start(f32[16,128,128]{2,1,0:T(8,128)} %own_left.1.start) | copy-start | bytes 3145732
  37.0 7.9 %collective-permute-start.6 = (bf16[528,128]{1,0:T(8,128)(2,1)S(1)}, bf16[528,128]{1,0:T(8,128)(2,1)S(1)}, u32[]{:S(2)}, u32[]{:S(2)}) collective-permute-start(bf16[528,128]{1,0:T(8,128)(2,1)S(1)} %get-tuple-element.12), channel_id=1, source_target_pairs={{0,12},{4,0},{8,4},{12,8},{1,13},{5,1},{9,5},{13,9},{2,14},{6,2},{... | collective-permute-start | bytes 405512 | tf_op jit(solution)/shard_map/ppermute | solution.py:234
  40.8 8.3 %collective-permute-start.4 = (bf16[528,128]{1,0:T(8,128)(2,1)S(1)}, bf16[528,128]{1,0:T(8,128)(2,1)S(1)}, u32[]{:S(2)}, u32[]{:S(2)}) collective-permute-start(bf16[528,128]{1,0:T(8,128)(2,1)S(1)} %get-tuple-element.10), channel_id=1, source_target_pairs={{0,4},{4,8},{8,12},{12,0},{1,5},{5,9},{9,13},{13,1},{2,6},{6,10},{... | collective-permute-start | bytes 405512 | tf_op jit(solution)/shard_map/ppermute | solution.py:234
  40.8 11.7 %collective-permute-start.5 = (bf16[528,128]{1,0:T(8,128)(2,1)S(1)}, bf16[528,128]{1,0:T(8,128)(2,1)S(1)}, u32[]{:S(2)}, u32[]{:S(2)}) collective-permute-start(bf16[528,128]{1,0:T(8,128)(2,1)S(1)} %get-tuple-element.11), channel_id=1, source_target_pairs={{0,8},{4,12},{8,0},{12,4},{1,9},{5,13},{9,1},{13,5},{2,10},{6,14},... | collective-permute-start | bytes 405512 | tf_op jit(solution)/shard_map/ppermute | solution.py:234
  43.1 9.4 %collective-permute-start.7 = (bf16[528,128]{1,0:T(8,128)(2,1)S(1)}, bf16[528,128]{1,0:T(8,128)(2,1)S(1)}, u32[]{:S(2)}, u32[]{:S(2)}) collective-permute-start(bf16[528,128]{1,0:T(8,128)(2,1)S(1)} %get-tuple-element.9.rest_0_), channel_id=1, source_target_pairs={{0,1},{1,0},{2,3},{3,2},{4,5},{5,4},{6,7},{7,6},{8,9},{9,8},{10,11... | collective-permute-start | bytes 405512 | tf_op jit(solution)/shard_map/ppermute | solution.py:236
  44.9 7.6 %collective-permute-start.10 = (bf16[528,128]{1,0:T(8,128)(2,1)S(1)}, bf16[528,128]{1,0:T(8,128)(2,1)S(1)}, u32[]{:S(2)}, u32[]{:S(2)}) collective-permute-start(bf16[528,128]{1,0:T(8,128)(2,1)S(1)} %collective-permute-done.6.rest_3_), channel_id=1, source_target_pairs={{0,1},{1,0},{2,3},{3,2},{4,5},{5,4},{6,7},{7,6},{8,9},{9,8},{10,11... | collective-permute-start | bytes 405512 | tf_op jit(solution)/shard_map/ppermute | solution.py:236
  49.1 3.5 %collective-permute-start.8 = (bf16[528,128]{1,0:T(8,128)(2,1)S(1)}, bf16[528,128]{1,0:T(8,128)(2,1)S(1)}, u32[]{:S(2)}, u32[]{:S(2)}) collective-permute-start(bf16[528,128]{1,0:T(8,128)(2,1)S(1)} %collective-permute-done.4.rest_1_), channel_id=1, source_target_pairs={{0,1},{1,0},{2,3},{3,2},{4,5},{5,4},{6,7},{7,6},{8,9},{9,8},{10,11... | collective-permute-start | bytes 405512 | tf_op jit(solution)/shard_map/ppermute | solution.py:236
  52.5 1.4 %collective-permute-start.9 = (bf16[528,128]{1,0:T(8,128)(2,1)S(1)}, bf16[528,128]{1,0:T(8,128)(2,1)S(1)}, u32[]{:S(2)}, u32[]{:S(2)}) collective-permute-start(bf16[528,128]{1,0:T(8,128)(2,1)S(1)} %collective-permute-done.5.rest_2_), channel_id=1, source_target_pairs={{0,1},{1,0},{2,3},{3,2},{4,5},{5,4},{6,7},{7,6},{8,9},{9,8},{10,11... | collective-permute-start | bytes 405512 | tf_op jit(solution)/shard_map/ppermute | solution.py:236

commit v3 on v2

v3 whole, which is shorter than its diff:
```python
import functools

import jax
import jax.numpy as jnp
from jax import lax
from jax.experimental import pallas as pl
from jax.experimental.pallas import tpu as pltpu
from jax.sharding import PartitionSpec as P

CAP = 4
GROUP = 4
BLOCK_K = 8
TAIL = 16
NT = (((1,), (1,)), ((), ()))


def arrange(left_qn, order, starts, blocks, left_local):
    mine = lax.axis_index("blk")
    count = left_qn.shape[0]

    def one_code(code, n):
        starts[code] = n
        owner = lax.rem(mine + lax.div(code, jnp.int32(left_local)), jnp.int32(blocks))
        wanted = owner * left_local + lax.rem(code, jnp.int32(left_local))

        def one_sector(s, n):
            order[n] = s
            return n + (left_qn[s] == wanted).astype(jnp.int32)

        return lax.fori_loop(0, count, one_sector, n)

    starts[blocks * left_local] = lax.fori_loop(0, blocks * left_local, one_code, jnp.int32(0))


def right_kernel(
    blocks, left_local, left_qn_in, right_qn_in, psi_in, right_in, half,
    left_qn, right_qn, psi, right, sources, order, starts, sems,
):
    sectors, width = psi.shape[0], psi.shape[1]
    right_count = right.shape[1]
    steps = right.shape[0] // BLOCK_K
    zero = jnp.zeros((width, width), jnp.bfloat16)

    def right_copy(i):
        at = pl.ds(i * BLOCK_K, BLOCK_K)
        return pltpu.make_async_copy(right_in.at[at], right.at[at], sems.at[3 + i])

    copies = [
        pltpu.make_async_copy(left_qn_in, left_qn, sems.at[0]),
        pltpu.make_async_copy(right_qn_in, right_qn, sems.at[1]),
        pltpu.make_async_copy(psi_in, psi, sems.at[2]),
    ]
    for copy in copies:
        copy.start()
    for i in range(steps):
        right_copy(i).start()
    copies[0].wait()
    copies[1].wait()
    arrange(left_qn, order, starts, blocks, left_local)
    copies[2].wait()
    for pair in range(sectors // 2):
        for e in range(2):
            s = order[2 * pair + e]
            block = psi[s]
            for r in range(right_count):
                sources[pair, e * width : (e + 1) * width, r * width : (r + 1) * width] = jnp.where(
                    right_qn[s] == r, block, zero
                )

    def one_step(i, unused):
        right_copy(i).wait()
        at = pl.ds(i * BLOCK_K, BLOCK_K)
        stream = jnp.concatenate([right[at, r].reshape(BLOCK_K * width, width) for r in range(right_count)], axis=1)
        for pair in range(sectors // 2):
            product = lax.dot_general(stream, sources[pair], NT, preferred_element_type=jnp.float32)
            half[pair // 2, at, pair % 2] = product.astype(jnp.bfloat16).reshape(BLOCK_K, width, 2 * width)
        return unused

    lax.fori_loop(0, steps, one_step, 0)


def accumulate(low, high, first, pieces, slots, half, total, order):
    width = total.shape[1]
    spare = total.shape[0] - 1
    zero = jnp.zeros((width, width), jnp.bfloat16)

    def one_group(g, unused):
        places = [g * GROUP + j for j in range(GROUP)]
        members = [order[at] for at in places]
        counts = [(low <= at) & (at < high) for at in places]
        k = 0
        for piece in pieces:
            for at in range(piece.shape[0]):
                block = piece[at]
                weights = jnp.concatenate(
                    [jnp.concatenate([block, zero], axis=1), jnp.concatenate([zero, block], axis=1)], axis=0
                )
                term = lax.dot_general(
                    half[g, first + k].reshape(GROUP // 2 * width, 2 * width),
                    weights,
                    NT,
                    preferred_element_type=jnp.float32,
                )
                for j in range(GROUP):
                    p, e = j // 2, j % 2
                    slot = jnp.where(counts[j], slots[members[j], first + k], spare)
                    total[slot] += term[p * width : (p + 1) * width, e * width : (e + 1) * width]
                k += 1
        return unused

    groups = jnp.where(low < high, lax.div(high + GROUP - 1, jnp.int32(GROUP)), 0)
    lax.fori_loop(lax.div(low, jnp.int32(GROUP)), groups, one_group, 0)


def own_kernel(blocks, left_qn, slots, half, left, total, order, starts):
    left_local = left.shape[1]
    total[...] = jnp.zeros_like(total)
    arrange(left_qn, order, starts, blocks, left_local)
    for l in range(left_local):
        accumulate(starts[l], starts[l + 1], 0, [left.at[:, l]], slots, half, total, order)


def other_kernel(last, offset, left_qn, slots, slot_target, half, start, *rest):
    lefts = rest[:2]
    if last:
        outs, (total, order, starts) = rest[2:-3], rest[-3:]
    else:
        total, order, starts = rest[2:]
    shifts, left_local = lefts[0].shape[0], lefts[0].shape[2]
    operators = slots.shape[1]
    total[...] = start[...]
    arrange(left_qn, order, starts, shifts + 1, left_local)
    row = lax.axis_index("sector")
    first = lax.rem(row + offset, jnp.int32(2)) * (operators // 2)

    def one_shift(d, unused):
        for l in range(left_local):
            code = (d + 1) * left_local + l
            pieces = [left.at[d, :, l] for left in lefts]
            accumulate(starts[code], starts[code + 1], first, pieces, slots, half, total, order)
        return unused

    lax.fori_loop(0, shifts, one_shift, 0)
    if not last:
        return
    width = total.shape[1]
    line = lax.broadcasted_iota(jnp.int32, (TAIL, width), 0)
    for d, out in enumerate(outs):
        owner = lax.rem(row + d, jnp.int32(len(outs)))
        ids = jnp.zeros((TAIL, width), jnp.int32)
        for m in range(CAP):
            out[m * width : (m + 1) * width, :] = total[owner * CAP + m].astype(jnp.bfloat16)
            ids = jnp.where(line == m, slot_target[0, 0, owner * CAP + m], ids)
        out[CAP * width :, :] = ids.astype(jnp.float32).astype(jnp.bfloat16)


def assemble_kernel(rows, *rest):
    mine, theirs, out = rest[:rows], rest[rows : 2 * rows], rest[-1]
    width = out.shape[1]
    out[...] = jnp.zeros_like(out)
    for d in range(rows):
        ids = mine[d][CAP * width :, :].astype(jnp.float32)
        for m in range(CAP):
            at = pl.ds(m * width, width)
            block = mine[d][at, :].astype(jnp.float32) + theirs[d][at, :].astype(jnp.float32)
            target = jnp.max(ids[m : m + 1, :]).astype(jnp.int32)
            out[target] += block.T


def shards(sizes, psi, left_ops, right_ops, left_qn, right_qn, pair_slot, slot_target):
    rows, blocks, halves = sizes
    sectors, width = psi.shape[0], psi.shape[1]
    operators, left_local = left_ops.shape[0], left_ops.shape[1]
    slots = pair_slot.T
    smem = pl.BlockSpec(memory_space=pltpu.SMEM)
    vmem = pl.BlockSpec(memory_space=pltpu.VMEM)
    hbm = pl.BlockSpec(memory_space=pltpu.HBM)
    total_shape = (rows * CAP + 1, width, width)
    right_count = right_ops.shape[1]
    lists = [pltpu.SMEM((sectors + 1,), jnp.int32), pltpu.SMEM((blocks * left_local + 1,), jnp.int32)]
    params = pltpu.CompilerParams(vmem_limit_bytes=12 * 2**20)

    def cost(share):
        flops = int(16 * operators * sectors * width**3 * share)
        return pl.CostEstimate(flops=flops, bytes_accessed=4 * 2**20, transcendentals=0)

    first = lax.rem(lax.axis_index("sector"), 2) * (operators // 2)
    quarter = operators // 4
    swap = [(i, i ^ 1) for i in range(rows)]
    sent = [lax.dynamic_slice_in_dim(left_ops, first + i * quarter, quarter, 0) for i in range(2)]
    near = [
        [lax.ppermute(part, "blk", [((b + d) % blocks, b) for b in range(blocks)]) for d in range(1, blocks)]
        for part in sent
    ]
    half = pl.pallas_call(
        functools.partial(right_kernel, blocks, left_local),
        out_shape=jax.ShapeDtypeStruct((sectors // GROUP, operators, GROUP // 2, width, 2 * width), jnp.bfloat16),
        in_specs=[hbm] * 4,
        out_specs=vmem,
        scratch_shapes=[
            pltpu.SMEM(left_qn.shape, jnp.int32),
            pltpu.SMEM(right_qn.shape, jnp.int32),
            pltpu.VMEM(psi.shape, psi.dtype),
            pltpu.VMEM(right_ops.shape, right_ops.dtype),
            pltpu.VMEM((sectors // 2, 2 * width, right_count * width), jnp.bfloat16),
            *lists,
            pltpu.SemaphoreType.DMA((3 + operators // BLOCK_K,)),
        ],
        compiler_params=params,
        cost_estimate=cost(0.5),
        name="right_side",
    )(*(pltpu.with_memory_space_constraint(x, pltpu.HBM) for x in (left_qn, right_qn, psi, right_ops)))
    half, near = lax.optimization_barrier((half, near))
    far = [[lax.ppermute(part, "sector", swap) for part in parts] for parts in near]
    near, far = ([jnp.stack(parts) for parts in side] for side in (near, far))
    total = pl.pallas_call(
        functools.partial(own_kernel, blocks),
        out_shape=jax.ShapeDtypeStruct(total_shape, jnp.float32),
        in_specs=[smem] * 2 + [vmem] * 2,
        out_specs=vmem,
        scratch_shapes=lists,
        compiler_params=params,
        cost_estimate=cost(0.25),
        name="own_left",
    )(left_qn, slots, half, left_ops)
    common = (left_qn, slots, slot_target, half)
    total = pl.pallas_call(
        functools.partial(other_kernel, False, 0),
        out_shape=jax.ShapeDtypeStruct(total_shape, jnp.float32),
        in_specs=[smem] * 3 + [vmem] * 4,
        out_specs=vmem,
        scratch_shapes=lists,
        compiler_params=params,
        cost_estimate=cost(0.125),
        name="other_left_near",
    )(*common, total, *near)
    partial = pl.pallas_call(
        functools.partial(other_kernel, True, 1),
        out_shape=[jax.ShapeDtypeStruct((CAP * width + TAIL, width), jnp.bfloat16)] * rows,
        in_specs=[smem] * 3 + [vmem] * 4,
        out_specs=[vmem] * rows,
        scratch_shapes=[pltpu.VMEM(total_shape, jnp.float32), *lists],
        compiler_params=params,
        cost_estimate=cost(0.125),
        name="other_left_far",
    )(*common, total, *far)
    mine = [partial[0]] + [
        lax.ppermute(partial[d], "sector", [(i, (i + d) % rows) for i in range(rows)]) for d in range(1, rows)
    ]
    theirs = [lax.ppermute(block, "op", [(h, halves - 1 - h) for h in range(halves)]) for block in mine]
    return pl.pallas_call(
        functools.partial(assemble_kernel, rows),
        out_shape=jax.ShapeDtypeStruct((sectors, width, width), jnp.float32),
        in_specs=[vmem] * (2 * rows),
        out_specs=vmem,
        compiler_params=params,
        name="assemble",
    )(*mine, *theirs)


def solution(mesh):
    in_specs = (
        P(("groups", "sector", "blk"), None, None),
        P(("groups", "op"), "blk", None, None),
        P(("groups", "op"), None, None, None),
        P(("groups", "sector", "blk")),
        P(("groups", "sector", "blk")),
        P(("groups", "op"), ("sector", "blk")),
        P(("groups", "sector"), "blk", None),
    )
    out_specs = P(("groups", "sector", "blk"), None, None)
    sizes = tuple(mesh.shape[name] for name in ("sector", "blk", "op"))
    return jax.shard_map(
        functools.partial(shards, sizes), mesh=mesh, in_specs=in_specs, out_specs=out_specs, check_vma=False
    )
```

time: 55.7 us -> 51.9 us (0.932)
  starting transfers between devices: 11.3 us -> 9.14 us
  local copies, waits for them, and re-layouts: 2.31 us -> 1.08 us
    ppermute x2, waiting for transfers between devices: 4.76 us -> 0.9 us  [shards(): lax.ppermute(part, 'sector', swap)]
    ppermute x2, waiting for transfers between devices: 0.01 us -> 2.89 us  [shards(): lax.ppermute(part, 'blk', [((b + d) % blocks, b) for b in range(blocks)])]
    ppermute x3, starting transfers between devices: 6.11 us -> 4 us  [shards(): lax.ppermute(partial[d], 'sector', [(i, (i + d) % rows) for i in range(ro...]
    unnamed x14 -> x8, local copies, waits for them, and re-layouts: 1.25 us -> 0.01 us
    ppermute x3, waiting for transfers between devices: 9.42 us -> 10.1 us  [shards(): lax.ppermute(partial[d], 'sector', [(i, (i + d) % rows) for i in range(ro...]
    pallas_call x1 -> x2, Pallas kernels: 14 us -> 13.5 us  [the longest x1 8.9 us: shards(): pl.pallas_call(functools.partial(right_kernel, blocks, left_local), out_s...]
  transfers between devices with their start and end apart: 11 -> 11, of which waited for: 6 -> 6; matrix products, arithmetic and copies ran while one was open for 0% -> 0% of each run, Pallas kernels for 35% -> 37%
where the time goes in v3:
time: 51.9 us; the launch traced here: 51.7 us
  Pallas kernels  26.2 us (50%)
  waiting for transfers between devices  15.2 us (29%)
  starting transfers between devices  9.14 us (18%)
  local copies, waits for them, and re-layouts  1.08 us (2%)
    ppermute x3, waiting for transfers between devices, shards(): lax.ppermute(partial[d], 'sector', [(i, (i + d) % rows) for i in range(ro...  10.1 us
    pallas_call x1, Pallas kernels, shards(): pl.pallas_call(functools.partial(right_kernel, blocks, left_local), out_s...  8.9 us
    pallas_call x1, Pallas kernels, shards(): pl.pallas_call(functools.partial(other_kernel, True, 1), out_shape=[jax.S...  5.6 us
    pallas_call x1, Pallas kernels, shards(): pl.pallas_call(functools.partial(other_kernel, False, 0), out_shape=jax.S...  5.57 us
    pallas_call x1, Pallas kernels, shards(): pl.pallas_call(functools.partial(own_kernel, blocks), out_shape=jax.Shape...  4.56 us
    ppermute x3, starting transfers between devices, shards(): lax.ppermute(partial[d], 'sector', [(i, (i + d) % rows) for i in range(ro...  4 us
    ppermute x2, starting transfers between devices, shards(): lax.ppermute(part, 'blk', [((b + d) % blocks, b) for b in range(blocks)])  3.11 us
    ppermute x2, waiting for transfers between devices, shards(): lax.ppermute(part, 'blk', [((b + d) % blocks, b) for b in range(blocks)])  2.89 us
  transfers between devices with their start and end apart: 11, of which 6 were waited for; matrix products, arithmetic and copies ran while one was open for 0% of the time, Pallas kernels for 37%

profile of v3, /device:TPU:0, one launch (start us, length us, event | category | flops | bytes accessed | tf_op | source)
XLA Modules:
  0.0 51.7 jit_solution(11140875097868524393)
XLA Ops:
  0.0 1.1 %constant_dynamic-slice_fusion = (bf16[8,1,128,128]{3,2,0,1:T(8,128)(2,1)S(1)}, bf16[8,1,128,128]{3,2,0,1:T(8,128)(2,1)S(1)}) fusion(bf16[32,1,128,128]{3,2,0,1:T(8,128)(2,1)} %bitcast.10, s32[]{:T(128)S(6)} %select_n.7, s32[]{:T(128)S(6)} %select_n.6), kind=kLoop, calls=%fused_computation | loop fusion | bytes 1048584 | tf_op jit(solution)/shard_map/dynamic_slice | solution.py:190
  1.1 3.0 %collective-permute-start = (bf16[8,1,128,128]{3,2,0,1:T(8,128)(2,1)S(1)}, bf16[8,1,128,128]{3,2,0,1:T(8,128)(2,1)S(1)}, u32[]{:S(2)}, u32[]{:S(2)}) collective-permute-start(bf16[8,1,128,128]{3,2,0,1:T(8,128)(2,1)S(1)} %get-tuple-element.20), channel_id=1, source_target_pairs={{2,0},{0,2},{3,1},{1,3},{6,4},{4,6},{7,5},{5,7},{10,8},{8,10},{11,... | collective-permute-start | bytes 786440 | tf_op jit(solution)/shard_map/ppermute | solution.py:192
  4.1 0.1 collective-permute-start.1
  4.2 8.9 %right_side.1.half = bf16[6,32,2,128,256]{4,3,2,1,0:T(8,128)(2,1)S(1)} custom-call(s32[24]{0:T(128)} %left_qn.5, s32[24]{0:T(128)} %right_qn_in.1, bf16[24,128,128]{2,1,0:T(8,128)(2,1)} %psi_in.1, bf16[32,2,128,128]{3,2,1,0:T(8,128)(2,1)} %right_in.1), custom_call_target="tpu_custom_call" | custom-call | flops 12884901888 | bytes 4194304 | tf_op jit(solution)/shard_map/right_side/pallas_call | solution.py:195
  13.1 0.0 collective-permute-done
  13.1 2.9 %collective-permute-done.1 = bf16[8,1,128,128]{3,2,0,1:T(8,128)(2,1)S(1)} collective-permute-done((bf16[8,1,128,128]{3,2,0,1:T(8,128)(2,1)S(1)}, bf16[8,1,128,128]{3,2,0,1:T(8,128)(2,1)S(1)}, u32[]{:S(2)}, u32[]{:S(2)}) %collective-permute-start.1) | collective-permute-done | bytes 262176 | tf_op jit(solution)/shard_map/ppermute | solution.py:192
  16.0 1.8 %collective-permute-start.2 = (bf16[8,1,128,128]{3,2,0,1:T(8,128)(2,1)S(1)}, bf16[8,1,128,128]{3,2,0,1:T(8,128)(2,1)S(1)}, u32[]{:S(2)}, u32[]{:S(2)}) collective-permute-start(bf16[8,1,128,128]{3,2,0,1:T(8,128)(2,1)S(1)} %collective-permute-done), channel_id=1, source_target_pairs={{0,4},{4,0},{8,12},{12,8},{1,5},{5,1},{9,13},{13,9},{2,6},{6,2},{1... | collective-permute-start | bytes 786440 | tf_op jit(solution)/shard_map/ppermute | solution.py:214
  17.8 0.2 collective-permute-start.3
  18.0 0.0 copy-done
  18.0 0.0 copy-done.1
  18.0 0.0 copy-done.2
  18.0 4.6 %own_left.1.start = f32[17,128,128]{2,1,0:T(8,128)S(1)} custom-call(s32[24]{0:T(128)S(1)} %copy-done.2, s32[24,32]{1,0:T(8,128)S(1)} %bitcast.15, bf16[6,32,2,128,256]{4,3,2,1,0:T(8,128)(2,1)S(1)} %right_side.1.half, bf16[32,1,128,128]{3,2,1,0:T(8,128)(2,1)S(1)} %copy-done), custom_call_target="tpu_custom_call" | custom-call | flops 6442450944 | bytes 4194304 | tf_op jit(solution)/shard_map/own_left/pallas_call | solution.py:216
  22.6 0.0 copy-done.3
  22.6 5.6 %other_left_near.1.start = f32[17,128,128]{2,1,0:T(8,128)S(1)} custom-call(s32[24]{0:T(128)S(1)} %copy-done.2, s32[24,32]{1,0:T(8,128)S(1)} %bitcast.16, s32[1,1,16]{2,1,0:T(1,128)S(1)} %copy-done.3, bf16[6,32,2,128,256]{4,3,2,1,0:T(8,128)(2,1)S(1)} %right_side.1.half, f32[17,128,128]{2,1,0:T(8,128)S(1)} %own_left.1.start, ...), custom_call_target="tpu_custom_call" | custom-call | flops 3221225472 | bytes 4194304 | tf_op jit(solution)/shard_map/other_left_near/pallas_call | solution.py:227
  28.2 0.0 collective-permute-done.2
  28.2 0.9 %collective-permute-done.3 = bf16[8,1,128,128]{3,2,0,1:T(8,128)(2,1)S(1)} collective-permute-done((bf16[8,1,128,128]{3,2,0,1:T(8,128)(2,1)S(1)}, bf16[8,1,128,128]{3,2,0,1:T(8,128)(2,1)S(1)}, u32[]{:S(2)}, u32[]{:S(2)}) %collective-permute-start.3) | collective-permute-done | bytes 262176 | tf_op jit(solution)/shard_map/ppermute | solution.py:214
  29.1 5.6 %other_left_far.1 = (bf16[528,128]{1,0:T(8,128)(2,1)S(1)}, bf16[528,128]{1,0:T(8,128)(2,1)S(1)}, bf16[528,128]{1,0:T(8,128)(2,1)S(1)}, bf16[528,128]{1,0:T(8,128)(2,1)S(1)}) custom-call(s32[24]{0:T(128)S(1)} %copy-done.2, s32[24,32]{1,0:T(8,128)S(1)} %bitcast.17, s32[1,1,16]{2,1,0:T(1,128)S(1)} %copy-done.3, ...), custom_call_target="tpu_custom_call" | custom-call | flops 3221225472 | bytes 4194304 | tf_op jit(solution)/shard_map/other_left_far/pallas_call | solution.py:237
  34.7 3.0 %collective-permute-start.6 = (bf16[528,128]{1,0:T(8,128)(2,1)S(1)}, bf16[528,128]{1,0:T(8,128)(2,1)S(1)}, u32[]{:S(2)}, u32[]{:S(2)}) collective-permute-start(bf16[528,128]{1,0:T(8,128)(2,1)S(1)} %get-tuple-element.18), channel_id=1, source_target_pairs={{0,12},{4,0},{8,4},{12,8},{1,13},{5,1},{9,5},{13,9},{2,14},{6,2},{... | collective-permute-start | bytes 405512 | tf_op jit(solution)/shard_map/ppermute | solution.py:248
  37.7 0.0 collective-permute-start.4
  37.7 1.0 %collective-permute-start.5 = (bf16[528,128]{1,0:T(8,128)(2,1)S(1)}, bf16[528,128]{1,0:T(8,128)(2,1)S(1)}, u32[]{:S(2)}, u32[]{:S(2)}) collective-permute-start(bf16[528,128]{1,0:T(8,128)(2,1)S(1)} %get-tuple-element.17), channel_id=1, source_target_pairs={{0,8},{4,12},{8,0},{12,4},{1,9},{5,13},{9,1},{13,5},{2,10},{6,14},... | collective-permute-start | bytes 405512 | tf_op jit(solution)/shard_map/ppermute | solution.py:248
  38.7 0.0 collective-permute-start.7
  38.7 3.0 %collective-permute-done.6.rest_3_ = bf16[528,128]{1,0:T(8,128)(2,1)S(1)} collective-permute-done((bf16[528,128]{1,0:T(8,128)(2,1)S(1)}, bf16[528,128]{1,0:T(8,128)(2,1)S(1)}, u32[]{:S(2)}, u32[]{:S(2)}) %collective-permute-start.6) | collective-permute-done | bytes 135200 | tf_op jit(solution)/shard_map/ppermute | solution.py:248
  41.8 0.0 collective-permute-start.10
  41.8 3.7 %collective-permute-done.4.rest_1_ = bf16[528,128]{1,0:T(8,128)(2,1)S(1)} collective-permute-done((bf16[528,128]{1,0:T(8,128)(2,1)S(1)}, bf16[528,128]{1,0:T(8,128)(2,1)S(1)}, u32[]{:S(2)}, u32[]{:S(2)}) %collective-permute-start.4) | collective-permute-done | bytes 135200 | tf_op jit(solution)/shard_map/ppermute | solution.py:248
  45.5 0.0 collective-permute-start.8
  45.5 3.3 %collective-permute-done.5.rest_2_ = bf16[528,128]{1,0:T(8,128)(2,1)S(1)} collective-permute-done((bf16[528,128]{1,0:T(8,128)(2,1)S(1)}, bf16[528,128]{1,0:T(8,128)(2,1)S(1)}, u32[]{:S(2)}, u32[]{:S(2)}) %collective-permute-start.5) | collective-permute-done | bytes 135200 | tf_op jit(solution)/shard_map/ppermute | solution.py:248
  48.8 0.0 collective-permute-start.9
  48.8 0.0 collective-permute-done.7.rest_4_
  48.8 0.0 collective-permute-done.10.rest_7_
  48.8 0.0 collective-permute-done.8.rest_5_
  48.8 1.3 %collective-permute-done.9.rest_6_ = bf16[528,128]{1,0:T(8,128)(2,1)S(1)} collective-permute-done((bf16[528,128]{1,0:T(8,128)(2,1)S(1)}, bf16[528,128]{1,0:T(8,128)(2,1)S(1)}, u32[]{:S(2)}, u32[]{:S(2)}) %collective-permute-start.9) | collective-permute-done | bytes 135200 | tf_op jit(solution)/shard_map/ppermute | solution.py:250
  50.1 1.6 %assemble.1 = f32[24,128,128]{2,1,0:T(8,128)} custom-call(bf16[528,128]{1,0:T(8,128)(2,1)S(1)} %get-tuple-element.15.rest_0_, bf16[528,128]{1,0:T(8,128)(2,1)S(1)} %collective-permute-done.4.rest_1_, bf16[528,128]{1,0:T(8,128)(2,1)S(1)} %collective-permute-done.5.rest_2_, bf16[528,128]{1,0:T(8,128)(2,1)S(1)} %collective-permute-done.6.rest_3_, ...), custom_call_target="tpu_custom_call" | custom-call | tf_op jit(solution)/shard_map/assemble/pallas_call | solution.py:251
  (4 shorter events, 0.0 us)
Async XLA Ops:
  1.1 12.0 %collective-permute-start = (bf16[8,1,128,128]{3,2,0,1:T(8,128)(2,1)S(1)}, bf16[8,1,128,128]{3,2,0,1:T(8,128)(2,1)S(1)}, u32[]{:S(2)}, u32[]{:S(2)}) collective-permute-start(bf16[8,1,128,128]{3,2,0,1:T(8,128)(2,1)S(1)} %get-tuple-element.20), channel_id=1, source_target_pairs={{2,0},{0,2},{3,1},{1,3},{6,4},{4,6},{7,5},{5,7},{10,8},{8,10},{11,... | collective-permute-start | bytes 786440 | tf_op jit(solution)/shard_map/ppermute | solution.py:192
  4.1 14.0 %copy-start = (bf16[32,1,128,128]{3,2,1,0:T(8,128)(2,1)S(1)}, bf16[32,1,128,128]{3,2,1,0:T(8,128)(2,1)}, u32[]{:S(2)}) copy-start(bf16[32,1,128,128]{3,2,1,0:T(8,128)(2,1)} %left.1) | copy-start | bytes 3145732
  4.1 14.0 %copy-start.1 = (s32[32,24]{0,1:T(8,128)S(1)}, s32[32,24]{0,1:T(8,128)}, u32[]{:S(2)}) copy-start(s32[32,24]{0,1:T(8,128)} %param.12) | copy-start | bytes 9220
  4.1 14.0 %copy-start.2 = (s32[24]{0:T(128)S(1)}, s32[24]{0:T(128)}, u32[]{:S(2)}) copy-start(s32[24]{0:T(128)} %left_qn.5) | copy-start | bytes 292
  4.1 11.9 %collective-permute-start.1 = (bf16[8,1,128,128]{3,2,0,1:T(8,128)(2,1)S(1)}, bf16[8,1,128,128]{3,2,0,1:T(8,128)(2,1)S(1)}, u32[]{:S(2)}, u32[]{:S(2)}) collective-permute-start(bf16[8,1,128,128]{3,2,0,1:T(8,128)(2,1)S(1)} %get-tuple-element.19), channel_id=1, source_target_pairs={{2,0},{0,2},{3,1},{1,3},{6,4},{4,6},{7,5},{5,7},{10,8},{8,10},{11,... | collective-permute-start | bytes 786440 | tf_op jit(solution)/shard_map/ppermute | solution.py:192
  16.0 12.2 %collective-permute-start.2 = (bf16[8,1,128,128]{3,2,0,1:T(8,128)(2,1)S(1)}, bf16[8,1,128,128]{3,2,0,1:T(8,128)(2,1)S(1)}, u32[]{:S(2)}, u32[]{:S(2)}) collective-permute-start(bf16[8,1,128,128]{3,2,0,1:T(8,128)(2,1)S(1)} %collective-permute-done), channel_id=1, source_target_pairs={{0,4},{4,0},{8,12},{12,8},{1,5},{5,1},{9,13},{13,9},{2,6},{6,2},{1... | collective-permute-start | bytes 786440 | tf_op jit(solution)/shard_map/ppermute | solution.py:214
  17.8 11.3 %collective-permute-start.3 = (bf16[8,1,128,128]{3,2,0,1:T(8,128)(2,1)S(1)}, bf16[8,1,128,128]{3,2,0,1:T(8,128)(2,1)S(1)}, u32[]{:S(2)}, u32[]{:S(2)}) collective-permute-start(bf16[8,1,128,128]{3,2,0,1:T(8,128)(2,1)S(1)} %collective-permute-done.1), channel_id=1, source_target_pairs={{0,4},{4,0},{8,12},{12,8},{1,5},{5,1},{9,13},{13,9},{2,6},{6,2},{1... | collective-permute-start | bytes 786440 | tf_op jit(solution)/shard_map/ppermute | solution.py:214
  18.0 4.6 %copy-start.3 = (s32[1,1,16]{2,1,0:T(1,128)S(1)}, s32[1,1,16]{2,1,0:T(1,128)}, u32[]{:S(2)}) copy-start(s32[1,1,16]{2,1,0:T(1,128)} %slot_target.3) | copy-start | bytes 196
  34.7 7.0 %collective-permute-start.6 = (bf16[528,128]{1,0:T(8,128)(2,1)S(1)}, bf16[528,128]{1,0:T(8,128)(2,1)S(1)}, u32[]{:S(2)}, u32[]{:S(2)}) collective-permute-start(bf16[528,128]{1,0:T(8,128)(2,1)S(1)} %get-tuple-element.18), channel_id=1, source_target_pairs={{0,12},{4,0},{8,4},{12,8},{1,13},{5,1},{9,5},{13,9},{2,14},{6,2},{... | collective-permute-start | bytes 405512 | tf_op jit(solution)/shard_map/ppermute | solution.py:248
  37.7 7.8 %collective-permute-start.4 = (bf16[528,128]{1,0:T(8,128)(2,1)S(1)}, bf16[528,128]{1,0:T(8,128)(2,1)S(1)}, u32[]{:S(2)}, u32[]{:S(2)}) collective-permute-start(bf16[528,128]{1,0:T(8,128)(2,1)S(1)} %get-tuple-element.16), channel_id=1, source_target_pairs={{0,4},{4,8},{8,12},{12,0},{1,5},{5,9},{9,13},{13,1},{2,6},{6,10},{... | collective-permute-start | bytes 405512 | tf_op jit(solution)/shard_map/ppermute | solution.py:248
  37.7 11.1 %collective-permute-start.5 = (bf16[528,128]{1,0:T(8,128)(2,1)S(1)}, bf16[528,128]{1,0:T(8,128)(2,1)S(1)}, u32[]{:S(2)}, u32[]{:S(2)}) collective-permute-start(bf16[528,128]{1,0:T(8,128)(2,1)S(1)} %get-tuple-element.17), channel_id=1, source_target_pairs={{0,8},{4,12},{8,0},{12,4},{1,9},{5,13},{9,1},{13,5},{2,10},{6,14},... | collective-permute-start | bytes 405512 | tf_op jit(solution)/shard_map/ppermute | solution.py:248
  38.7 10.1 %collective-permute-start.7 = (bf16[528,128]{1,0:T(8,128)(2,1)S(1)}, bf16[528,128]{1,0:T(8,128)(2,1)S(1)}, u32[]{:S(2)}, u32[]{:S(2)}) collective-permute-start(bf16[528,128]{1,0:T(8,128)(2,1)S(1)} %get-tuple-element.15.rest_0_), channel_id=1, source_target_pairs={{0,1},{1,0},{2,3},{3,2},{4,5},{5,4},{6,7},{7,6},{8,9},{9,8},{10,11... | collective-permute-start | bytes 405512 | tf_op jit(solution)/shard_map/ppermute | solution.py:250
  41.8 7.0 %collective-permute-start.10 = (bf16[528,128]{1,0:T(8,128)(2,1)S(1)}, bf16[528,128]{1,0:T(8,128)(2,1)S(1)}, u32[]{:S(2)}, u32[]{:S(2)}) collective-permute-start(bf16[528,128]{1,0:T(8,128)(2,1)S(1)} %collective-permute-done.6.rest_3_), channel_id=1, source_target_pairs={{0,1},{1,0},{2,3},{3,2},{4,5},{5,4},{6,7},{7,6},{8,9},{9,8},{10,11... | collective-permute-start | bytes 405512 | tf_op jit(solution)/shard_map/ppermute | solution.py:250
  45.5 3.3 %collective-permute-start.8 = (bf16[528,128]{1,0:T(8,128)(2,1)S(1)}, bf16[528,128]{1,0:T(8,128)(2,1)S(1)}, u32[]{:S(2)}, u32[]{:S(2)}) collective-permute-start(bf16[528,128]{1,0:T(8,128)(2,1)S(1)} %collective-permute-done.4.rest_1_), channel_id=1, source_target_pairs={{0,1},{1,0},{2,3},{3,2},{4,5},{5,4},{6,7},{7,6},{8,9},{9,8},{10,11... | collective-permute-start | bytes 405512 | tf_op jit(solution)/shard_map/ppermute | solution.py:250
  48.8 1.4 %collective-permute-start.9 = (bf16[528,128]{1,0:T(8,128)(2,1)S(1)}, bf16[528,128]{1,0:T(8,128)(2,1)S(1)}, u32[]{:S(2)}, u32[]{:S(2)}) collective-permute-start(bf16[528,128]{1,0:T(8,128)(2,1)S(1)} %collective-permute-done.5.rest_2_), channel_id=1, source_target_pairs={{0,1},{1,0},{2,3},{3,2},{4,5},{5,4},{6,7},{7,6},{8,9},{9,8},{10,11... | collective-permute-start | bytes 405512 | tf_op jit(solution)/shard_map/ppermute | solution.py:250

commit v4 on v3

v4 whole, which is shorter than its diff:
```python
import functools

import jax
import jax.numpy as jnp
from jax import lax
from jax.experimental import pallas as pl
from jax.experimental.pallas import tpu as pltpu
from jax.sharding import PartitionSpec as P

CAP = 4
GROUP = 4
SETS = 4
MOST_SLOTS = 64
BLOCK_K = 8
TAIL = 16
NT = (((1,), (1,)), ((), ()))


def arrange(left_qn, plan, blocks, left_local):
    mine = lax.axis_index("blk")
    count = left_qn.shape[0]

    def one_code(code, n):
        plan[count + 1 + code] = n
        owner = lax.rem(mine + lax.div(code, jnp.int32(left_local)), jnp.int32(blocks))
        wanted = owner * left_local + lax.rem(code, jnp.int32(left_local))

        def one_sector(s, n):
            plan[n] = s
            return n + (left_qn[s] == wanted).astype(jnp.int32)

        return lax.fori_loop(0, count, one_sector, n)

    plan[count + 1 + blocks * left_local] = lax.fori_loop(0, blocks * left_local, one_code, jnp.int32(0))


def right_kernel(
    blocks, left_local, left_qn_in, right_qn_in, psi_in, right_in, half, plan,
    left_qn, right_qn, psi, right, sources, sems,
):
    sectors, width = psi.shape[0], psi.shape[1]
    right_count = right.shape[1]
    steps = right.shape[0] // BLOCK_K
    zero = jnp.zeros((width, width), jnp.bfloat16)

    def right_copy(i):
        at = pl.ds(i * BLOCK_K, BLOCK_K)
        return pltpu.make_async_copy(right_in.at[at], right.at[at], sems.at[3 + i])

    copies = [
        pltpu.make_async_copy(left_qn_in, left_qn, sems.at[0]),
        pltpu.make_async_copy(right_qn_in, right_qn, sems.at[1]),
        pltpu.make_async_copy(psi_in, psi, sems.at[2]),
    ]
    for copy in copies:
        copy.start()
    for i in range(steps):
        right_copy(i).start()
    copies[0].wait()
    copies[1].wait()
    arrange(left_qn, plan, blocks, left_local)
    copies[2].wait()
    for pair in range(sectors // 2):
        for e in range(2):
            s = plan[2 * pair + e]
            block = psi[s]
            for r in range(right_count):
                sources[pair, e * width : (e + 1) * width, r * width : (r + 1) * width] = jnp.where(
                    right_qn[s] == r, block, zero
                )

    def one_step(i, unused):
        right_copy(i).wait()
        at = pl.ds(i * BLOCK_K, BLOCK_K)
        stream = jnp.concatenate([right[at, r].reshape(BLOCK_K * width, width) for r in range(right_count)], axis=1)
        for pair in range(sectors // 2):
            product = lax.dot_general(stream, sources[pair], NT, preferred_element_type=jnp.float32)
            half[pair // 2, at, pair % 2] = product.astype(jnp.bfloat16).reshape(BLOCK_K, width, 2 * width)
        return unused

    lax.fori_loop(0, steps, one_step, 0)


def accumulate(code, pieces, plan, slots, half, totals):
    sectors, width = slots.shape[0], totals[0].shape[1]
    spare = totals[0].shape[0] - 1
    low, high = plan[sectors + 1 + code], plan[sectors + 2 + code]
    zero = jnp.zeros((width, width), jnp.bfloat16)

    def one_group(g, unused):
        places = [g * GROUP + j for j in range(GROUP)]
        members = [plan[at] for at in places]
        counts = [(low <= at) & (at < high) for at in places]
        for first, left in pieces:
            for i in range(left.shape[0]):
                k = first + i
                block = left[i]
                weights = jnp.concatenate(
                    [jnp.concatenate([block, zero], axis=1), jnp.concatenate([zero, block], axis=1)], axis=0
                )
                term = lax.dot_general(
                    half[g, k].reshape(GROUP // 2 * width, 2 * width),
                    weights,
                    NT,
                    preferred_element_type=jnp.float32,
                )
                for j in range(GROUP):
                    p, e = j // 2, j % 2
                    slot = jnp.where(counts[j], slots[members[j], k], spare)
                    totals[j % len(totals)][slot] += term[p * width : (p + 1) * width, e * width : (e + 1) * width]
        return unused

    groups = jnp.where(low < high, lax.div(high + GROUP - 1, jnp.int32(GROUP)), 0)
    lax.fori_loop(lax.div(low, jnp.int32(GROUP)), groups, one_group, 0)


def own_kernel(plan, slots, half, left, *totals):
    for total in totals:
        total[...] = jnp.zeros_like(total)
    for l in range(left.shape[1]):
        accumulate(l, [(0, left.at[:, l])], plan, slots, half, totals)


def other_kernel(rows, sets, plan, slots, half, swapped, direct, middle, *rest):
    totals, (keep, give) = rest[sets : 2 * sets], rest[2 * sets :]
    shifts, quarter, left_local = swapped.shape[0], swapped.shape[1], swapped.shape[2]
    row, side = lax.axis_index("sector"), lax.axis_index("op")
    operators, width = slots.shape[1], totals[0].shape[1]
    odd = lax.rem(row, jnp.int32(2))
    near = odd * (operators - quarter)
    far = (1 - odd) * (operators - quarter)

    def one_shift(d, unused):
        for l in range(left_local):
            pieces = [
                (near, direct.at[d, :, l]), (quarter, middle.at[d, :, l]), (far, swapped.at[d, :, l])
            ]
            accumulate((d + 1) * left_local + l, pieces, plan, slots, half, totals)
        return unused

    lax.fori_loop(0, shifts, one_shift, 0)
    part = CAP // 2
    for owner in range(rows):
        for m in range(part):
            at = owner * CAP + side * part + m
            keep[owner * part + m] = sum(total[at] for total in totals)
            at = owner * CAP + (1 - side) * part + m
            give[owner * part + m] = sum(total[at] for total in totals).astype(jnp.bfloat16)


def combine_kernel(slot_target, keep, taken, *outs):
    part, width = CAP // 2, keep.shape[1]
    row, side = lax.axis_index("sector"), lax.axis_index("op")
    line = lax.broadcasted_iota(jnp.int32, (TAIL, width), 0)
    for d, out in enumerate(outs):
        owner = lax.rem(row + d, jnp.int32(len(outs)))
        ids = jnp.zeros((TAIL, width), jnp.int32)
        for m in range(part):
            block = keep[owner * part + m] + taken[owner * part + m].astype(jnp.float32)
            out[m * width : (m + 1) * width, :] = block.astype(jnp.bfloat16)
            ids = jnp.where(line == m, slot_target[0, 0, owner * CAP + side * part + m], ids)
        out[part * width :, :] = ids.astype(jnp.float32).astype(jnp.bfloat16)


def assemble_kernel(rows, *rest):
    mine, theirs, out = rest[:rows], rest[rows : 2 * rows], rest[-1]
    part, width = CAP // 2, out.shape[1]
    side = lax.axis_index("op")
    out[...] = jnp.zeros_like(out)
    for d in range(rows):
        for h in range(2):
            ids = jnp.where(side == h, mine[d][part * width :, :], theirs[d][part * width :, :]).astype(jnp.float32)
            for m in range(part):
                at = pl.ds(m * width, width)
                block = jnp.where(side == h, mine[d][at, :], theirs[d][at, :]).astype(jnp.float32)
                target = jnp.max(ids[m : m + 1, :]).astype(jnp.int32)
                out[target] += block.T


def shards(sizes, psi, left_ops, right_ops, left_qn, right_qn, pair_slot, slot_target):
    rows, blocks, halves = sizes
    sectors, width = psi.shape[0], psi.shape[1]
    operators, left_local = left_ops.shape[0], left_ops.shape[1]
    slots = pair_slot.T
    smem = pl.BlockSpec(memory_space=pltpu.SMEM)
    vmem = pl.BlockSpec(memory_space=pltpu.VMEM)
    hbm = pl.BlockSpec(memory_space=pltpu.HBM)
    sets = max(1, min(SETS, MOST_SLOTS // (rows * CAP)))
    total_shape = (rows * CAP + 1, width, width)
    right_count = right_ops.shape[1]
    params = pltpu.CompilerParams(vmem_limit_bytes=12 * 2**20)

    def cost(share):
        flops = int(16 * operators * sectors * width**3 * share)
        return pl.CostEstimate(flops=flops, bytes_accessed=4 * 2**20, transcendentals=0)

    odd = lax.rem(lax.axis_index("sector"), 2)
    quarter = operators // 4
    swap = [(i, i ^ 1) for i in range(rows)]

    def over_blocks(part):
        return [lax.ppermute(part, "blk", [((b + d) % blocks, b) for b in range(blocks)]) for d in range(1, blocks)]

    direct = over_blocks(lax.dynamic_slice_in_dim(left_ops, odd * (operators - quarter), quarter, 0))
    middle = over_blocks(left_ops[quarter : operators - quarter])

    half, plan = pl.pallas_call(
        functools.partial(right_kernel, blocks, left_local),
        out_shape=[
            jax.ShapeDtypeStruct((sectors // GROUP, operators, GROUP // 2, width, 2 * width), jnp.bfloat16),
            jax.ShapeDtypeStruct((sectors + 2 + blocks * left_local,), jnp.int32),
        ],
        in_specs=[hbm] * 4,
        out_specs=[vmem, smem],
        scratch_shapes=[
            pltpu.SMEM(left_qn.shape, jnp.int32),
            pltpu.SMEM(right_qn.shape, jnp.int32),
            pltpu.VMEM(psi.shape, psi.dtype),
            pltpu.VMEM(right_ops.shape, right_ops.dtype),
            pltpu.VMEM((sectors // 2, 2 * width, right_count * width), jnp.bfloat16),
            pltpu.SemaphoreType.DMA((3 + operators // BLOCK_K,)),
        ],
        compiler_params=params,
        cost_estimate=cost(0.5),
        name="right_side",
    )(*(pltpu.with_memory_space_constraint(x, pltpu.HBM) for x in (left_qn, right_qn, psi, right_ops)))
    half, direct = lax.optimization_barrier((half, direct))
    swapped = [lax.ppermute(part, "sector", swap) for part in direct]
    totals = pl.pallas_call(
        own_kernel,
        out_shape=[jax.ShapeDtypeStruct(total_shape, jnp.float32)] * sets,
        in_specs=[smem] * 2 + [vmem] * 2,
        out_specs=[vmem] * sets,
        compiler_params=params,
        cost_estimate=cost(0.25),
        name="own_left",
    )(plan, slots, half, left_ops)
    results = pl.pallas_call(
        functools.partial(other_kernel, rows, sets),
        out_shape=[jax.ShapeDtypeStruct(total_shape, jnp.float32)] * sets
        + [jax.ShapeDtypeStruct((rows * CAP // 2, width, width), kind) for kind in (jnp.float32, jnp.bfloat16)],
        in_specs=[smem] * 2 + [vmem] * (4 + sets),
        out_specs=[vmem] * (sets + 2),
        input_output_aliases={6 + j: j for j in range(sets)},
        compiler_params=params,
        cost_estimate=cost(0.25),
        name="other_left",
    )(plan, slots, half, jnp.stack(swapped), jnp.stack(direct), jnp.stack(middle), *totals)
    keep, give = results[sets:]

    def over_cores(block):
        return lax.ppermute(block, "op", [(h, halves - 1 - h) for h in range(halves)])

    partial = pl.pallas_call(
        combine_kernel,
        out_shape=[jax.ShapeDtypeStruct((CAP // 2 * width + TAIL, width), jnp.bfloat16)] * rows,
        in_specs=[smem] + [vmem] * 2,
        out_specs=[vmem] * rows,
        compiler_params=params,
        name="combine",
    )(slot_target, keep, over_cores(give))
    mine = [partial[0]] + [
        lax.ppermute(partial[d], "sector", [(i, (i + d) % rows) for i in range(rows)]) for d in range(1, rows)
    ]
    theirs = [over_cores(block) for block in mine]
    return pl.pallas_call(
        functools.partial(assemble_kernel, rows),
        out_shape=jax.ShapeDtypeStruct((sectors, width, width), jnp.float32),
        in_specs=[vmem] * (2 * rows),
        out_specs=vmem,
        compiler_params=params,
        name="assemble",
    )(*mine, *theirs)


def solution(mesh):
    in_specs = (
        P(("groups", "sector", "blk"), None, None),
        P(("groups", "op"), "blk", None, None),
        P(("groups", "op"), None, None, None),
        P(("groups", "sector", "blk")),
        P(("groups", "sector", "blk")),
        P(("groups", "op"), ("sector", "blk")),
        P(("groups", "sector"), "blk", None),
    )
    out_specs = P(("groups", "sector", "blk"), None, None)
    sizes = tuple(mesh.shape[name] for name in ("sector", "blk", "op"))
    return jax.shard_map(
        functools.partial(shards, sizes), mesh=mesh, in_specs=in_specs, out_specs=out_specs, check_vma=False
    )
```

time: 51.9 us -> 43.5 us (0.84); the launches traced: 51.7 us -> 42.7 us
  waiting for transfers between devices: 15.2 us -> 8.95 us
  Pallas kernels: 26.2 us -> 21.1 us
  starting transfers between devices: 9.14 us -> 10.5 us
  local copies, waits for them, and re-layouts: 1.08 us -> 2.06 us
    ppermute x3, waiting for transfers between devices: 10.1 us -> 4.43 us  [shards(): lax.ppermute(partial[d], 'sector', [(i, (i + d) % rows) for i in range(ro...]
    pallas_call x3, Pallas kernels: 15.7 us -> 10.7 us  [the longest x1 6.44 us: shards(): pl.pallas_call(functools.partial(other_kernel, rows, sets), out_shape=[ja...]
    slice x0 -> x1, local copies, waits for them, and re-layouts: none -> 1.08 us  [shards(): middle = over_blocks(left_ops[quarter:operators - quarter])]
    ppermute x3, starting transfers between devices: 4 us -> 4.71 us  [shards(): lax.ppermute(partial[d], 'sector', [(i, (i + d) % rows) for i in range(ro...]
    ppermute x8, starting transfers between devices: 5.15 us -> 5.76 us  [the longest x2 3.09 us: over_blocks(): lax.ppermute(part, 'blk', [((b + d) % blocks, b) for b in range(blocks)])]
    ppermute x8, waiting for transfers between devices: 5.13 us -> 4.52 us  [the longest x5 2.43 us: over_cores(): lax.ppermute(block, 'op', [(h, halves - 1 - h) for h in range(halves)])]
  transfers between devices with their start and end apart: 11 -> 11, of which waited for: 6 -> 7; matrix products, arithmetic and copies ran while one was open for 0% -> 3% of each run, Pallas kernels for 37% -> 29%
where the time goes in v4:
time: 43.5 us; the launch traced here: 42.7 us
  Pallas kernels  21.1 us (49%)
  starting transfers between devices  10.5 us (24%)
  waiting for transfers between devices  8.95 us (21%)
  local copies, waits for them, and re-layouts  2.06 us (5%)
    pallas_call x1, Pallas kernels, shards(): pl.pallas_call(functools.partial(right_kernel, blocks, left_local), out_s...  8.92 us
    pallas_call x1, Pallas kernels, shards(): pl.pallas_call(functools.partial(other_kernel, rows, sets), out_shape=[ja...  6.44 us
    ppermute x3, starting transfers between devices, shards(): lax.ppermute(partial[d], 'sector', [(i, (i + d) % rows) for i in range(ro...  4.71 us
    ppermute x3, waiting for transfers between devices, shards(): lax.ppermute(partial[d], 'sector', [(i, (i + d) % rows) for i in range(ro...  4.43 us
    pallas_call x1, Pallas kernels, shards(): pl.pallas_call(own_kernel, out_shape=[jax.ShapeDtypeStruct(total_shape, j...  3.64 us
    ppermute x2, starting transfers between devices, over_blocks(): lax.ppermute(part, 'blk', [((b + d) % blocks, b) for b in range(blocks)])  3.09 us
    ppermute x5, waiting for transfers between devices, over_cores(): lax.ppermute(block, 'op', [(h, halves - 1 - h) for h in range(halves)])  2.43 us
    ppermute x1, starting transfers between devices, shards(): swapped = [lax.ppermute(part, 'sector', swap) for part in direct]  2.09 us
  transfers between devices with their start and end apart: 11, of which 7 were waited for; matrix products, arithmetic and copies ran while one was open for 3% of the time, Pallas kernels for 29%

profile of v4, /device:TPU:0, one launch (start us, length us, event | category | flops | bytes accessed | tf_op | source)
XLA Modules:
  0.0 42.7 jit_solution(16066471239672667383)
XLA Ops:
  0.0 1.0 %constant_dynamic-slice_fusion = bf16[8,1,128,128]{3,2,0,1:T(8,128)(2,1)S(1)} fusion(bf16[32,1,128,128]{3,2,0,1:T(8,128)(2,1)} %bitcast.7, s32[]{:T(128)S(6)} %select_n.3), kind=kLoop, calls=%fused_computation | loop fusion | bytes 524292 | tf_op jit(solution)/shard_map/dynamic_slice | solution.py:204
  1.0 3.0 %collective-permute-start = (bf16[8,1,128,128]{3,2,0,1:T(8,128)(2,1)S(1)}, bf16[8,1,128,128]{3,2,0,1:T(8,128)(2,1)S(1)}, u32[]{:S(2)}, u32[]{:S(2)}) collective-permute-start(bf16[8,1,128,128]{3,2,0,1:T(8,128)(2,1)S(1)} %constant_dynamic-slice_fusion), channel_id=1, source_target_pairs={{2,0},{0,2},{3,1},{1,3},{6,4},{4,6},{7,5},{5,7},{10,8},{8,10},{11,... | collective-permute-start | bytes 786440 | tf_op jit(solution)/shard_map/ppermute | solution.py:202
  4.0 1.1 %slice.4 = bf16[16,1,128,128]{3,2,0,1:T(8,128)(2,1)S(1)} slice(bf16[32,1,128,128]{3,2,0,1:T(8,128)(2,1)} %bitcast.8), slice={[8:24], [0:1], [0:128], [0:128]} | slice | bytes 1048576 | tf_op jit(solution)/shard_map/slice | solution.py:205
  5.1 0.0 copy-start
  5.1 0.0 copy-start.1
  5.1 0.1 collective-permute-start.2
  5.2 8.9 %right_side.1 = (bf16[6,32,2,128,256]{4,3,2,1,0:T(8,128)(2,1)S(1)}, s32[28]{0:T(128)S(1)}) custom-call(s32[24]{0:T(128)} %left_qn_in.1, s32[24]{0:T(128)} %right_qn_in.1, bf16[24,128,128]{2,1,0:T(8,128)(2,1)} %psi_in.1, bf16[32,2,128,128]{3,2,1,0:T(8,128)(2,1)} %right_in.1), custom_call_target="tpu_custom_call" | custom-call | flops 12884901888 | bytes 4194304 | tf_op jit(solution)/shard_map/right_side/pallas_call | solution.py:207
  14.1 0.0 collective-permute-done
  14.1 2.1 %collective-permute-start.1 = (bf16[8,1,128,128]{3,2,0,1:T(8,128)(2,1)S(1)}, bf16[8,1,128,128]{3,2,0,1:T(8,128)(2,1)S(1)}, u32[]{:S(2)}, u32[]{:S(2)}) collective-permute-start(bf16[8,1,128,128]{3,2,0,1:T(8,128)(2,1)S(1)} %collective-permute-done), channel_id=1, source_target_pairs={{0,4},{4,0},{8,12},{12,8},{1,5},{5,1},{9,13},{13,9},{2,6},{6,2},{1... | collective-permute-start | bytes 786440 | tf_op jit(solution)/shard_map/ppermute | solution.py:228
  16.2 0.0 copy-done
  16.2 3.6 %own_left.1 = (f32[17,128,128]{2,1,0:T(8,128)S(1)}, f32[17,128,128]{2,1,0:T(8,128)S(1)}, f32[17,128,128]{2,1,0:T(8,128)S(1)}, f32[17,128,128]{2,1,0:T(8,128)S(1)}) custom-call(s32[28]{0:T(128)S(1)} %get-tuple-element.19.plan, s32[24,32]{1,0:T(8,128)S(1)} %bitcast.12, bf16[6,32,2,128,256]{4,3,2,1,0:T(8,128)(2,1)S(1)} %get-tuple-element.21.half, ...), custom_call_target="tpu_custom_call" | custom-call | flops 6442450944 | bytes 4194304 | tf_op jit(solution)/shard_map/own_left/pallas_call | solution.py:229
  19.8 1.7 %collective-permute-done.2 = bf16[16,1,128,128]{3,2,0,1:T(8,128)(2,1)S(1)} collective-permute-done((bf16[16,1,128,128]{3,2,0,1:T(8,128)(2,1)S(1)}, bf16[16,1,128,128]{3,2,0,1:T(8,128)(2,1)S(1)}, u32[]{:S(2)}, u32[]{:S(2)}) %collective-permute-start.2) | collective-permute-done | bytes 524320 | tf_op jit(solution)/shard_map/ppermute | solution.py:202
  21.5 0.4 collective-permute-done.1
  21.9 6.4 %other_left.1 = (f32[17,128,128]{2,1,0:T(8,128)S(1)}, f32[17,128,128]{2,1,0:T(8,128)S(1)}, f32[17,128,128]{2,1,0:T(8,128)S(1)}, f32[17,128,128]{2,1,0:T(8,128)S(...) custom-call(s32[28]{0:T(128)S(1)} %get-tuple-element.19.plan, ...), custom_call_target="tpu_custom_call", output_to_operand_aliasing={{0}: (6, {}), {1}: (7, {}), {2}: (8, {}), {3}: (9, {})} | custom-call | flops 6442450944 | bytes 4194304 | tf_op jit(solution)/shard_map/other_left/pallas_call | solution.py:238
  28.4 0.1 collective-permute-start.3
  28.5 1.5 %collective-permute-done.3.taken = bf16[8,128,128]{2,1,0:T(8,128)(2,1)S(1)} collective-permute-done((bf16[8,128,128]{2,1,0:T(8,128)(2,1)S(1)}, bf16[8,128,128]{2,1,0:T(8,128)(2,1)S(1)}, u32[]{:S(2)}, u32[]{:S(2)}) %collective-permute-start.3) | collective-permute-done | bytes 262176 | tf_op jit(solution)/shard_map/ppermute | solution.py:252
  30.0 0.6 %combine.1 = (bf16[272,128]{1,0:T(8,128)(2,1)S(1)}, bf16[272,128]{1,0:T(8,128)(2,1)S(1)}, bf16[272,128]{1,0:T(8,128)(2,1)S(1)}, bf16[272,128]{1,0:T(8,128)(2,1)S(1)}) custom-call(s32[1,1,16]{2,1,0:T(1,128)S(1)} %copy-done.2, f32[8,128,128]{2,1,0:T(8,128)S(1)} %get-tuple-element.27.keep, bf16[8,128,128]{2,1,0:T(8,128)(2,1)S(1)} %collective-permute-done.3.taken), custom_call_target="tpu_custom_call" | custom-call | tf_op jit(solution)/shard_map/combine/pallas_call | solution.py:254
  30.6 1.8 %collective-permute-start.4 = (bf16[272,128]{1,0:T(8,128)(2,1)S(1)}, bf16[272,128]{1,0:T(8,128)(2,1)S(1)}, u32[]{:S(2)}, u32[]{:S(2)}) collective-permute-start(bf16[272,128]{1,0:T(8,128)(2,1)S(1)} %get-tuple-element.30), channel_id=1, source_target_pairs={{0,4},{4,8},{8,12},{12,0},{1,5},{5,9},{9,13},{13,1},{2,6},{6,10},{... | collective-permute-start | bytes 208904 | tf_op jit(solution)/shard_map/ppermute | solution.py:263
  32.4 1.2 %collective-permute-start.5 = (bf16[272,128]{1,0:T(8,128)(2,1)S(1)}, bf16[272,128]{1,0:T(8,128)(2,1)S(1)}, u32[]{:S(2)}, u32[]{:S(2)}) collective-permute-start(bf16[272,128]{1,0:T(8,128)(2,1)S(1)} %get-tuple-element.31), channel_id=1, source_target_pairs={{0,8},{4,12},{8,0},{12,4},{1,9},{5,13},{9,1},{13,5},{2,10},{6,14},... | collective-permute-start | bytes 208904 | tf_op jit(solution)/shard_map/ppermute | solution.py:263
  33.6 1.7 %collective-permute-start.6 = (bf16[272,128]{1,0:T(8,128)(2,1)S(1)}, bf16[272,128]{1,0:T(8,128)(2,1)S(1)}, u32[]{:S(2)}, u32[]{:S(2)}) collective-permute-start(bf16[272,128]{1,0:T(8,128)(2,1)S(1)} %get-tuple-element.32), channel_id=1, source_target_pairs={{0,12},{4,0},{8,4},{12,8},{1,13},{5,1},{9,5},{13,9},{2,14},{6,2},{... | collective-permute-start | bytes 208904 | tf_op jit(solution)/shard_map/ppermute | solution.py:263
  35.3 0.0 collective-permute-start.7
  35.3 2.2 %collective-permute-done.4.rest_1_ = bf16[272,128]{1,0:T(8,128)(2,1)S(1)} collective-permute-done((bf16[272,128]{1,0:T(8,128)(2,1)S(1)}, bf16[272,128]{1,0:T(8,128)(2,1)S(1)}, u32[]{:S(2)}, u32[]{:S(2)}) %collective-permute-start.4) | collective-permute-done | bytes 69664 | tf_op jit(solution)/shard_map/ppermute | solution.py:263
  37.5 0.0 collective-permute-start.8
  37.5 2.2 %collective-permute-done.5.rest_2_ = bf16[272,128]{1,0:T(8,128)(2,1)S(1)} collective-permute-done((bf16[272,128]{1,0:T(8,128)(2,1)S(1)}, bf16[272,128]{1,0:T(8,128)(2,1)S(1)}, u32[]{:S(2)}, u32[]{:S(2)}) %collective-permute-start.5) | collective-permute-done | bytes 69664 | tf_op jit(solution)/shard_map/ppermute | solution.py:263
  39.7 0.0 collective-permute-start.9
  39.8 0.0 collective-permute-done.6.rest_3_
  39.8 0.5 %collective-permute-start.10 = (bf16[272,128]{1,0:T(8,128)(2,1)S(1)}, bf16[272,128]{1,0:T(8,128)(2,1)S(1)}, u32[]{:S(2)}, u32[]{:S(2)}) collective-permute-start(bf16[272,128]{1,0:T(8,128)(2,1)S(1)} %collective-permute-done.6.rest_3_), channel_id=1, source_target_pairs={{0,1},{1,0},{2,3},{3,2},{4,5},{5,4},{6,7},{7,6},{8,9},{9,8},{10,11... | collective-permute-start | bytes 208904 | tf_op jit(solution)/shard_map/ppermute | solution.py:252
  40.3 0.0 collective-permute-done.7.rest_4_
  40.3 0.0 collective-permute-done.8.rest_5_
  40.3 0.7 %collective-permute-done.9.rest_6_ = bf16[272,128]{1,0:T(8,128)(2,1)S(1)} collective-permute-done((bf16[272,128]{1,0:T(8,128)(2,1)S(1)}, bf16[272,128]{1,0:T(8,128)(2,1)S(1)}, u32[]{:S(2)}, u32[]{:S(2)}) %collective-permute-start.9) | collective-permute-done | bytes 69664 | tf_op jit(solution)/shard_map/ppermute | solution.py:252
  41.0 0.2 collective-permute-done.10.rest_7_
  41.2 1.5 %assemble.1 = f32[24,128,128]{2,1,0:T(8,128)} custom-call(bf16[272,128]{1,0:T(8,128)(2,1)S(1)} %get-tuple-element.29.rest_0_, bf16[272,128]{1,0:T(8,128)(2,1)S(1)} %collective-permute-done.4.rest_1_, bf16[272,128]{1,0:T(8,128)(2,1)S(1)} %collective-permute-done.5.rest_2_, bf16[272,128]{1,0:T(8,128)(2,1)S(1)} %collective-permute-done.6.rest_3_, ...), custom_call_target="tpu_custom_call" | custom-call | tf_op jit(solution)/shard_map/assemble/pallas_call | solution.py:266
  (3 shorter events, 0.0 us)
Async XLA Ops:
  1.0 13.1 %collective-permute-start = (bf16[8,1,128,128]{3,2,0,1:T(8,128)(2,1)S(1)}, bf16[8,1,128,128]{3,2,0,1:T(8,128)(2,1)S(1)}, u32[]{:S(2)}, u32[]{:S(2)}) collective-permute-start(bf16[8,1,128,128]{3,2,0,1:T(8,128)(2,1)S(1)} %constant_dynamic-slice_fusion), channel_id=1, source_target_pairs={{2,0},{0,2},{3,1},{1,3},{6,4},{4,6},{7,5},{5,7},{10,8},{8,10},{11,... | collective-permute-start | bytes 786440 | tf_op jit(solution)/shard_map/ppermute | solution.py:202
  5.1 11.1 %copy-start = (bf16[32,1,128,128]{3,2,1,0:T(8,128)(2,1)S(1)}, bf16[32,1,128,128]{3,2,1,0:T(8,128)(2,1)}, u32[]{:S(2)}) copy-start(bf16[32,1,128,128]{3,2,1,0:T(8,128)(2,1)} %left.1) | copy-start | bytes 3145732
  5.1 11.1 %copy-start.1 = (s32[32,24]{0,1:T(8,128)S(1)}, s32[32,24]{0,1:T(8,128)}, u32[]{:S(2)}) copy-start(s32[32,24]{0,1:T(8,128)} %param.12) | copy-start | bytes 9220
  5.1 16.4 %collective-permute-start.2 = (bf16[16,1,128,128]{3,2,0,1:T(8,128)(2,1)S(1)}, bf16[16,1,128,128]{3,2,0,1:T(8,128)(2,1)S(1)}, u32[]{:S(2)}, u32[]{:S(2)}) collective-permute-start(bf16[16,1,128,128]{3,2,0,1:T(8,128)(2,1)S(1)} %slice.4), channel_id=1, source_target_pairs={{2,0},{0,2},{3,1},{1,3},{6,4},{4,6},{7,5},{5,7},{10,8},{8,10},{11,... | collective-permute-start | bytes 1572872 | tf_op jit(solution)/shard_map/ppermute | solution.py:202
  14.1 7.8 %collective-permute-start.1 = (bf16[8,1,128,128]{3,2,0,1:T(8,128)(2,1)S(1)}, bf16[8,1,128,128]{3,2,0,1:T(8,128)(2,1)S(1)}, u32[]{:S(2)}, u32[]{:S(2)}) collective-permute-start(bf16[8,1,128,128]{3,2,0,1:T(8,128)(2,1)S(1)} %collective-permute-done), channel_id=1, source_target_pairs={{0,4},{4,0},{8,12},{12,8},{1,5},{5,1},{9,13},{13,9},{2,6},{6,2},{1... | collective-permute-start | bytes 786440 | tf_op jit(solution)/shard_map/ppermute | solution.py:228
  21.9 8.1 %copy-start.2 = (s32[1,1,16]{2,1,0:T(1,128)S(1)}, s32[1,1,16]{2,1,0:T(1,128)}, u32[]{:S(2)}) copy-start(s32[1,1,16]{2,1,0:T(1,128)} %slot_target.1) | copy-start | bytes 196
  28.4 1.6 %collective-permute-start.3 = (bf16[8,128,128]{2,1,0:T(8,128)(2,1)S(1)}, bf16[8,128,128]{2,1,0:T(8,128)(2,1)S(1)}, u32[]{:S(2)}, u32[]{:S(2)}) collective-permute-start(bf16[8,128,128]{2,1,0:T(8,128)(2,1)S(1)} %get-tuple-element.28), channel_id=1, source_target_pairs={{0,1},{1,0},{2,3},{3,2},{4,5},{5,4},{6,7},{7,6},{8,9},{9,8},{10,11... | collective-permute-start | bytes 786440 | tf_op jit(solution)/shard_map/ppermute | solution.py:252
  30.6 6.9 %collective-permute-start.4 = (bf16[272,128]{1,0:T(8,128)(2,1)S(1)}, bf16[272,128]{1,0:T(8,128)(2,1)S(1)}, u32[]{:S(2)}, u32[]{:S(2)}) collective-permute-start(bf16[272,128]{1,0:T(8,128)(2,1)S(1)} %get-tuple-element.30), channel_id=1, source_target_pairs={{0,4},{4,8},{8,12},{12,0},{1,5},{5,9},{9,13},{13,1},{2,6},{6,10},{... | collective-permute-start | bytes 208904 | tf_op jit(solution)/shard_map/ppermute | solution.py:263
  32.4 7.4 %collective-permute-start.5 = (bf16[272,128]{1,0:T(8,128)(2,1)S(1)}, bf16[272,128]{1,0:T(8,128)(2,1)S(1)}, u32[]{:S(2)}, u32[]{:S(2)}) collective-permute-start(bf16[272,128]{1,0:T(8,128)(2,1)S(1)} %get-tuple-element.31), channel_id=1, source_target_pairs={{0,8},{4,12},{8,0},{12,4},{1,9},{5,13},{9,1},{13,5},{2,10},{6,14},... | collective-permute-start | bytes 208904 | tf_op jit(solution)/shard_map/ppermute | solution.py:263
  33.6 6.1 %collective-permute-start.6 = (bf16[272,128]{1,0:T(8,128)(2,1)S(1)}, bf16[272,128]{1,0:T(8,128)(2,1)S(1)}, u32[]{:S(2)}, u32[]{:S(2)}) collective-permute-start(bf16[272,128]{1,0:T(8,128)(2,1)S(1)} %get-tuple-element.32), channel_id=1, source_target_pairs={{0,12},{4,0},{8,4},{12,8},{1,13},{5,1},{9,5},{13,9},{2,14},{6,2},{... | collective-permute-start | bytes 208904 | tf_op jit(solution)/shard_map/ppermute | solution.py:263
  35.3 5.0 %collective-permute-start.7 = (bf16[272,128]{1,0:T(8,128)(2,1)S(1)}, bf16[272,128]{1,0:T(8,128)(2,1)S(1)}, u32[]{:S(2)}, u32[]{:S(2)}) collective-permute-start(bf16[272,128]{1,0:T(8,128)(2,1)S(1)} %get-tuple-element.29.rest_0_), channel_id=1, source_target_pairs={{0,1},{1,0},{2,3},{3,2},{4,5},{5,4},{6,7},{7,6},{8,9},{9,8},{10,11... | collective-permute-start | bytes 208904 | tf_op jit(solution)/shard_map/ppermute | solution.py:252
  37.5 2.7 %collective-permute-start.8 = (bf16[272,128]{1,0:T(8,128)(2,1)S(1)}, bf16[272,128]{1,0:T(8,128)(2,1)S(1)}, u32[]{:S(2)}, u32[]{:S(2)}) collective-permute-start(bf16[272,128]{1,0:T(8,128)(2,1)S(1)} %collective-permute-done.4.rest_1_), channel_id=1, source_target_pairs={{0,1},{1,0},{2,3},{3,2},{4,5},{5,4},{6,7},{7,6},{8,9},{9,8},{10,11... | collective-permute-start | bytes 208904 | tf_op jit(solution)/shard_map/ppermute | solution.py:252
  39.7 1.3 %collective-permute-start.9 = (bf16[272,128]{1,0:T(8,128)(2,1)S(1)}, bf16[272,128]{1,0:T(8,128)(2,1)S(1)}, u32[]{:S(2)}, u32[]{:S(2)}) collective-permute-start(bf16[272,128]{1,0:T(8,128)(2,1)S(1)} %collective-permute-done.5.rest_2_), channel_id=1, source_target_pairs={{0,1},{1,0},{2,3},{3,2},{4,5},{5,4},{6,7},{7,6},{8,9},{9,8},{10,11... | collective-permute-start | bytes 208904 | tf_op jit(solution)/shard_map/ppermute | solution.py:252
  39.8 1.4 %collective-permute-start.10 = (bf16[272,128]{1,0:T(8,128)(2,1)S(1)}, bf16[272,128]{1,0:T(8,128)(2,1)S(1)}, u32[]{:S(2)}, u32[]{:S(2)}) collective-permute-start(bf16[272,128]{1,0:T(8,128)(2,1)S(1)} %collective-permute-done.6.rest_3_), channel_id=1, source_target_pairs={{0,1},{1,0},{2,3},{3,2},{4,5},{5,4},{6,7},{7,6},{8,9},{9,8},{10,11... | collective-permute-start | bytes 208904 | tf_op jit(solution)/shard_map/ppermute | solution.py:252

commit v5 on v4

--- a/solution.py
+++ b/solution.py
@@ -9,7 +9,7 @@
 
 CAP = 4
 GROUP = 4
-SETS = 4
+SETS = 2
 MOST_SLOTS = 64
 BLOCK_K = 8
 TAIL = 16
@@ -32,6 +32,19 @@
         return lax.fori_loop(0, count, one_sector, n)
 
     plan[count + 1 + blocks * left_local] = lax.fori_loop(0, blocks * left_local, one_code, jnp.int32(0))
+
+
+def cut_kernel(left, direct, middle, sems):
+    quarter, count = direct.shape[0], middle.shape[0]
+    first = lax.rem(lax.axis_index("sector"), jnp.int32(2)) * (left.shape[0] - quarter)
+    copies = [
+        pltpu.make_async_copy(left.at[pl.ds(first, quarter)], direct, sems.at[0]),
+        pltpu.make_async_copy(left.at[pl.ds(quarter, count)], middle, sems.at[1]),
+    ]
+    for copy in copies:
+        copy.start()
+    for copy in copies:
+        copy.wait()
 
 
 def right_kernel(
@@ -153,7 +166,7 @@
     row, side = lax.axis_index("sector"), lax.axis_index("op")
     line = lax.broadcasted_iota(jnp.int32, (TAIL, width), 0)
     for d, out in enumerate(outs):
-        owner = lax.rem(row + d, jnp.int32(len(outs)))
+        owner = lax.bitwise_xor(row, jnp.int32(d))
         ids = jnp.zeros((TAIL, width), jnp.int32)
         for m in range(part):
             block = keep[owner * part + m] + taken[owner * part + m].astype(jnp.float32)
@@ -194,15 +207,26 @@
         flops = int(16 * operators * sectors * width**3 * share)
         return pl.CostEstimate(flops=flops, bytes_accessed=4 * 2**20, transcendentals=0)
 
-    odd = lax.rem(lax.axis_index("sector"), 2)
+    assert rows & (rows - 1) == 0
     quarter = operators // 4
     swap = [(i, i ^ 1) for i in range(rows)]
 
     def over_blocks(part):
         return [lax.ppermute(part, "blk", [((b + d) % blocks, b) for b in range(blocks)]) for d in range(1, blocks)]
 
-    direct = over_blocks(lax.dynamic_slice_in_dim(left_ops, odd * (operators - quarter), quarter, 0))
-    middle = over_blocks(left_ops[quarter : operators - quarter])
+    direct, middle = pl.pallas_call(
+        cut_kernel,
+        out_shape=[
+            jax.ShapeDtypeStruct((count, *left_ops.shape[1:]), left_ops.dtype)
+            for count in (quarter, operators - 2 * quarter)
+        ],
+        in_specs=[hbm],
+        out_specs=[vmem] * 2,
+        scratch_shapes=[pltpu.SemaphoreType.DMA((2,))],
+        compiler_params=params,
+        name="cut_left",
+    )(pltpu.with_memory_space_constraint(left_ops, pltpu.HBM))
+    direct, middle = over_blocks(direct), over_blocks(middle)
 
     half, plan = pl.pallas_call(
         functools.partial(right_kernel, blocks, left_local),
@@ -259,9 +283,10 @@
         compiler_params=params,
         name="combine",
     )(slot_target, keep, over_cores(give))
-    mine = [partial[0]] + [
-        lax.ppermute(partial[d], "sector", [(i, (i + d) % rows) for i in range(rows)]) for d in range(1, rows)
-    ]
+    crossed = {
+        d: lax.ppermute(partial[d], "sector", [(i, i ^ d) for i in range(rows)]) for d in reversed(range(1, rows))
+    }
+    mine = [partial[0]] + [crossed[d] for d in range(1, rows)]
     theirs = [over_cores(block) for block in mine]
     return pl.pallas_call(
         functools.partial(assemble_kernel, rows),

time: 43.5 us -> 43.9 us (level)
  Pallas kernels: 21.1 us -> 23.8 us
  local copies, waits for them, and re-layouts: 2.06 us -> 0.01 us
  waiting for transfers between devices: 8.95 us -> 7.46 us
  starting transfers between devices: 10.5 us -> 11.8 us
    pallas_call x1, Pallas kernels: 3.64 us -> 6.54 us  [shards(): pl.pallas_call(own_kernel, out_shape=[jax.ShapeDtypeStruct(total_shape, j...]
    ppermute x2, waiting for transfers between devices: 1.67 us -> 0.01 us  [over_blocks(): lax.ppermute(part, 'blk', [((b + d) % blocks, b) for b in range(blocks)])]
    pallas_call x1, Pallas kernels: 6.44 us -> 5.04 us  [shards(): pl.pallas_call(functools.partial(other_kernel, rows, sets), out_shape=[ja...]
    pallas_call x0 -> x1, Pallas kernels: none -> 1.14 us  [shards(): pl.pallas_call(cut_kernel, out_shape=[jax.ShapeDtypeStruct((count, *left_...]
    slice x1 -> x0, local copies, waits for them, and re-layouts: 1.08 us -> none  [shards(): middle = over_blocks(left_ops[quarter:operators - quarter])]
    dynamic_slice x1 -> x0, local copies, waits for them, and re-layouts: 0.97 us -> none  [shards(): lax.dynamic_slice_in_dim(left_ops, odd * (operators - quarter), quarter, 0)]
    ppermute x3, starting transfers between devices: 4.71 us -> 5.62 us  [shards(): lax.ppermute(partial[d], 'sector', [(i, i ^ d) for i in range(rows)])]
    ppermute x3, waiting for transfers between devices: 4.43 us -> 5.03 us  [shards(): lax.ppermute(partial[d], 'sector', [(i, i ^ d) for i in range(rows)])]
  transfers between devices with their start and end apart: 11 -> 11, of which waited for: 7 -> 4; matrix products, arithmetic and copies ran while one was open for 3% -> 0% of each run, Pallas kernels for 29% -> 36%
where the time goes in v5:
time: 43.9 us; the launch traced here: 43.1 us
  Pallas kernels  23.8 us (54%)
  starting transfers between devices  11.8 us (27%)
  waiting for transfers between devices  7.46 us (17%)
    pallas_call x1, Pallas kernels, shards(): pl.pallas_call(functools.partial(right_kernel, blocks, left_local), out_s...  8.92 us
    pallas_call x1, Pallas kernels, shards(): pl.pallas_call(own_kernel, out_shape=[jax.ShapeDtypeStruct(total_shape, j...  6.54 us
    ppermute x3, starting transfers between devices, shards(): lax.ppermute(partial[d], 'sector', [(i, i ^ d) for i in range(rows)])  5.62 us
    pallas_call x1, Pallas kernels, shards(): pl.pallas_call(functools.partial(other_kernel, rows, sets), out_shape=[ja...  5.04 us
    ppermute x3, waiting for transfers between devices, shards(): lax.ppermute(partial[d], 'sector', [(i, i ^ d) for i in range(rows)])  5.03 us
    ppermute x2, starting transfers between devices, over_blocks(): lax.ppermute(part, 'blk', [((b + d) % blocks, b) for b in range(blocks)])  3.1 us
    ppermute x5, waiting for transfers between devices, over_cores(): lax.ppermute(block, 'op', [(h, halves - 1 - h) for h in range(halves)])  2.43 us
    ppermute x1, starting transfers between devices, shards(): swapped = [lax.ppermute(part, 'sector', swap) for part in direct]  2 us
  transfers between devices with their start and end apart: 11, of which 4 were waited for; matrix products, arithmetic and copies ran while one was open for 0% of the time, Pallas kernels for 36%

profile of v5, /device:TPU:0, one launch (start us, length us, event | category | flops | bytes accessed | tf_op | source)
XLA Modules:
  0.0 43.1 jit_solution(17498723456514364641)
XLA Ops:
  0.0 1.1 %cut_left.1 = (bf16[8,1,128,128]{3,2,1,0:T(8,128)(2,1)S(1)}, bf16[16,1,128,128]{3,2,1,0:T(8,128)(2,1)S(1)}) custom-call(bf16[32,1,128,128]{3,2,1,0:T(8,128)(2,1)} %left.3), custom_call_target="tpu_custom_call" | custom-call | tf_op jit(solution)/shard_map/cut_left/pallas_call | solution.py:217
  1.1 3.0 %collective-permute-start = (bf16[8,1,128,128]{3,2,0,1:T(8,128)(2,1)S(1)}, bf16[8,1,128,128]{3,2,0,1:T(8,128)(2,1)S(1)}, u32[]{:S(2)}, u32[]{:S(2)}) collective-permute-start(bf16[8,1,128,128]{3,2,0,1:T(8,128)(2,1)S(1)} %bitcast.14), channel_id=1, source_target_pairs={{2,0},{0,2},{3,1},{1,3},{6,4},{4,6},{7,5},{5,7},{10,8},{8,10},{11,... | collective-permute-start | bytes 786440 | tf_op jit(solution)/shard_map/ppermute | solution.py:215
  4.2 0.1 collective-permute-start.2
  4.3 8.9 %right_side.1 = (bf16[6,32,2,128,256]{4,3,2,1,0:T(8,128)(2,1)S(1)}, s32[28]{0:T(128)S(1)}) custom-call(s32[24]{0:T(128)} %left_qn_in.1, s32[24]{0:T(128)} %right_qn_in.1, bf16[24,128,128]{2,1,0:T(8,128)(2,1)} %psi_in.1, bf16[32,2,128,128]{3,2,1,0:T(8,128)(2,1)} %right_in.1), custom_call_target="tpu_custom_call" | custom-call | flops 12884901888 | bytes 4194304 | tf_op jit(solution)/shard_map/right_side/pallas_call | solution.py:231
  13.2 0.0 collective-permute-done
  13.2 2.0 %collective-permute-start.1 = (bf16[8,1,128,128]{3,2,0,1:T(8,128)(2,1)S(1)}, bf16[8,1,128,128]{3,2,0,1:T(8,128)(2,1)S(1)}, u32[]{:S(2)}, u32[]{:S(2)}) collective-permute-start(bf16[8,1,128,128]{3,2,0,1:T(8,128)(2,1)S(1)} %collective-permute-done), channel_id=1, source_target_pairs={{0,4},{4,0},{8,12},{12,8},{1,5},{5,1},{9,13},{13,9},{2,6},{6,2},{1... | collective-permute-start | bytes 786440 | tf_op jit(solution)/shard_map/ppermute | solution.py:252
  15.2 0.0 copy-done
  15.2 0.0 copy-done.1
  15.2 6.5 %own_left.1 = (f32[17,128,128]{2,1,0:T(8,128)S(1)}, f32[17,128,128]{2,1,0:T(8,128)S(1)}) custom-call(s32[28]{0:T(128)S(1)} %get-tuple-element.19.plan, s32[24,32]{1,0:T(8,128)S(1)} %bitcast.11, bf16[6,32,2,128,256]{4,3,2,1,0:T(8,128)(2,1)S(1)} %get-tuple-element.22.half, bf16[32,1,128,128]{3,2,1,0:T(8,128)(2,1)S(1)} %copy-done), custom_call_target="tpu_custom_call" | custom-call | flops 6442450944 | bytes 4194304 | tf_op jit(solution)/shard_map/own_left/pallas_call | solution.py:253
  21.8 0.0 collective-permute-done.2
  21.8 0.0 collective-permute-done.1
  21.8 0.0 copy-start.2
  21.8 5.0 %other_left.1 = (f32[17,128,128]{2,1,0:T(8,128)S(1)}, f32[17,128,128]{2,1,0:T(8,128)S(1)}, f32[8,128,128]{2,1,0:T(8,128)S(1)}, bf16[8,128,128]{2,1,0:T(8,128)(2,1)S(1)}) custom-call(s32[28]{0:T(128)S(1)} %get-tuple-element.19.plan, s32[24,32]{1,0:T(8,128)S(1)} %bitcast.12, ...), custom_call_target="tpu_custom_call", output_to_operand_aliasing={{0}: (6, {}), {1}: (7, {})} | custom-call | flops 6442450944 | bytes 4194304 | tf_op jit(solution)/shard_map/other_left/pallas_call | solution.py:262
  26.8 0.1 collective-permute-start.3
  26.9 1.5 %collective-permute-done.3.taken = bf16[8,128,128]{2,1,0:T(8,128)(2,1)S(1)} collective-permute-done((bf16[8,128,128]{2,1,0:T(8,128)(2,1)S(1)}, bf16[8,128,128]{2,1,0:T(8,128)(2,1)S(1)}, u32[]{:S(2)}, u32[]{:S(2)}) %collective-permute-start.3) | collective-permute-done | bytes 262176 | tf_op jit(solution)/shard_map/ppermute | solution.py:276
  28.4 0.0 copy-done.2
  28.4 0.6 %combine.1 = (bf16[272,128]{1,0:T(8,128)(2,1)S(1)}, bf16[272,128]{1,0:T(8,128)(2,1)S(1)}, bf16[272,128]{1,0:T(8,128)(2,1)S(1)}, bf16[272,128]{1,0:T(8,128)(2,1)S(1)}) custom-call(s32[1,1,16]{2,1,0:T(1,128)S(1)} %copy-done.2, f32[8,128,128]{2,1,0:T(8,128)S(1)} %get-tuple-element.27.keep, bf16[8,128,128]{2,1,0:T(8,128)(2,1)S(1)} %collective-permute-done.3.taken), custom_call_target="tpu_custom_call" | custom-call | tf_op jit(solution)/shard_map/combine/pallas_call | solution.py:278
  29.0 3.2 %collective-permute-start.4 = (bf16[272,128]{1,0:T(8,128)(2,1)S(1)}, bf16[272,128]{1,0:T(8,128)(2,1)S(1)}, u32[]{:S(2)}, u32[]{:S(2)}) collective-permute-start(bf16[272,128]{1,0:T(8,128)(2,1)S(1)} %get-tuple-element.30), channel_id=1, source_target_pairs={{0,4},{4,0},{8,12},{12,8},{1,5},{5,1},{9,13},{13,9},{2,6},{6,2},{1... | collective-permute-start | bytes 208904 | tf_op jit(solution)/shard_map/ppermute | solution.py:287
  32.2 1.2 %collective-permute-start.5 = (bf16[272,128]{1,0:T(8,128)(2,1)S(1)}, bf16[272,128]{1,0:T(8,128)(2,1)S(1)}, u32[]{:S(2)}, u32[]{:S(2)}) collective-permute-start(bf16[272,128]{1,0:T(8,128)(2,1)S(1)} %get-tuple-element.31), channel_id=1, source_target_pairs={{0,8},{4,12},{8,0},{12,4},{1,9},{5,13},{9,1},{13,5},{2,10},{6,14},... | collective-permute-start | bytes 208904 | tf_op jit(solution)/shard_map/ppermute | solution.py:287
  33.4 1.2 %collective-permute-start.6 = (bf16[272,128]{1,0:T(8,128)(2,1)S(1)}, bf16[272,128]{1,0:T(8,128)(2,1)S(1)}, u32[]{:S(2)}, u32[]{:S(2)}) collective-permute-start(bf16[272,128]{1,0:T(8,128)(2,1)S(1)} %get-tuple-element.32), channel_id=1, source_target_pairs={{0,12},{4,8},{8,4},{12,0},{1,13},{5,9},{9,5},{13,1},{2,14},{6,10},... | collective-permute-start | bytes 208904 | tf_op jit(solution)/shard_map/ppermute | solution.py:287
  34.7 0.0 collective-permute-start.7
  34.7 0.0 collective-permute-done.4.rest_1_
  34.7 0.5 %collective-permute-start.8 = (bf16[272,128]{1,0:T(8,128)(2,1)S(1)}, bf16[272,128]{1,0:T(8,128)(2,1)S(1)}, u32[]{:S(2)}, u32[]{:S(2)}) collective-permute-start(bf16[272,128]{1,0:T(8,128)(2,1)S(1)} %collective-permute-done.4.rest_1_), channel_id=1, source_target_pairs={{0,1},{1,0},{2,3},{3,2},{4,5},{5,4},{6,7},{7,6},{8,9},{9,8},{10,11... | collective-permute-start | bytes 208904 | tf_op jit(solution)/shard_map/ppermute | solution.py:276
  35.2 5.0 %collective-permute-done.5.rest_2_ = bf16[272,128]{1,0:T(8,128)(2,1)S(1)} collective-permute-done((bf16[272,128]{1,0:T(8,128)(2,1)S(1)}, bf16[272,128]{1,0:T(8,128)(2,1)S(1)}, u32[]{:S(2)}, u32[]{:S(2)}) %collective-permute-start.5) | collective-permute-done | bytes 69664 | tf_op jit(solution)/shard_map/ppermute | solution.py:287
  40.2 0.0 collective-permute-start.9
  40.2 0.0 collective-permute-done.6.rest_3_
  40.2 0.5 %collective-permute-start.10 = (bf16[272,128]{1,0:T(8,128)(2,1)S(1)}, bf16[272,128]{1,0:T(8,128)(2,1)S(1)}, u32[]{:S(2)}, u32[]{:S(2)}) collective-permute-start(bf16[272,128]{1,0:T(8,128)(2,1)S(1)} %collective-permute-done.6.rest_3_), channel_id=1, source_target_pairs={{0,1},{1,0},{2,3},{3,2},{4,5},{5,4},{6,7},{7,6},{8,9},{9,8},{10,11... | collective-permute-start | bytes 208904 | tf_op jit(solution)/shard_map/ppermute | solution.py:276
  40.7 0.0 collective-permute-done.7.rest_4_
  40.7 0.0 collective-permute-done.8.rest_5_
  40.7 0.7 %collective-permute-done.9.rest_6_ = bf16[272,128]{1,0:T(8,128)(2,1)S(1)} collective-permute-done((bf16[272,128]{1,0:T(8,128)(2,1)S(1)}, bf16[272,128]{1,0:T(8,128)(2,1)S(1)}, u32[]{:S(2)}, u32[]{:S(2)}) %collective-permute-start.9) | collective-permute-done | bytes 69664 | tf_op jit(solution)/shard_map/ppermute | solution.py:276
  41.4 0.2 collective-permute-done.10.rest_7_
  41.6 1.5 %assemble.1 = f32[24,128,128]{2,1,0:T(8,128)} custom-call(bf16[272,128]{1,0:T(8,128)(2,1)S(1)} %get-tuple-element.29.rest_0_, bf16[272,128]{1,0:T(8,128)(2,1)S(1)} %collective-permute-done.4.rest_1_, bf16[272,128]{1,0:T(8,128)(2,1)S(1)} %collective-permute-done.5.rest_2_, bf16[272,128]{1,0:T(8,128)(2,1)S(1)} %collective-permute-done.6.rest_3_, ...), custom_call_target="tpu_custom_call" | custom-call | tf_op jit(solution)/shard_map/assemble/pallas_call | solution.py:291
  (2 shorter events, 0.0 us)
Async XLA Ops:
  1.1 12.0 %collective-permute-start = (bf16[8,1,128,128]{3,2,0,1:T(8,128)(2,1)S(1)}, bf16[8,1,128,128]{3,2,0,1:T(8,128)(2,1)S(1)}, u32[]{:S(2)}, u32[]{:S(2)}) collective-permute-start(bf16[8,1,128,128]{3,2,0,1:T(8,128)(2,1)S(1)} %bitcast.14), channel_id=1, source_target_pairs={{2,0},{0,2},{3,1},{1,3},{6,4},{4,6},{7,5},{5,7},{10,8},{8,10},{11,... | collective-permute-start | bytes 786440 | tf_op jit(solution)/shard_map/ppermute | solution.py:215
  4.2 11.0 %copy-start = (bf16[32,1,128,128]{3,2,1,0:T(8,128)(2,1)S(1)}, bf16[32,1,128,128]{3,2,1,0:T(8,128)(2,1)}, u32[]{:S(2)}) copy-start(bf16[32,1,128,128]{3,2,1,0:T(8,128)(2,1)} %left.3) | copy-start | bytes 3145732
  4.2 11.0 %copy-start.1 = (s32[32,24]{0,1:T(8,128)S(1)}, s32[32,24]{0,1:T(8,128)}, u32[]{:S(2)}) copy-start(s32[32,24]{0,1:T(8,128)} %param.12) | copy-start | bytes 9220
  4.2 17.6 %collective-permute-start.2 = (bf16[16,1,128,128]{3,2,0,1:T(8,128)(2,1)S(1)}, bf16[16,1,128,128]{3,2,0,1:T(8,128)(2,1)S(1)}, u32[]{:S(2)}, u32[]{:S(2)}) collective-permute-start(bf16[16,1,128,128]{3,2,0,1:T(8,128)(2,1)S(1)} %bitcast.13), channel_id=1, source_target_pairs={{2,0},{0,2},{3,1},{1,3},{6,4},{4,6},{7,5},{5,7},{10,8},{8,10},{11,... | collective-permute-start | bytes 1572872 | tf_op jit(solution)/shard_map/ppermute | solution.py:215
  13.2 8.6 %collective-permute-start.1 = (bf16[8,1,128,128]{3,2,0,1:T(8,128)(2,1)S(1)}, bf16[8,1,128,128]{3,2,0,1:T(8,128)(2,1)S(1)}, u32[]{:S(2)}, u32[]{:S(2)}) collective-permute-start(bf16[8,1,128,128]{3,2,0,1:T(8,128)(2,1)S(1)} %collective-permute-done), channel_id=1, source_target_pairs={{0,4},{4,0},{8,12},{12,8},{1,5},{5,1},{9,13},{13,9},{2,6},{6,2},{1... | collective-permute-start | bytes 786440 | tf_op jit(solution)/shard_map/ppermute | solution.py:252
  21.8 6.7 %copy-start.2 = (s32[1,1,16]{2,1,0:T(1,128)S(1)}, s32[1,1,16]{2,1,0:T(1,128)}, u32[]{:S(2)}) copy-start(s32[1,1,16]{2,1,0:T(1,128)} %slot_target.1) | copy-start | bytes 196
  26.8 1.6 %collective-permute-start.3 = (bf16[8,128,128]{2,1,0:T(8,128)(2,1)S(1)}, bf16[8,128,128]{2,1,0:T(8,128)(2,1)S(1)}, u32[]{:S(2)}, u32[]{:S(2)}) collective-permute-start(bf16[8,128,128]{2,1,0:T(8,128)(2,1)S(1)} %get-tuple-element.28), channel_id=1, source_target_pairs={{0,1},{1,0},{2,3},{3,2},{4,5},{5,4},{6,7},{7,6},{8,9},{9,8},{10,11... | collective-permute-start | bytes 786440 | tf_op jit(solution)/shard_map/ppermute | solution.py:276
  29.0 5.7 %collective-permute-start.4 = (bf16[272,128]{1,0:T(8,128)(2,1)S(1)}, bf16[272,128]{1,0:T(8,128)(2,1)S(1)}, u32[]{:S(2)}, u32[]{:S(2)}) collective-permute-start(bf16[272,128]{1,0:T(8,128)(2,1)S(1)} %get-tuple-element.30), channel_id=1, source_target_pairs={{0,4},{4,0},{8,12},{12,8},{1,5},{5,1},{9,13},{13,9},{2,6},{6,2},{1... | collective-permute-start | bytes 208904 | tf_op jit(solution)/shard_map/ppermute | solution.py:287
  32.2 7.9 %collective-permute-start.5 = (bf16[272,128]{1,0:T(8,128)(2,1)S(1)}, bf16[272,128]{1,0:T(8,128)(2,1)S(1)}, u32[]{:S(2)}, u32[]{:S(2)}) collective-permute-start(bf16[272,128]{1,0:T(8,128)(2,1)S(1)} %get-tuple-element.31), channel_id=1, source_target_pairs={{0,8},{4,12},{8,0},{12,4},{1,9},{5,13},{9,1},{13,5},{2,10},{6,14},... | collective-permute-start | bytes 208904 | tf_op jit(solution)/shard_map/ppermute | solution.py:287
  33.4 6.7 %collective-permute-start.6 = (bf16[272,128]{1,0:T(8,128)(2,1)S(1)}, bf16[272,128]{1,0:T(8,128)(2,1)S(1)}, u32[]{:S(2)}, u32[]{:S(2)}) collective-permute-start(bf16[272,128]{1,0:T(8,128)(2,1)S(1)} %get-tuple-element.32), channel_id=1, source_target_pairs={{0,12},{4,8},{8,4},{12,0},{1,13},{5,9},{9,5},{13,1},{2,14},{6,10},... | collective-permute-start | bytes 208904 | tf_op jit(solution)/shard_map/ppermute | solution.py:287
  34.7 6.0 %collective-permute-start.7 = (bf16[272,128]{1,0:T(8,128)(2,1)S(1)}, bf16[272,128]{1,0:T(8,128)(2,1)S(1)}, u32[]{:S(2)}, u32[]{:S(2)}) collective-permute-start(bf16[272,128]{1,0:T(8,128)(2,1)S(1)} %get-tuple-element.29.rest_0_), channel_id=1, source_target_pairs={{0,1},{1,0},{2,3},{3,2},{4,5},{5,4},{6,7},{7,6},{8,9},{9,8},{10,11... | collective-permute-start | bytes 208904 | tf_op jit(solution)/shard_map/ppermute | solution.py:276
  34.7 6.0 %collective-permute-start.8 = (bf16[272,128]{1,0:T(8,128)(2,1)S(1)}, bf16[272,128]{1,0:T(8,128)(2,1)S(1)}, u32[]{:S(2)}, u32[]{:S(2)}) collective-permute-start(bf16[272,128]{1,0:T(8,128)(2,1)S(1)} %collective-permute-done.4.rest_1_), channel_id=1, source_target_pairs={{0,1},{1,0},{2,3},{3,2},{4,5},{5,4},{6,7},{7,6},{8,9},{9,8},{10,11... | collective-permute-start | bytes 208904 | tf_op jit(solution)/shard_map/ppermute | solution.py:276
  40.2 1.3 %collective-permute-start.9 = (bf16[272,128]{1,0:T(8,128)(2,1)S(1)}, bf16[272,128]{1,0:T(8,128)(2,1)S(1)}, u32[]{:S(2)}, u32[]{:S(2)}) collective-permute-start(bf16[272,128]{1,0:T(8,128)(2,1)S(1)} %collective-permute-done.5.rest_2_), channel_id=1, source_target_pairs={{0,1},{1,0},{2,3},{3,2},{4,5},{5,4},{6,7},{7,6},{8,9},{9,8},{10,11... | collective-permute-start | bytes 208904 | tf_op jit(solution)/shard_map/ppermute | solution.py:276
  40.2 1.4 %collective-permute-start.10 = (bf16[272,128]{1,0:T(8,128)(2,1)S(1)}, bf16[272,128]{1,0:T(8,128)(2,1)S(1)}, u32[]{:S(2)}, u32[]{:S(2)}) collective-permute-start(bf16[272,128]{1,0:T(8,128)(2,1)S(1)} %collective-permute-done.6.rest_3_), channel_id=1, source_target_pairs={{0,1},{1,0},{2,3},{3,2},{4,5},{5,4},{6,7},{7,6},{8,9},{9,8},{10,11... | collective-permute-start | bytes 208904 | tf_op jit(solution)/shard_map/ppermute | solution.py:276

commit v6 on v4

v6 whole, which is shorter than its diff:
```python
import functools

import jax
import jax.numpy as jnp
from jax import lax
from jax.experimental import pallas as pl
from jax.experimental.pallas import tpu as pltpu
from jax.sharding import PartitionSpec as P

CAP = 4
GROUP = 4
SETS = 4
MOST_SLOTS = 64
BLOCK_K = 8
TAIL = 16
NT = (((1,), (1,)), ((), ()))


def arrange(left_qn, right_qn, plan, blocks, left_local):
    mine = lax.axis_index("blk")
    count = left_qn.shape[0]

    def one_code(code, n):
        plan[2 * count + 2 + code] = n
        owner = lax.rem(mine + lax.div(code, jnp.int32(left_local)), jnp.int32(blocks))
        wanted = owner * left_local + lax.rem(code, jnp.int32(left_local))

        def one_sector(s, n):
            plan[n] = s
            plan[count + 1 + n] = right_qn[s]
            return n + (left_qn[s] == wanted).astype(jnp.int32)

        return lax.fori_loop(0, count, one_sector, n)

    plan[2 * count + 2 + blocks * left_local] = lax.fori_loop(0, blocks * left_local, one_code, jnp.int32(0))


def first_kernel(blocks, left_qn_in, right_qn_in, psi_in, right_in, left, direct, middle, psi, head, plan, *rest):
    totals, (left_qn, right_qn, sems) = rest[:-3], rest[-3:]
    relayed, count = direct.shape[0], middle.shape[0]
    first = lax.rem(lax.axis_index("sector"), jnp.int32(2)) * (left.shape[0] - relayed)
    pairs = [
        (left_qn_in, left_qn),
        (right_qn_in, right_qn),
        (left.at[pl.ds(first, relayed)], direct),
        (left.at[pl.ds(relayed, count)], middle),
        (psi_in, psi),
        (right_in.at[pl.ds(0, head.shape[0])], head),
    ]
    copies = [pltpu.make_async_copy(src, dst, sems.at[i]) for i, (src, dst) in enumerate(pairs)]
    for copy in copies:
        copy.start()
    for total in totals:
        total[...] = jnp.zeros_like(total)
    copies[0].wait()
    copies[1].wait()
    arrange(left_qn, right_qn, plan, blocks, left.shape[1])
    for copy in copies[2:]:
        copy.wait()


def right_kernel(plan, psi, head, right_in, half, right, sources, sems):
    sectors, width = psi.shape[0], psi.shape[1]
    right_count = right.shape[1]
    steps = right_in.shape[0] // BLOCK_K
    zero = jnp.zeros((width, width), jnp.bfloat16)

    def right_copy(i):
        src = right_in.at[pl.ds(i * BLOCK_K, BLOCK_K)]
        dst = right.at[pl.ds((i - 1) * BLOCK_K, BLOCK_K)]
        return pltpu.make_async_copy(src, dst, sems.at[i - 1])

    for i in range(1, steps):
        right_copy(i).start()
    for pair in range(sectors // 2):
        for e in range(2):
            block = psi[plan[2 * pair + e]]
            quantum = plan[sectors + 1 + 2 * pair + e]
            for r in range(right_count):
                sources[pair, e * width : (e + 1) * width, r * width : (r + 1) * width] = jnp.where(
                    quantum == r, block, zero
                )

    def products(blocks, first):
        stream = jnp.concatenate([block.reshape(BLOCK_K * width, width) for block in blocks], axis=1)
        for pair in range(sectors // 2):
            product = lax.dot_general(stream, sources[pair], NT, preferred_element_type=jnp.float32)
            half[pair // 2, pl.ds(first, BLOCK_K), pair % 2] = product.astype(jnp.bfloat16).reshape(
                BLOCK_K, width, 2 * width
            )

    products([head[:, r] for r in range(right_count)], 0)

    def one_step(i, unused):
        right_copy(i).wait()
        at = pl.ds((i - 1) * BLOCK_K, BLOCK_K)
        products([right[at, r] for r in range(right_count)], i * BLOCK_K)
        return unused

    lax.fori_loop(1, steps, one_step, 0)


def accumulate(code, pieces, plan, slots, half, totals):
    sectors, width = slots.shape[0], totals[0].shape[1]
    spare = totals[0].shape[0] - 1
    low, high = plan[2 * sectors + 2 + code], plan[2 * sectors + 3 + code]
    zero = jnp.zeros((width, width), jnp.bfloat16)

    def terms(place, count, rows):
        members = [plan[place + j] for j in range(count)]
        counts = [(low <= place + j) & (place + j < high) for j in range(count)]
        for first, left in pieces:
            for i in range(left.shape[0]):
                k = first + i
                block = left[i]
                weights = jnp.concatenate(
                    [jnp.concatenate([block, zero], axis=1), jnp.concatenate([zero, block], axis=1)], axis=0
                )
                term = lax.dot_general(rows(k), weights, NT, preferred_element_type=jnp.float32)
                for j in range(count):
                    p, e = j // 2, j % 2
                    slot = jnp.where(counts[j], slots[members[j], k], spare)
                    totals[j % len(totals)][slot] += term[
                        p * width : (p + 1) * width, e * width : (e + 1) * width
                    ]

    def one_group(g, unused):
        terms(g * GROUP, GROUP, lambda k: half[g, k].reshape(GROUP // 2 * width, 2 * width))
        return unused

    def one_pair(i, unused):
        pair = jnp.where((odd_start == 1) & (i == 0), start, stop - 1)
        terms(pair * 2, 2, lambda k: half[lax.div(pair, 2), k, lax.rem(pair, 2)])
        return unused

    some = low < high
    start = jnp.where(some, lax.div(low, 2), 0)
    stop = jnp.where(some, lax.div(high + 1, 2), 0)
    odd_start, odd_stop = lax.rem(start, 2), lax.rem(stop, 2)
    lax.fori_loop(lax.div(start + 1, 2), lax.div(stop, 2), one_group, 0)
    lax.fori_loop(0, odd_start + odd_stop, one_pair, 0)


def own_kernel(plan, slots, half, left, *rest):
    totals = rest[len(rest) // 2 :]
    for l in range(left.shape[1]):
        accumulate(l, [(0, left.at[:, l])], plan, slots, half, totals)


def other_kernel(rows, sets, plan, slots, half, swapped, direct, middle, *rest):
    totals, (keep, give) = rest[sets : 2 * sets], rest[2 * sets :]
    shifts, relayed, left_local = swapped.shape[0], swapped.shape[1], swapped.shape[2]
    row, side = lax.axis_index("sector"), lax.axis_index("op")
    operators, width = slots.shape[1], totals[0].shape[1]
    odd = lax.rem(row, jnp.int32(2))
    near = odd * (operators - relayed)
    far = (1 - odd) * (operators - relayed)

    def one_shift(d, unused):
        for l in range(left_local):
            pieces = [
                (near, direct.at[d, :, l]), (relayed, middle.at[d, :, l]), (far, swapped.at[d, :, l])
            ]
            accumulate((d + 1) * left_local + l, pieces, plan, slots, half, totals)
        return unused

    lax.fori_loop(0, shifts, one_shift, 0)
    part = CAP // 2
    for owner in range(rows):
        for m in range(part):
            at = owner * CAP + side * part + m
            keep[owner * part + m] = sum(total[at] for total in totals)
            at = owner * CAP + (1 - side) * part + m
            give[owner * part + m] = sum(total[at] for total in totals).astype(jnp.bfloat16)


def combine_kernel(slot_target, keep, taken, *outs):
    part, width = CAP // 2, keep.shape[1]
    row, side = lax.axis_index("sector"), lax.axis_index("op")
    line = lax.broadcasted_iota(jnp.int32, (TAIL, width), 0)
    for d, out in enumerate(outs):
        owner = lax.rem(row + d, jnp.int32(len(outs)))
        ids = jnp.zeros((TAIL, width), jnp.int32)
        for m in range(part):
            block = keep[owner * part + m] + taken[owner * part + m].astype(jnp.float32)
            out[m * width : (m + 1) * width, :] = block.astype(jnp.bfloat16)
            ids = jnp.where(line == m, slot_target[0, 0, owner * CAP + side * part + m], ids)
        out[part * width :, :] = ids.astype(jnp.float32).astype(jnp.bfloat16)


def assemble_kernel(rows, *rest):
    mine, theirs, out = rest[:rows], rest[rows : 2 * rows], rest[-1]
    part, width = CAP // 2, out.shape[1]
    side = lax.axis_index("op")
    out[...] = jnp.zeros_like(out)
    for d in range(rows):
        for h in range(2):
            ids = jnp.where(side == h, mine[d][part * width :, :], theirs[d][part * width :, :]).astype(jnp.float32)
            for m in range(part):
                at = pl.ds(m * width, width)
                block = jnp.where(side == h, mine[d][at, :], theirs[d][at, :]).astype(jnp.float32)
                target = jnp.max(ids[m : m + 1, :]).astype(jnp.int32)
                out[target] += block.T


def shards(sizes, psi, left_ops, right_ops, left_qn, right_qn, pair_slot, slot_target):
    rows, blocks, halves = sizes
    sectors, width = psi.shape[0], psi.shape[1]
    operators, left_local = left_ops.shape[0], left_ops.shape[1]
    slots = pair_slot.T
    smem = pl.BlockSpec(memory_space=pltpu.SMEM)
    vmem = pl.BlockSpec(memory_space=pltpu.VMEM)
    hbm = pl.BlockSpec(memory_space=pltpu.HBM)
    sets = max(1, min(SETS, MOST_SLOTS // (rows * CAP)))
    total_shape = (rows * CAP + 1, width, width)
    right_count = right_ops.shape[1]
    params = pltpu.CompilerParams(vmem_limit_bytes=8 * 2**20)

    def cost(share):
        flops = int(16 * operators * sectors * width**3 * share)
        return pl.CostEstimate(flops=flops, bytes_accessed=4 * 2**20, transcendentals=0)

    assert rows % 2 == 0
    relayed = operators * 5 // 16
    swap = [(i, i ^ 1) for i in range(rows)]

    def over_blocks(part):
        return [lax.ppermute(part, "blk", [((b + d) % blocks, b) for b in range(blocks)]) for d in range(1, blocks)]

    direct, middle, psi_near, head, plan, *totals = pl.pallas_call(
        functools.partial(first_kernel, blocks),
        out_shape=[
            jax.ShapeDtypeStruct((relayed, *left_ops.shape[1:]), left_ops.dtype),
            jax.ShapeDtypeStruct((operators - 2 * relayed, *left_ops.shape[1:]), left_ops.dtype),
            jax.ShapeDtypeStruct(psi.shape, psi.dtype),
            jax.ShapeDtypeStruct((BLOCK_K, *right_ops.shape[1:]), right_ops.dtype),
            jax.ShapeDtypeStruct((2 * sectors + 3 + blocks * left_local,), jnp.int32),
            *[jax.ShapeDtypeStruct(total_shape, jnp.float32)] * sets,
        ],
        in_specs=[hbm] * 5,
        out_specs=[vmem] * 4 + [smem] + [vmem] * sets,
        scratch_shapes=[
            pltpu.SMEM(left_qn.shape, jnp.int32),
            pltpu.SMEM(right_qn.shape, jnp.int32),
            pltpu.SemaphoreType.DMA((6,)),
        ],
        compiler_params=params,
        name="first_loads",
    )(*(pltpu.with_memory_space_constraint(x, pltpu.HBM) for x in (left_qn, right_qn, psi, right_ops, left_ops)))
    direct, middle = over_blocks(direct), over_blocks(middle)

    half = pl.pallas_call(
        right_kernel,
        out_shape=jax.ShapeDtypeStruct((sectors // GROUP, operators, GROUP // 2, width, 2 * width), jnp.bfloat16),
        in_specs=[smem, vmem, vmem, hbm],
        out_specs=vmem,
        scratch_shapes=[
            pltpu.VMEM((operators - BLOCK_K, *right_ops.shape[1:]), right_ops.dtype),
            pltpu.VMEM((sectors // 2, 2 * width, right_count * width), jnp.bfloat16),
            pltpu.SemaphoreType.DMA((operators // BLOCK_K - 1,)),
        ],
        compiler_params=params,
        cost_estimate=cost(0.5),
        name="right_side",
    )(plan, psi_near, head, pltpu.with_memory_space_constraint(right_ops, pltpu.HBM))
    half, direct = lax.optimization_barrier((half, direct))
    swapped = [lax.ppermute(part, "sector", swap) for part in direct]
    totals = pl.pallas_call(
        own_kernel,
        out_shape=[jax.ShapeDtypeStruct(total_shape, jnp.float32)] * sets,
        in_specs=[smem] * 2 + [vmem] * (2 + sets),
        out_specs=[vmem] * sets,
        input_output_aliases={4 + j: j for j in range(sets)},
        compiler_params=params,
        cost_estimate=cost(0.25),
        name="own_left",
    )(plan, slots, half, left_ops, *totals)
    results = pl.pallas_call(
        functools.partial(other_kernel, rows, sets),
        out_shape=[jax.ShapeDtypeStruct(total_shape, jnp.float32)] * sets
        + [jax.ShapeDtypeStruct((rows * CAP // 2, width, width), kind) for kind in (jnp.float32, jnp.bfloat16)],
        in_specs=[smem] * 2 + [vmem] * (4 + sets),
        out_specs=[vmem] * (sets + 2),
        input_output_aliases={6 + j: j for j in range(sets)},
        compiler_params=params,
        cost_estimate=cost(0.25),
        name="other_left",
    )(plan, slots, half, jnp.stack(swapped), jnp.stack(direct), jnp.stack(middle), *totals)
    keep, give = results[sets:]

    def over_cores(block):
        return lax.ppermute(block, "op", [(h, halves - 1 - h) for h in range(halves)])

    partial = pl.pallas_call(
        combine_kernel,
        out_shape=[jax.ShapeDtypeStruct((CAP // 2 * width + TAIL, width), jnp.bfloat16)] * rows,
        in_specs=[smem] + [vmem] * 2,
        out_specs=[vmem] * rows,
        compiler_params=params,
        name="combine",
    )(slot_target, keep, over_cores(give))
    crossed = {
        d: lax.ppermute(partial[d], "sector", [(i, (i + d) % rows) for i in range(rows)]) for d in range(1, rows)
    }
    mine = [partial[0]] + [crossed[d] for d in range(1, rows)]
    theirs = [over_cores(block) for block in mine]
    return pl.pallas_call(
        functools.partial(assemble_kernel, rows),
        out_shape=jax.ShapeDtypeStruct((sectors, width, width), jnp.float32),
        in_specs=[vmem] * (2 * rows),
        out_specs=vmem,
        compiler_params=params,
        name="assemble",
    )(*mine, *theirs)


def solution(mesh):
    in_specs = (
        P(("groups", "sector", "blk"), None, None),
        P(("groups", "op"), "blk", None, None),
        P(("groups", "op"), None, None, None),
        P(("groups", "sector", "blk")),
        P(("groups", "sector", "blk")),
        P(("groups", "op"), ("sector", "blk")),
        P(("groups", "sector"), "blk", None),
    )
    out_specs = P(("groups", "sector", "blk"), None, None)
    sizes = tuple(mesh.shape[name] for name in ("sector", "blk", "op"))
    return jax.shard_map(
        functools.partial(shards, sizes), mesh=mesh, in_specs=in_specs, out_specs=out_specs, check_vma=False
    )
```

time: 43.5 us -> 45.2 us (1.039)
  Pallas kernels: 21.1 us -> 25.7 us
  waiting for transfers between devices: 8.95 us -> 5.59 us
  starting transfers between devices: 10.5 us -> 13.4 us
  local copies, waits for them, and re-layouts: 2.06 us -> 0.01 us
    pallas_call x1, Pallas kernels: 3.64 us -> 6.68 us  [shards(): pl.pallas_call(own_kernel, out_shape=[jax.ShapeDtypeStruct(total_shape, j...]
    pallas_call x1 -> x2, Pallas kernels: 8.92 us -> 11.4 us  [the longest x1 8.97 us: shards(): pl.pallas_call(right_kernel, out_shape=jax.ShapeDtypeStruct((sectors // G...]
    ppermute x3, starting transfers between devices: 4.71 us -> 7.16 us  [shards(): lax.ppermute(partial[d], 'sector', [(i, (i + d) % rows) for i in range(ro...]
    ppermute x3, waiting for transfers between devices: 4.43 us -> 2.7 us  [shards(): lax.ppermute(partial[d], 'sector', [(i, (i + d) % rows) for i in range(ro...]
    ppermute x2, waiting for transfers between devices: 1.67 us -> 0.01 us  [over_blocks(): lax.ppermute(part, 'blk', [((b + d) % blocks, b) for b in range(blocks)])]
    slice x1 -> x0, local copies, waits for them, and re-layouts: 1.08 us -> none  [shards(): middle = over_blocks(left_ops[quarter:operators - quarter])]
    dynamic_slice x1 -> x0, local copies, waits for them, and re-layouts: 0.97 us -> none  [shards(): lax.dynamic_slice_in_dim(left_ops, odd * (operators - quarter), quarter, 0)]
    pallas_call x1, Pallas kernels: 6.44 us -> 5.48 us  [shards(): pl.pallas_call(functools.partial(other_kernel, rows, sets), out_shape=[ja...]
  transfers between devices with their start and end apart: 11 -> 11, of which waited for: 7 -> 5; matrix products, arithmetic and copies ran while one was open for 3% -> 0% of each run, Pallas kernels for 29% -> 35%
where the time goes in v6:
time: 45.2 us; the launch traced here: 44.8 us
  Pallas kernels  25.7 us (57%)
  starting transfers between devices  13.4 us (30%)
  waiting for transfers between devices  5.59 us (12%)
    pallas_call x1, Pallas kernels, shards(): pl.pallas_call(right_kernel, out_shape=jax.ShapeDtypeStruct((sectors // G...  8.97 us
    ppermute x3, starting transfers between devices, shards(): lax.ppermute(partial[d], 'sector', [(i, (i + d) % rows) for i in range(ro...  7.16 us
    pallas_call x1, Pallas kernels, shards(): pl.pallas_call(own_kernel, out_shape=[jax.ShapeDtypeStruct(total_shape, j...  6.68 us
    pallas_call x1, Pallas kernels, shards(): pl.pallas_call(functools.partial(other_kernel, rows, sets), out_shape=[ja...  5.48 us
    ppermute x2, starting transfers between devices, over_blocks(): lax.ppermute(part, 'blk', [((b + d) % blocks, b) for b in range(blocks)])  3.08 us
    ppermute x3, waiting for transfers between devices, shards(): lax.ppermute(partial[d], 'sector', [(i, (i + d) % rows) for i in range(ro...  2.7 us
    pallas_call x1, Pallas kernels, shards(): pl.pallas_call(functools.partial(first_kernel, blocks), out_shape=[jax.Sh...  2.43 us
    ppermute x5, waiting for transfers between devices, over_cores(): lax.ppermute(block, 'op', [(h, halves - 1 - h) for h in range(halves)])  2.43 us
  transfers between devices with their start and end apart: 11, of which 5 were waited for; matrix products, arithmetic and copies ran while one was open for 0% of the time, Pallas kernels for 35%

profile of v6, /device:TPU:0, one launch (start us, length us, event | category | flops | bytes accessed | tf_op | source)
XLA Modules:
  0.0 44.8 jit_solution(5575212925225409914)
XLA Ops:
  0.0 2.4 %first_loads.1 = (bf16[10,1,128,128]{3,2,1,0:T(8,128)(2,1)S(1)}, bf16[12,1,128,128]{3,2,1,0:T(8,128)(2,1)S(1)}, bf16[24,128,128]{2,1,0:T(8,128)(2,1)S(1)}, bf16[...) custom-call(s32[24]{0:T(128)} %left_qn_in.1, ...), custom_call_target="tpu_custom_call" | custom-call | tf_op jit(solution)/shard_map/first_loads/pallas_call | solution.py:230
  2.4 3.0 %collective-permute-start = (bf16[10,1,128,128]{3,2,0,1:T(8,128)(2,1)S(1)}, bf16[10,1,128,128]{3,2,0,1:T(8,128)(2,1)S(1)}, u32[]{:S(2)}, u32[]{:S(2)}) collective-permute-start(bf16[10,1,128,128]{3,2,0,1:T(8,128)(2,1)S(1)} %bitcast.14), channel_id=1, source_target_pairs={{2,0},{0,2},{3,1},{1,3},{6,4},{4,6},{7,5},{5,7},{10,8},{8,10},{11,... | collective-permute-start | bytes 983048 | tf_op jit(solution)/shard_map/ppermute | solution.py:228
  5.4 0.1 collective-permute-start.2
  5.5 0.0 copy-start
  5.5 9.0 %right_side.1.half = bf16[6,32,2,128,256]{4,3,2,1,0:T(8,128)(2,1)S(1)} custom-call(s32[53]{0:T(128)S(1)} %get-tuple-element.26.plan, bf16[24,128,128]{2,1,0:T(8,128)(2,1)S(1)} %get-tuple-element.27.psi, bf16[8,2,128,128]{3,2,1,0:T(8,128)(2,1)S(1)} %get-tuple-element.28.head, bf16[32,2,128,128]{3,2,1,0:T(8,128)(2,1)} %right_in.3), custom_call_target="tpu_custom_call" | custom-call | flops 12884901888 | bytes 4194304 | tf_op jit(solution)/shard_map/right_side/pallas_call | solution.py:252
  14.5 0.0 collective-permute-done
  14.5 2.1 %collective-permute-start.1 = (bf16[10,1,128,128]{3,2,0,1:T(8,128)(2,1)S(1)}, bf16[10,1,128,128]{3,2,0,1:T(8,128)(2,1)S(1)}, u32[]{:S(2)}, u32[]{:S(2)}) collective-permute-start(bf16[10,1,128,128]{3,2,0,1:T(8,128)(2,1)S(1)} %collective-permute-done), channel_id=1, source_target_pairs={{0,4},{4,0},{8,12},{12,8},{1,5},{5,1},{9,13},{13,9},{2,6},{6,2},{1... | collective-permute-start | bytes 983048 | tf_op jit(solution)/shard_map/ppermute | solution.py:267
  16.6 0.0 copy-done
  16.6 0.0 copy-done.1
  16.6 6.7 %own_left.1 = (f32[17,128,128]{2,1,0:T(8,128)S(1)}, f32[17,128,128]{2,1,0:T(8,128)S(1)}, f32[17,128,128]{2,1,0:T(8,128)S(1)}, f32[17,128,128]{2,1,0:T(8,128)S(1)}) custom-call(s32[53]{0:T(128)S(1)} %get-tuple-element.26.plan, s32[24,32]{1,0:T(8,128)S(1)} %bitcast.11, ...), custom_call_target="tpu_custom_call", output_to_operand_aliasing={{0}: (4, {}), {1}: (5, {}), {2}: (6, {}), {3}: (7, {})} | custom-call | flops 6442450944 | bytes 4194304 | tf_op jit(solution)/shard_map/own_left/pallas_call | solution.py:268
  23.3 0.0 collective-permute-done.2
  23.3 0.5 %collective-permute-done.1 = bf16[10,1,128,128]{3,2,0,1:T(8,128)(2,1)S(1)} collective-permute-done((bf16[10,1,128,128]{3,2,0,1:T(8,128)(2,1)S(1)}, bf16[10,1,128,128]{3,2,0,1:T(8,128)(2,1)S(1)}, u32[]{:S(2)}, u32[]{:S(2)}) %collective-permute-start.1) | collective-permute-done | bytes 327712 | tf_op jit(solution)/shard_map/ppermute | solution.py:267
  23.8 5.5 %other_left.1 = (f32[17,128,128]{2,1,0:T(8,128)S(1)}, f32[17,128,128]{2,1,0:T(8,128)S(1)}, f32[17,128,128]{2,1,0:T(8,128)S(1)}, f32[17,128,128]{2,1,0:T(8,128)S(...) custom-call(s32[53]{0:T(128)S(1)} %get-tuple-element.26.plan, ...), custom_call_target="tpu_custom_call", output_to_operand_aliasing={{0}: (6, {}), {1}: (7, {}), {2}: (8, {}), {3}: (9, {})} | custom-call | flops 6442450944 | bytes 4194304 | tf_op jit(solution)/shard_map/other_left/pallas_call | solution.py:278
  29.3 0.1 collective-permute-start.3
  29.3 1.5 %collective-permute-done.3.taken = bf16[8,128,128]{2,1,0:T(8,128)(2,1)S(1)} collective-permute-done((bf16[8,128,128]{2,1,0:T(8,128)(2,1)S(1)}, bf16[8,128,128]{2,1,0:T(8,128)(2,1)S(1)}, u32[]{:S(2)}, u32[]{:S(2)}) %collective-permute-start.3) | collective-permute-done | bytes 262176 | tf_op jit(solution)/shard_map/ppermute | solution.py:292
  30.9 0.0 copy-done.2
  30.9 0.6 %combine.1 = (bf16[272,128]{1,0:T(8,128)(2,1)S(1)}, bf16[272,128]{1,0:T(8,128)(2,1)S(1)}, bf16[272,128]{1,0:T(8,128)(2,1)S(1)}, bf16[272,128]{1,0:T(8,128)(2,1)S(1)}) custom-call(s32[1,1,16]{2,1,0:T(1,128)S(1)} %copy-done.2, f32[8,128,128]{2,1,0:T(8,128)S(1)} %get-tuple-element.41.keep, bf16[8,128,128]{2,1,0:T(8,128)(2,1)S(1)} %collective-permute-done.3.taken), custom_call_target="tpu_custom_call" | custom-call | tf_op jit(solution)/shard_map/combine/pallas_call | solution.py:294
  31.5 3.3 %collective-permute-start.4 = (bf16[272,128]{1,0:T(8,128)(2,1)S(1)}, bf16[272,128]{1,0:T(8,128)(2,1)S(1)}, u32[]{:S(2)}, u32[]{:S(2)}) collective-permute-start(bf16[272,128]{1,0:T(8,128)(2,1)S(1)} %get-tuple-element.44), channel_id=1, source_target_pairs={{0,4},{4,8},{8,12},{12,0},{1,5},{5,9},{9,13},{13,1},{2,6},{6,10},{... | collective-permute-start | bytes 208904 | tf_op jit(solution)/shard_map/ppermute | solution.py:303
  34.8 1.1 %collective-permute-start.5 = (bf16[272,128]{1,0:T(8,128)(2,1)S(1)}, bf16[272,128]{1,0:T(8,128)(2,1)S(1)}, u32[]{:S(2)}, u32[]{:S(2)}) collective-permute-start(bf16[272,128]{1,0:T(8,128)(2,1)S(1)} %get-tuple-element.45), channel_id=1, source_target_pairs={{0,8},{4,12},{8,0},{12,4},{1,9},{5,13},{9,1},{13,5},{2,10},{6,14},... | collective-permute-start | bytes 208904 | tf_op jit(solution)/shard_map/ppermute | solution.py:303
  35.9 2.8 %collective-permute-start.6 = (bf16[272,128]{1,0:T(8,128)(2,1)S(1)}, bf16[272,128]{1,0:T(8,128)(2,1)S(1)}, u32[]{:S(2)}, u32[]{:S(2)}) collective-permute-start(bf16[272,128]{1,0:T(8,128)(2,1)S(1)} %get-tuple-element.46), channel_id=1, source_target_pairs={{0,12},{4,0},{8,4},{12,8},{1,13},{5,1},{9,5},{13,9},{2,14},{6,2},{... | collective-permute-start | bytes 208904 | tf_op jit(solution)/shard_map/ppermute | solution.py:303
  38.6 0.0 collective-permute-start.7
  38.6 0.0 collective-permute-done.4.rest_1_
  38.7 0.5 %collective-permute-start.8 = (bf16[272,128]{1,0:T(8,128)(2,1)S(1)}, bf16[272,128]{1,0:T(8,128)(2,1)S(1)}, u32[]{:S(2)}, u32[]{:S(2)}) collective-permute-start(bf16[272,128]{1,0:T(8,128)(2,1)S(1)} %collective-permute-done.4.rest_1_), channel_id=1, source_target_pairs={{0,1},{1,0},{2,3},{3,2},{4,5},{5,4},{6,7},{7,6},{8,9},{9,8},{10,11... | collective-permute-start | bytes 208904 | tf_op jit(solution)/shard_map/ppermute | solution.py:292
  39.2 2.7 %collective-permute-done.5.rest_2_ = bf16[272,128]{1,0:T(8,128)(2,1)S(1)} collective-permute-done((bf16[272,128]{1,0:T(8,128)(2,1)S(1)}, bf16[272,128]{1,0:T(8,128)(2,1)S(1)}, u32[]{:S(2)}, u32[]{:S(2)}) %collective-permute-start.5) | collective-permute-done | bytes 69664 | tf_op jit(solution)/shard_map/ppermute | solution.py:303
  41.9 0.0 collective-permute-start.9
  41.9 0.0 collective-permute-done.6.rest_3_
  41.9 0.5 %collective-permute-start.10 = (bf16[272,128]{1,0:T(8,128)(2,1)S(1)}, bf16[272,128]{1,0:T(8,128)(2,1)S(1)}, u32[]{:S(2)}, u32[]{:S(2)}) collective-permute-start(bf16[272,128]{1,0:T(8,128)(2,1)S(1)} %collective-permute-done.6.rest_3_), channel_id=1, source_target_pairs={{0,1},{1,0},{2,3},{3,2},{4,5},{5,4},{6,7},{7,6},{8,9},{9,8},{10,11... | collective-permute-start | bytes 208904 | tf_op jit(solution)/shard_map/ppermute | solution.py:292
  42.4 0.0 collective-permute-done.7.rest_4_
  42.4 0.0 collective-permute-done.8.rest_5_
  42.4 0.7 %collective-permute-done.9.rest_6_ = bf16[272,128]{1,0:T(8,128)(2,1)S(1)} collective-permute-done((bf16[272,128]{1,0:T(8,128)(2,1)S(1)}, bf16[272,128]{1,0:T(8,128)(2,1)S(1)}, u32[]{:S(2)}, u32[]{:S(2)}) %collective-permute-start.9) | collective-permute-done | bytes 69664 | tf_op jit(solution)/shard_map/ppermute | solution.py:292
  43.1 0.2 collective-permute-done.10.rest_7_
  43.3 1.5 %assemble.1 = f32[24,128,128]{2,1,0:T(8,128)} custom-call(bf16[272,128]{1,0:T(8,128)(2,1)S(1)} %get-tuple-element.43.rest_0_, bf16[272,128]{1,0:T(8,128)(2,1)S(1)} %collective-permute-done.4.rest_1_, bf16[272,128]{1,0:T(8,128)(2,1)S(1)} %collective-permute-done.5.rest_2_, bf16[272,128]{1,0:T(8,128)(2,1)S(1)} %collective-permute-done.6.rest_3_, ...), custom_call_target="tpu_custom_call" | custom-call | tf_op jit(solution)/shard_map/assemble/pallas_call | solution.py:307
  (2 shorter events, 0.0 us)
Async XLA Ops:
  2.4 12.1 %collective-permute-start = (bf16[10,1,128,128]{3,2,0,1:T(8,128)(2,1)S(1)}, bf16[10,1,128,128]{3,2,0,1:T(8,128)(2,1)S(1)}, u32[]{:S(2)}, u32[]{:S(2)}) collective-permute-start(bf16[10,1,128,128]{3,2,0,1:T(8,128)(2,1)S(1)} %bitcast.14), channel_id=1, source_target_pairs={{2,0},{0,2},{3,1},{1,3},{6,4},{4,6},{7,5},{5,7},{10,8},{8,10},{11,... | collective-permute-start | bytes 983048 | tf_op jit(solution)/shard_map/ppermute | solution.py:228
  5.4 17.9 %collective-permute-start.2 = (bf16[12,1,128,128]{3,2,0,1:T(8,128)(2,1)S(1)}, bf16[12,1,128,128]{3,2,0,1:T(8,128)(2,1)S(1)}, u32[]{:S(2)}, u32[]{:S(2)}) collective-permute-start(bf16[12,1,128,128]{3,2,0,1:T(8,128)(2,1)S(1)} %bitcast.13), channel_id=1, source_target_pairs={{2,0},{0,2},{3,1},{1,3},{6,4},{4,6},{7,5},{5,7},{10,8},{8,10},{11,... | collective-permute-start | bytes 1179656 | tf_op jit(solution)/shard_map/ppermute | solution.py:228
  5.5 11.1 %copy-start = (bf16[32,1,128,128]{3,2,1,0:T(8,128)(2,1)S(1)}, bf16[32,1,128,128]{3,2,1,0:T(8,128)(2,1)}, u32[]{:S(2)}) copy-start(bf16[32,1,128,128]{3,2,1,0:T(8,128)(2,1)} %left.3) | copy-start | bytes 3145732
  5.5 11.1 %copy-start.1 = (s32[32,24]{0,1:T(8,128)S(1)}, s32[32,24]{0,1:T(8,128)}, u32[]{:S(2)}) copy-start(s32[32,24]{0,1:T(8,128)} %param.12) | copy-start | bytes 9220
  14.5 9.3 %collective-permute-start.1 = (bf16[10,1,128,128]{3,2,0,1:T(8,128)(2,1)S(1)}, bf16[10,1,128,128]{3,2,0,1:T(8,128)(2,1)S(1)}, u32[]{:S(2)}, u32[]{:S(2)}) collective-permute-start(bf16[10,1,128,128]{3,2,0,1:T(8,128)(2,1)S(1)} %collective-permute-done), channel_id=1, source_target_pairs={{0,4},{4,0},{8,12},{12,8},{1,5},{5,1},{9,13},{13,9},{2,6},{6,2},{1... | collective-permute-start | bytes 983048 | tf_op jit(solution)/shard_map/ppermute | solution.py:267
  23.8 7.1 %copy-start.2 = (s32[1,1,16]{2,1,0:T(1,128)S(1)}, s32[1,1,16]{2,1,0:T(1,128)}, u32[]{:S(2)}) copy-start(s32[1,1,16]{2,1,0:T(1,128)} %slot_target.1) | copy-start | bytes 196
  29.3 1.6 %collective-permute-start.3 = (bf16[8,128,128]{2,1,0:T(8,128)(2,1)S(1)}, bf16[8,128,128]{2,1,0:T(8,128)(2,1)S(1)}, u32[]{:S(2)}, u32[]{:S(2)}) collective-permute-start(bf16[8,128,128]{2,1,0:T(8,128)(2,1)S(1)} %get-tuple-element.42), channel_id=1, source_target_pairs={{0,1},{1,0},{2,3},{3,2},{4,5},{5,4},{6,7},{7,6},{8,9},{9,8},{10,11... | collective-permute-start | bytes 786440 | tf_op jit(solution)/shard_map/ppermute | solution.py:292
  31.5 7.2 %collective-permute-start.4 = (bf16[272,128]{1,0:T(8,128)(2,1)S(1)}, bf16[272,128]{1,0:T(8,128)(2,1)S(1)}, u32[]{:S(2)}, u32[]{:S(2)}) collective-permute-start(bf16[272,128]{1,0:T(8,128)(2,1)S(1)} %get-tuple-element.44), channel_id=1, source_target_pairs={{0,4},{4,8},{8,12},{12,0},{1,5},{5,9},{9,13},{13,1},{2,6},{6,10},{... | collective-permute-start | bytes 208904 | tf_op jit(solution)/shard_map/ppermute | solution.py:303
  34.8 7.1 %collective-permute-start.5 = (bf16[272,128]{1,0:T(8,128)(2,1)S(1)}, bf16[272,128]{1,0:T(8,128)(2,1)S(1)}, u32[]{:S(2)}, u32[]{:S(2)}) collective-permute-start(bf16[272,128]{1,0:T(8,128)(2,1)S(1)} %get-tuple-element.45), channel_id=1, source_target_pairs={{0,8},{4,12},{8,0},{12,4},{1,9},{5,13},{9,1},{13,5},{2,10},{6,14},... | collective-permute-start | bytes 208904 | tf_op jit(solution)/shard_map/ppermute | solution.py:303
  35.9 6.0 %collective-permute-start.6 = (bf16[272,128]{1,0:T(8,128)(2,1)S(1)}, bf16[272,128]{1,0:T(8,128)(2,1)S(1)}, u32[]{:S(2)}, u32[]{:S(2)}) collective-permute-start(bf16[272,128]{1,0:T(8,128)(2,1)S(1)} %get-tuple-element.46), channel_id=1, source_target_pairs={{0,12},{4,0},{8,4},{12,8},{1,13},{5,1},{9,5},{13,9},{2,14},{6,2},{... | collective-permute-start | bytes 208904 | tf_op jit(solution)/shard_map/ppermute | solution.py:303
  38.6 3.7 %collective-permute-start.7 = (bf16[272,128]{1,0:T(8,128)(2,1)S(1)}, bf16[272,128]{1,0:T(8,128)(2,1)S(1)}, u32[]{:S(2)}, u32[]{:S(2)}) collective-permute-start(bf16[272,128]{1,0:T(8,128)(2,1)S(1)} %get-tuple-element.43.rest_0_), channel_id=1, source_target_pairs={{0,1},{1,0},{2,3},{3,2},{4,5},{5,4},{6,7},{7,6},{8,9},{9,8},{10,11... | collective-permute-start | bytes 208904 | tf_op jit(solution)/shard_map/ppermute | solution.py:292
  38.7 3.7 %collective-permute-start.8 = (bf16[272,128]{1,0:T(8,128)(2,1)S(1)}, bf16[272,128]{1,0:T(8,128)(2,1)S(1)}, u32[]{:S(2)}, u32[]{:S(2)}) collective-permute-start(bf16[272,128]{1,0:T(8,128)(2,1)S(1)} %collective-permute-done.4.rest_1_), channel_id=1, source_target_pairs={{0,1},{1,0},{2,3},{3,2},{4,5},{5,4},{6,7},{7,6},{8,9},{9,8},{10,11... | collective-permute-start | bytes 208904 | tf_op jit(solution)/shard_map/ppermute | solution.py:292
  41.9 1.3 %collective-permute-start.9 = (bf16[272,128]{1,0:T(8,128)(2,1)S(1)}, bf16[272,128]{1,0:T(8,128)(2,1)S(1)}, u32[]{:S(2)}, u32[]{:S(2)}) collective-permute-start(bf16[272,128]{1,0:T(8,128)(2,1)S(1)} %collective-permute-done.5.rest_2_), channel_id=1, source_target_pairs={{0,1},{1,0},{2,3},{3,2},{4,5},{5,4},{6,7},{7,6},{8,9},{9,8},{10,11... | collective-permute-start | bytes 208904 | tf_op jit(solution)/shard_map/ppermute | solution.py:292
  41.9 1.4 %collective-permute-start.10 = (bf16[272,128]{1,0:T(8,128)(2,1)S(1)}, bf16[272,128]{1,0:T(8,128)(2,1)S(1)}, u32[]{:S(2)}, u32[]{:S(2)}) collective-permute-start(bf16[272,128]{1,0:T(8,128)(2,1)S(1)} %collective-permute-done.6.rest_3_), channel_id=1, source_target_pairs={{0,1},{1,0},{2,3},{3,2},{4,5},{5,4},{6,7},{7,6},{8,9},{9,8},{10,11... | collective-permute-start | bytes 208904 | tf_op jit(solution)/shard_map/ppermute | solution.py:292

commit v7 on v5

--- a/solution.py
+++ b/solution.py
@@ -9,9 +9,9 @@
 
 CAP = 4
 GROUP = 4
-SETS = 2
+SETS = 4
 MOST_SLOTS = 64
-BLOCK_K = 8
+BLOCK_K = 16
 TAIL = 16
 NT = (((1,), (1,)), ((), ()))
 
@@ -76,9 +76,9 @@
     for pair in range(sectors // 2):
         for e in range(2):
             s = plan[2 * pair + e]
-            block = psi[s]
+            block = psi[s].T
             for r in range(right_count):
-                sources[pair, e * width : (e + 1) * width, r * width : (r + 1) * width] = jnp.where(
+                sources[pair, r * width : (r + 1) * width, e * width : (e + 1) * width] = jnp.where(
                     right_qn[s] == r, block, zero
                 )
 
@@ -87,7 +87,7 @@
         at = pl.ds(i * BLOCK_K, BLOCK_K)
         stream = jnp.concatenate([right[at, r].reshape(BLOCK_K * width, width) for r in range(right_count)], axis=1)
         for pair in range(sectors // 2):
-            product = lax.dot_general(stream, sources[pair], NT, preferred_element_type=jnp.float32)
+            product = jnp.dot(stream, sources[pair], preferred_element_type=jnp.float32)
             half[pair // 2, at, pair % 2] = product.astype(jnp.bfloat16).reshape(BLOCK_K, width, 2 * width)
         return unused
 
@@ -166,7 +166,7 @@
     row, side = lax.axis_index("sector"), lax.axis_index("op")
     line = lax.broadcasted_iota(jnp.int32, (TAIL, width), 0)
     for d, out in enumerate(outs):
-        owner = lax.bitwise_xor(row, jnp.int32(d))
+        owner = lax.rem(row + d, jnp.int32(len(outs)))
         ids = jnp.zeros((TAIL, width), jnp.int32)
         for m in range(part):
             block = keep[owner * part + m] + taken[owner * part + m].astype(jnp.float32)
@@ -207,7 +207,7 @@
         flops = int(16 * operators * sectors * width**3 * share)
         return pl.CostEstimate(flops=flops, bytes_accessed=4 * 2**20, transcendentals=0)
 
-    assert rows & (rows - 1) == 0
+    assert rows % 2 == 0
     quarter = operators // 4
     swap = [(i, i ^ 1) for i in range(rows)]
 
@@ -241,7 +241,7 @@
             pltpu.SMEM(right_qn.shape, jnp.int32),
             pltpu.VMEM(psi.shape, psi.dtype),
             pltpu.VMEM(right_ops.shape, right_ops.dtype),
-            pltpu.VMEM((sectors // 2, 2 * width, right_count * width), jnp.bfloat16),
+            pltpu.VMEM((sectors // 2, right_count * width, 2 * width), jnp.bfloat16),
             pltpu.SemaphoreType.DMA((3 + operators // BLOCK_K,)),
         ],
         compiler_params=params,
@@ -284,7 +284,7 @@
         name="combine",
     )(slot_target, keep, over_cores(give))
     crossed = {
-        d: lax.ppermute(partial[d], "sector", [(i, i ^ d) for i in range(rows)]) for d in reversed(range(1, rows))
+        d: lax.ppermute(partial[d], "sector", [(i, (i + d) % rows) for i in range(rows)]) for d in range(1, rows)
     }
     mine = [partial[0]] + [crossed[d] for d in range(1, rows)]
     theirs = [over_cores(block) for block in mine]

time: 43.9 us -> 43.3 us (0.986); the launches traced: 43.1 us -> 43.6 us
  waiting for transfers between devices: 7.46 us -> 10.1 us
  starting transfers between devices: 11.8 us -> 10.1 us
  Pallas kernels: 23.8 us -> 23.3 us
    ppermute x2, waiting for transfers between devices: 0.01 us -> 3.21 us  [over_blocks(): lax.ppermute(part, 'blk', [((b + d) % blocks, b) for b in range(blocks)])]
    pallas_call x1, Pallas kernels: 6.54 us -> 3.72 us  [shards(): pl.pallas_call(own_kernel, out_shape=[jax.ShapeDtypeStruct(total_shape, j...]
    pallas_call x1, Pallas kernels: 5.04 us -> 7.81 us  [shards(): pl.pallas_call(functools.partial(other_kernel, rows, sets), out_shape=[ja...]
    ppermute x3, starting transfers between devices: 5.62 us -> 4.44 us  [shards(): lax.ppermute(partial[d], 'sector', [(i, (i + d) % rows) for i in range(ro...]
    ppermute x3, waiting for transfers between devices: 5.03 us -> 4.51 us  [shards(): lax.ppermute(partial[d], 'sector', [(i, (i + d) % rows) for i in range(ro...]
    ppermute x5, starting transfers between devices: 1.05 us -> 0.59 us  [over_cores(): lax.ppermute(block, 'op', [(h, halves - 1 - h) for h in range(halves)])]
    pallas_call x1, Pallas kernels: 8.92 us -> 8.47 us  [shards(): pl.pallas_call(functools.partial(right_kernel, blocks, left_local), out_s...]
  transfers between devices with their start and end apart: 11 -> 11, of which waited for: 4 -> 6; matrix products, arithmetic and copies ran while one was open for 0% -> 0% of each run, Pallas kernels for 36% -> 28%
where the time goes in v7:
time: 43.3 us; the launch traced here: 43.6 us
  Pallas kernels  23.3 us (54%)
  starting transfers between devices  10.1 us (23%)
  waiting for transfers between devices  10.1 us (23%)
    pallas_call x1, Pallas kernels, shards(): pl.pallas_call(functools.partial(right_kernel, blocks, left_local), out_s...  8.47 us
    pallas_call x1, Pallas kernels, shards(): pl.pallas_call(functools.partial(other_kernel, rows, sets), out_shape=[ja...  7.81 us
    ppermute x3, waiting for transfers between devices, shards(): lax.ppermute(partial[d], 'sector', [(i, (i + d) % rows) for i in range(ro...  4.51 us
    ppermute x3, starting transfers between devices, shards(): lax.ppermute(partial[d], 'sector', [(i, (i + d) % rows) for i in range(ro...  4.44 us
    pallas_call x1, Pallas kernels, shards(): pl.pallas_call(own_kernel, out_shape=[jax.ShapeDtypeStruct(total_shape, j...  3.72 us
    ppermute x2, waiting for transfers between devices, over_blocks(): lax.ppermute(part, 'blk', [((b + d) % blocks, b) for b in range(blocks)])  3.21 us
    ppermute x2, starting transfers between devices, over_blocks(): lax.ppermute(part, 'blk', [((b + d) % blocks, b) for b in range(blocks)])  3.1 us
    ppermute x5, waiting for transfers between devices, over_cores(): lax.ppermute(block, 'op', [(h, halves - 1 - h) for h in range(halves)])  2.43 us
  transfers between devices with their start and end apart: 11, of which 6 were waited for; matrix products, arithmetic and copies ran while one was open for 0% of the time, Pallas kernels for 28%

profile of v7, /device:TPU:0, one launch (start us, length us, event | category | flops | bytes accessed | tf_op | source)
XLA Modules:
  0.0 43.6 jit_solution(5365380516090336488)
XLA Ops:
  0.0 1.1 %cut_left.1 = (bf16[8,1,128,128]{3,2,1,0:T(8,128)(2,1)S(1)}, bf16[16,1,128,128]{3,2,1,0:T(8,128)(2,1)S(1)}) custom-call(bf16[32,1,128,128]{3,2,1,0:T(8,128)(2,1)} %left.3), custom_call_target="tpu_custom_call" | custom-call | tf_op jit(solution)/shard_map/cut_left/pallas_call | solution.py:217
  1.1 3.0 %collective-permute-start = (bf16[8,1,128,128]{3,2,0,1:T(8,128)(2,1)S(1)}, bf16[8,1,128,128]{3,2,0,1:T(8,128)(2,1)S(1)}, u32[]{:S(2)}, u32[]{:S(2)}) collective-permute-start(bf16[8,1,128,128]{3,2,0,1:T(8,128)(2,1)S(1)} %bitcast.14), channel_id=1, source_target_pairs={{2,0},{0,2},{3,1},{1,3},{6,4},{4,6},{7,5},{5,7},{10,8},{8,10},{11,... | collective-permute-start | bytes 786440 | tf_op jit(solution)/shard_map/ppermute | solution.py:215
  4.2 0.0 copy-start
  4.2 0.1 collective-permute-start.2
  4.3 8.5 %right_side.1 = (bf16[6,32,2,128,256]{4,3,2,1,0:T(8,128)(2,1)S(1)}, s32[28]{0:T(128)S(1)}) custom-call(s32[24]{0:T(128)} %left_qn_in.1, s32[24]{0:T(128)} %right_qn_in.1, bf16[24,128,128]{2,1,0:T(8,128)(2,1)} %psi_in.1, bf16[32,2,128,128]{3,2,1,0:T(8,128)(2,1)} %right_in.1), custom_call_target="tpu_custom_call" | custom-call | flops 12884901888 | bytes 4194304 | tf_op jit(solution)/shard_map/right_side/pallas_call | solution.py:231
  12.7 0.0 collective-permute-done
  12.7 2.0 %collective-permute-start.1 = (bf16[8,1,128,128]{3,2,0,1:T(8,128)(2,1)S(1)}, bf16[8,1,128,128]{3,2,0,1:T(8,128)(2,1)S(1)}, u32[]{:S(2)}, u32[]{:S(2)}) collective-permute-start(bf16[8,1,128,128]{3,2,0,1:T(8,128)(2,1)S(1)} %collective-permute-done), channel_id=1, source_target_pairs={{0,4},{4,0},{8,12},{12,8},{1,5},{5,1},{9,13},{13,9},{2,6},{6,2},{1... | collective-permute-start | bytes 786440 | tf_op jit(solution)/shard_map/ppermute | solution.py:252
  14.8 0.0 copy-done
  14.8 0.0 copy-done.1
  14.8 3.7 %own_left.1 = (f32[17,128,128]{2,1,0:T(8,128)S(1)}, f32[17,128,128]{2,1,0:T(8,128)S(1)}, f32[17,128,128]{2,1,0:T(8,128)S(1)}, f32[17,128,128]{2,1,0:T(8,128)S(1)}) custom-call(s32[28]{0:T(128)S(1)} %get-tuple-element.21.plan, s32[24,32]{1,0:T(8,128)S(1)} %bitcast.11, bf16[6,32,2,128,256]{4,3,2,1,0:T(8,128)(2,1)S(1)} %get-tuple-element.24.half, ...), custom_call_target="tpu_custom_call" | custom-call | flops 6442450944 | bytes 4194304 | tf_op jit(solution)/shard_map/own_left/pallas_call | solution.py:253
  18.5 3.2 %collective-permute-done.2 = bf16[16,1,128,128]{3,2,0,1:T(8,128)(2,1)S(1)} collective-permute-done((bf16[16,1,128,128]{3,2,0,1:T(8,128)(2,1)S(1)}, bf16[16,1,128,128]{3,2,0,1:T(8,128)(2,1)S(1)}, u32[]{:S(2)}, u32[]{:S(2)}) %collective-permute-start.2) | collective-permute-done | bytes 524320 | tf_op jit(solution)/shard_map/ppermute | solution.py:215
  21.7 0.0 collective-permute-done.1
  21.7 7.8 %other_left.1 = (f32[17,128,128]{2,1,0:T(8,128)S(1)}, f32[17,128,128]{2,1,0:T(8,128)S(1)}, f32[17,128,128]{2,1,0:T(8,128)S(1)}, f32[17,128,128]{2,1,0:T(8,128)S(...) custom-call(s32[28]{0:T(128)S(1)} %get-tuple-element.21.plan, ...), custom_call_target="tpu_custom_call", output_to_operand_aliasing={{0}: (6, {}), {1}: (7, {}), {2}: (8, {}), {3}: (9, {})} | custom-call | flops 6442450944 | bytes 4194304 | tf_op jit(solution)/shard_map/other_left/pallas_call | solution.py:262
  29.5 0.1 collective-permute-start.3
  29.6 1.5 %collective-permute-done.3.taken = bf16[8,128,128]{2,1,0:T(8,128)(2,1)S(1)} collective-permute-done((bf16[8,128,128]{2,1,0:T(8,128)(2,1)S(1)}, bf16[8,128,128]{2,1,0:T(8,128)(2,1)S(1)}, u32[]{:S(2)}, u32[]{:S(2)}) %collective-permute-start.3) | collective-permute-done | bytes 262176 | tf_op jit(solution)/shard_map/ppermute | solution.py:276
  31.1 0.0 copy-done.2
  31.1 0.6 %combine.1 = (bf16[272,128]{1,0:T(8,128)(2,1)S(1)}, bf16[272,128]{1,0:T(8,128)(2,1)S(1)}, bf16[272,128]{1,0:T(8,128)(2,1)S(1)}, bf16[272,128]{1,0:T(8,128)(2,1)S(1)}) custom-call(s32[1,1,16]{2,1,0:T(1,128)S(1)} %copy-done.2, f32[8,128,128]{2,1,0:T(8,128)S(1)} %get-tuple-element.31.keep, bf16[8,128,128]{2,1,0:T(8,128)(2,1)S(1)} %collective-permute-done.3.taken), custom_call_target="tpu_custom_call" | custom-call | tf_op jit(solution)/shard_map/combine/pallas_call | solution.py:278
  31.7 0.1 collective-permute-start.4
  31.8 1.7 %collective-permute-start.5 = (bf16[272,128]{1,0:T(8,128)(2,1)S(1)}, bf16[272,128]{1,0:T(8,128)(2,1)S(1)}, u32[]{:S(2)}, u32[]{:S(2)}) collective-permute-start(bf16[272,128]{1,0:T(8,128)(2,1)S(1)} %get-tuple-element.35), channel_id=1, source_target_pairs={{0,8},{4,12},{8,0},{12,4},{1,9},{5,13},{9,1},{13,5},{2,10},{6,14},... | collective-permute-start | bytes 208904 | tf_op jit(solution)/shard_map/ppermute | solution.py:287
  33.5 2.7 %collective-permute-start.6 = (bf16[272,128]{1,0:T(8,128)(2,1)S(1)}, bf16[272,128]{1,0:T(8,128)(2,1)S(1)}, u32[]{:S(2)}, u32[]{:S(2)}) collective-permute-start(bf16[272,128]{1,0:T(8,128)(2,1)S(1)} %get-tuple-element.36), channel_id=1, source_target_pairs={{0,12},{4,0},{8,4},{12,8},{1,13},{5,1},{9,5},{13,9},{2,14},{6,2},{... | collective-permute-start | bytes 208904 | tf_op jit(solution)/shard_map/ppermute | solution.py:287
  36.2 0.0 collective-permute-start.7
  36.2 2.5 %collective-permute-done.4.rest_1_ = bf16[272,128]{1,0:T(8,128)(2,1)S(1)} collective-permute-done((bf16[272,128]{1,0:T(8,128)(2,1)S(1)}, bf16[272,128]{1,0:T(8,128)(2,1)S(1)}, u32[]{:S(2)}, u32[]{:S(2)}) %collective-permute-start.4) | collective-permute-done | bytes 69664 | tf_op jit(solution)/shard_map/ppermute | solution.py:287
  38.7 0.0 collective-permute-start.8
  38.7 2.0 %collective-permute-done.5.rest_2_ = bf16[272,128]{1,0:T(8,128)(2,1)S(1)} collective-permute-done((bf16[272,128]{1,0:T(8,128)(2,1)S(1)}, bf16[272,128]{1,0:T(8,128)(2,1)S(1)}, u32[]{:S(2)}, u32[]{:S(2)}) %collective-permute-start.5) | collective-permute-done | bytes 69664 | tf_op jit(solution)/shard_map/ppermute | solution.py:287
  40.7 0.0 collective-permute-start.9
  40.7 0.0 collective-permute-done.6.rest_3_
  40.7 0.5 %collective-permute-start.10 = (bf16[272,128]{1,0:T(8,128)(2,1)S(1)}, bf16[272,128]{1,0:T(8,128)(2,1)S(1)}, u32[]{:S(2)}, u32[]{:S(2)}) collective-permute-start(bf16[272,128]{1,0:T(8,128)(2,1)S(1)} %collective-permute-done.6.rest_3_), channel_id=1, source_target_pairs={{0,1},{1,0},{2,3},{3,2},{4,5},{5,4},{6,7},{7,6},{8,9},{9,8},{10,11... | collective-permute-start | bytes 208904 | tf_op jit(solution)/shard_map/ppermute | solution.py:276
  41.2 0.0 collective-permute-done.7.rest_4_
  41.2 0.0 collective-permute-done.8.rest_5_
  41.2 0.7 %collective-permute-done.9.rest_6_ = bf16[272,128]{1,0:T(8,128)(2,1)S(1)} collective-permute-done((bf16[272,128]{1,0:T(8,128)(2,1)S(1)}, bf16[272,128]{1,0:T(8,128)(2,1)S(1)}, u32[]{:S(2)}, u32[]{:S(2)}) %collective-permute-start.9) | collective-permute-done | bytes 69664 | tf_op jit(solution)/shard_map/ppermute | solution.py:276
  41.9 0.2 collective-permute-done.10.rest_7_
  42.1 1.5 %assemble.1 = f32[24,128,128]{2,1,0:T(8,128)} custom-call(bf16[272,128]{1,0:T(8,128)(2,1)S(1)} %get-tuple-element.33.rest_0_, bf16[272,128]{1,0:T(8,128)(2,1)S(1)} %collective-permute-done.4.rest_1_, bf16[272,128]{1,0:T(8,128)(2,1)S(1)} %collective-permute-done.5.rest_2_, bf16[272,128]{1,0:T(8,128)(2,1)S(1)} %collective-permute-done.6.rest_3_, ...), custom_call_target="tpu_custom_call" | custom-call | tf_op jit(solution)/shard_map/assemble/pallas_call | solution.py:291
  (2 shorter events, 0.0 us)
Async XLA Ops:
  1.1 11.6 %collective-permute-start = (bf16[8,1,128,128]{3,2,0,1:T(8,128)(2,1)S(1)}, bf16[8,1,128,128]{3,2,0,1:T(8,128)(2,1)S(1)}, u32[]{:S(2)}, u32[]{:S(2)}) collective-permute-start(bf16[8,1,128,128]{3,2,0,1:T(8,128)(2,1)S(1)} %bitcast.14), channel_id=1, source_target_pairs={{2,0},{0,2},{3,1},{1,3},{6,4},{4,6},{7,5},{5,7},{10,8},{8,10},{11,... | collective-permute-start | bytes 786440 | tf_op jit(solution)/shard_map/ppermute | solution.py:215
  4.2 10.6 %copy-start = (bf16[32,1,128,128]{3,2,1,0:T(8,128)(2,1)S(1)}, bf16[32,1,128,128]{3,2,1,0:T(8,128)(2,1)}, u32[]{:S(2)}) copy-start(bf16[32,1,128,128]{3,2,1,0:T(8,128)(2,1)} %left.3) | copy-start | bytes 3145732
  4.2 10.6 %copy-start.1 = (s32[32,24]{0,1:T(8,128)S(1)}, s32[32,24]{0,1:T(8,128)}, u32[]{:S(2)}) copy-start(s32[32,24]{0,1:T(8,128)} %param.12) | copy-start | bytes 9220
  4.2 17.5 %collective-permute-start.2 = (bf16[16,1,128,128]{3,2,0,1:T(8,128)(2,1)S(1)}, bf16[16,1,128,128]{3,2,0,1:T(8,128)(2,1)S(1)}, u32[]{:S(2)}, u32[]{:S(2)}) collective-permute-start(bf16[16,1,128,128]{3,2,0,1:T(8,128)(2,1)S(1)} %bitcast.13), channel_id=1, source_target_pairs={{2,0},{0,2},{3,1},{1,3},{6,4},{4,6},{7,5},{5,7},{10,8},{8,10},{11,... | collective-permute-start | bytes 1572872 | tf_op jit(solution)/shard_map/ppermute | solution.py:215
  12.7 8.9 %collective-permute-start.1 = (bf16[8,1,128,128]{3,2,0,1:T(8,128)(2,1)S(1)}, bf16[8,1,128,128]{3,2,0,1:T(8,128)(2,1)S(1)}, u32[]{:S(2)}, u32[]{:S(2)}) collective-permute-start(bf16[8,1,128,128]{3,2,0,1:T(8,128)(2,1)S(1)} %collective-permute-done), channel_id=1, source_target_pairs={{0,4},{4,0},{8,12},{12,8},{1,5},{5,1},{9,13},{13,9},{2,6},{6,2},{1... | collective-permute-start | bytes 786440 | tf_op jit(solution)/shard_map/ppermute | solution.py:252
  21.7 9.4 %copy-start.2 = (s32[1,1,16]{2,1,0:T(1,128)S(1)}, s32[1,1,16]{2,1,0:T(1,128)}, u32[]{:S(2)}) copy-start(s32[1,1,16]{2,1,0:T(1,128)} %slot_target.1) | copy-start | bytes 196
  29.5 1.6 %collective-permute-start.3 = (bf16[8,128,128]{2,1,0:T(8,128)(2,1)S(1)}, bf16[8,128,128]{2,1,0:T(8,128)(2,1)S(1)}, u32[]{:S(2)}, u32[]{:S(2)}) collective-permute-start(bf16[8,128,128]{2,1,0:T(8,128)(2,1)S(1)} %get-tuple-element.32), channel_id=1, source_target_pairs={{0,1},{1,0},{2,3},{3,2},{4,5},{5,4},{6,7},{7,6},{8,9},{9,8},{10,11... | collective-permute-start | bytes 786440 | tf_op jit(solution)/shard_map/ppermute | solution.py:276
  31.7 6.9 %collective-permute-start.4 = (bf16[272,128]{1,0:T(8,128)(2,1)S(1)}, bf16[272,128]{1,0:T(8,128)(2,1)S(1)}, u32[]{:S(2)}, u32[]{:S(2)}) collective-permute-start(bf16[272,128]{1,0:T(8,128)(2,1)S(1)} %get-tuple-element.34), channel_id=1, source_target_pairs={{0,4},{4,8},{8,12},{12,0},{1,5},{5,9},{9,13},{13,1},{2,6},{6,10},{... | collective-permute-start | bytes 208904 | tf_op jit(solution)/shard_map/ppermute | solution.py:287
  31.8 8.9 %collective-permute-start.5 = (bf16[272,128]{1,0:T(8,128)(2,1)S(1)}, bf16[272,128]{1,0:T(8,128)(2,1)S(1)}, u32[]{:S(2)}, u32[]{:S(2)}) collective-permute-start(bf16[272,128]{1,0:T(8,128)(2,1)S(1)} %get-tuple-element.35), channel_id=1, source_target_pairs={{0,8},{4,12},{8,0},{12,4},{1,9},{5,13},{9,1},{13,5},{2,10},{6,14},... | collective-permute-start | bytes 208904 | tf_op jit(solution)/shard_map/ppermute | solution.py:287
  33.5 7.2 %collective-permute-start.6 = (bf16[272,128]{1,0:T(8,128)(2,1)S(1)}, bf16[272,128]{1,0:T(8,128)(2,1)S(1)}, u32[]{:S(2)}, u32[]{:S(2)}) collective-permute-start(bf16[272,128]{1,0:T(8,128)(2,1)S(1)} %get-tuple-element.36), channel_id=1, source_target_pairs={{0,12},{4,0},{8,4},{12,8},{1,13},{5,1},{9,5},{13,9},{2,14},{6,2},{... | collective-permute-start | bytes 208904 | tf_op jit(solution)/shard_map/ppermute | solution.py:287
  36.2 5.0 %collective-permute-start.7 = (bf16[272,128]{1,0:T(8,128)(2,1)S(1)}, bf16[272,128]{1,0:T(8,128)(2,1)S(1)}, u32[]{:S(2)}, u32[]{:S(2)}) collective-permute-start(bf16[272,128]{1,0:T(8,128)(2,1)S(1)} %get-tuple-element.33.rest_0_), channel_id=1, source_target_pairs={{0,1},{1,0},{2,3},{3,2},{4,5},{5,4},{6,7},{7,6},{8,9},{9,8},{10,11... | collective-permute-start | bytes 208904 | tf_op jit(solution)/shard_map/ppermute | solution.py:276
  38.7 2.6 %collective-permute-start.8 = (bf16[272,128]{1,0:T(8,128)(2,1)S(1)}, bf16[272,128]{1,0:T(8,128)(2,1)S(1)}, u32[]{:S(2)}, u32[]{:S(2)}) collective-permute-start(bf16[272,128]{1,0:T(8,128)(2,1)S(1)} %collective-permute-done.4.rest_1_), channel_id=1, source_target_pairs={{0,1},{1,0},{2,3},{3,2},{4,5},{5,4},{6,7},{7,6},{8,9},{9,8},{10,11... | collective-permute-start | bytes 208904 | tf_op jit(solution)/shard_map/ppermute | solution.py:276
  40.7 1.3 %collective-permute-start.9 = (bf16[272,128]{1,0:T(8,128)(2,1)S(1)}, bf16[272,128]{1,0:T(8,128)(2,1)S(1)}, u32[]{:S(2)}, u32[]{:S(2)}) collective-permute-start(bf16[272,128]{1,0:T(8,128)(2,1)S(1)} %collective-permute-done.5.rest_2_), channel_id=1, source_target_pairs={{0,1},{1,0},{2,3},{3,2},{4,5},{5,4},{6,7},{7,6},{8,9},{9,8},{10,11... | collective-permute-start | bytes 208904 | tf_op jit(solution)/shard_map/ppermute | solution.py:276
  40.7 1.4 %collective-permute-start.10 = (bf16[272,128]{1,0:T(8,128)(2,1)S(1)}, bf16[272,128]{1,0:T(8,128)(2,1)S(1)}, u32[]{:S(2)}, u32[]{:S(2)}) collective-permute-start(bf16[272,128]{1,0:T(8,128)(2,1)S(1)} %collective-permute-done.6.rest_3_), channel_id=1, source_target_pairs={{0,1},{1,0},{2,3},{3,2},{4,5},{5,4},{6,7},{7,6},{8,9},{9,8},{10,11... | collective-permute-start | bytes 208904 | tf_op jit(solution)/shard_map/ppermute | solution.py:276

commit v8 on v7

--- a/solution.py
+++ b/solution.py
@@ -127,27 +127,32 @@
     lax.fori_loop(lax.div(low, jnp.int32(GROUP)), groups, one_group, 0)
 
 
-def own_kernel(plan, slots, half, left, *totals):
+def own_kernel(plan, slots, half, left, direct, *totals):
+    shifts, quarter, left_local = direct.shape[0], direct.shape[1], direct.shape[2]
+    near = lax.rem(lax.axis_index("sector"), jnp.int32(2)) * (left.shape[0] - quarter)
     for total in totals:
         total[...] = jnp.zeros_like(total)
-    for l in range(left.shape[1]):
+    for l in range(left_local):
         accumulate(l, [(0, left.at[:, l])], plan, slots, half, totals)
 
-
-def other_kernel(rows, sets, plan, slots, half, swapped, direct, middle, *rest):
+    def one_shift(d, unused):
+        for l in range(left_local):
+            accumulate((d + 1) * left_local + l, [(near, direct.at[d, :, l])], plan, slots, half, totals)
+        return unused
+
+    lax.fori_loop(0, shifts, one_shift, 0)
+
+
+def other_kernel(rows, sets, plan, slots, half, swapped, middle, *rest):
     totals, (keep, give) = rest[sets : 2 * sets], rest[2 * sets :]
     shifts, quarter, left_local = swapped.shape[0], swapped.shape[1], swapped.shape[2]
     row, side = lax.axis_index("sector"), lax.axis_index("op")
     operators, width = slots.shape[1], totals[0].shape[1]
-    odd = lax.rem(row, jnp.int32(2))
-    near = odd * (operators - quarter)
-    far = (1 - odd) * (operators - quarter)
+    far = (1 - lax.rem(row, jnp.int32(2))) * (operators - quarter)
 
     def one_shift(d, unused):
         for l in range(left_local):
-            pieces = [
-                (near, direct.at[d, :, l]), (quarter, middle.at[d, :, l]), (far, swapped.at[d, :, l])
-            ]
+            pieces = [(quarter, middle.at[d, :, l]), (far, swapped.at[d, :, l])]
             accumulate((d + 1) * left_local + l, pieces, plan, slots, half, totals)
         return unused
 
@@ -253,23 +258,23 @@
     totals = pl.pallas_call(
         own_kernel,
         out_shape=[jax.ShapeDtypeStruct(total_shape, jnp.float32)] * sets,
-        in_specs=[smem] * 2 + [vmem] * 2,
+        in_specs=[smem] * 2 + [vmem] * 3,
         out_specs=[vmem] * sets,
         compiler_params=params,
         cost_estimate=cost(0.25),
         name="own_left",
-    )(plan, slots, half, left_ops)
+    )(plan, slots, half, left_ops, jnp.stack(direct))
     results = pl.pallas_call(
         functools.partial(other_kernel, rows, sets),
         out_shape=[jax.ShapeDtypeStruct(total_shape, jnp.float32)] * sets
         + [jax.ShapeDtypeStruct((rows * CAP // 2, width, width), kind) for kind in (jnp.float32, jnp.bfloat16)],
-        in_specs=[smem] * 2 + [vmem] * (4 + sets),
+        in_specs=[smem] * 2 + [vmem] * (3 + sets),
         out_specs=[vmem] * (sets + 2),
-        input_output_aliases={6 + j: j for j in range(sets)},
+        input_output_aliases={5 + j: j for j in range(sets)},
         compiler_params=params,
         cost_estimate=cost(0.25),
         name="other_left",
-    )(plan, slots, half, jnp.stack(swapped), jnp.stack(direct), jnp.stack(middle), *totals)
+    )(plan, slots, half, jnp.stack(swapped), jnp.stack(middle), *totals)
     keep, give = results[sets:]
 
     def over_cores(block):

time: 43.3 us -> 41.5 us (0.958); the launches traced: 43.6 us -> 41.2 us
  waiting for transfers between devices: 10.1 us -> 5.87 us
  starting transfers between devices: 10.1 us -> 11.4 us
  Pallas kernels: 23.3 us -> 23.8 us
    pallas_call x1, Pallas kernels: 3.72 us -> 7 us  [shards(): pl.pallas_call(own_kernel, out_shape=[jax.ShapeDtypeStruct(total_shape, j...]
    ppermute x2, waiting for transfers between devices: 3.21 us -> 0.01 us  [over_blocks(): lax.ppermute(part, 'blk', [((b + d) % blocks, b) for b in range(blocks)])]
    pallas_call x1, Pallas kernels: 7.81 us -> 5.09 us  [shards(): pl.pallas_call(functools.partial(other_kernel, rows, sets), out_shape=[ja...]
    ppermute x3, starting transfers between devices: 4.44 us -> 5.71 us  [shards(): lax.ppermute(partial[d], 'sector', [(i, (i + d) % rows) for i in range(ro...]
    ppermute x3, waiting for transfers between devices: 4.51 us -> 3.43 us  [shards(): lax.ppermute(partial[d], 'sector', [(i, (i + d) % rows) for i in range(ro...]
  transfers between devices with their start and end apart: 11 -> 11, of which waited for: 6 -> 5; matrix products, arithmetic and copies ran while one was open for 0% -> 0% of each run, Pallas kernels for 28% -> 38%
where the time goes in v8:
time: 41.5 us; the launch traced here: 41.2 us
  Pallas kernels  23.8 us (57%)
  starting transfers between devices  11.4 us (27%)
  waiting for transfers between devices  5.87 us (14%)
    pallas_call x1, Pallas kernels, shards(): pl.pallas_call(functools.partial(right_kernel, blocks, left_local), out_s...  8.47 us
    pallas_call x1, Pallas kernels, shards(): pl.pallas_call(own_kernel, out_shape=[jax.ShapeDtypeStruct(total_shape, j...  7 us
    ppermute x3, starting transfers between devices, shards(): lax.ppermute(partial[d], 'sector', [(i, (i + d) % rows) for i in range(ro...  5.71 us
    pallas_call x1, Pallas kernels, shards(): pl.pallas_call(functools.partial(other_kernel, rows, sets), out_shape=[ja...  5.09 us
    ppermute x3, waiting for transfers between devices, shards(): lax.ppermute(partial[d], 'sector', [(i, (i + d) % rows) for i in range(ro...  3.43 us
    ppermute x2, starting transfers between devices, over_blocks(): lax.ppermute(part, 'blk', [((b + d) % blocks, b) for b in range(blocks)])  3.1 us
    ppermute x5, waiting for transfers between devices, over_cores(): lax.ppermute(block, 'op', [(h, halves - 1 - h) for h in range(halves)])  2.43 us
    ppermute x1, starting transfers between devices, shards(): swapped = [lax.ppermute(part, 'sector', swap) for part in direct]  2.01 us
  transfers between devices with their start and end apart: 11, of which 5 were waited for; matrix products, arithmetic and copies ran while one was open for 0% of the time, Pallas kernels for 38%

profile of v8, /device:TPU:0, one launch (start us, length us, event | category | flops | bytes accessed | tf_op | source)
XLA Modules:
  0.0 41.2 jit_solution(10234495299212758352)
XLA Ops:
  0.0 1.1 %cut_left.1 = (bf16[8,1,128,128]{3,2,1,0:T(8,128)(2,1)S(1)}, bf16[16,1,128,128]{3,2,1,0:T(8,128)(2,1)S(1)}) custom-call(bf16[32,1,128,128]{3,2,1,0:T(8,128)(2,1)} %left.3), custom_call_target="tpu_custom_call" | custom-call | tf_op jit(solution)/shard_map/cut_left/pallas_call | solution.py:222
  1.1 3.0 %collective-permute-start = (bf16[8,1,128,128]{3,2,0,1:T(8,128)(2,1)S(1)}, bf16[8,1,128,128]{3,2,0,1:T(8,128)(2,1)S(1)}, u32[]{:S(2)}, u32[]{:S(2)}) collective-permute-start(bf16[8,1,128,128]{3,2,0,1:T(8,128)(2,1)S(1)} %bitcast.14), channel_id=1, source_target_pairs={{2,0},{0,2},{3,1},{1,3},{6,4},{4,6},{7,5},{5,7},{10,8},{8,10},{11,... | collective-permute-start | bytes 786440 | tf_op jit(solution)/shard_map/ppermute | solution.py:220
  4.2 0.1 collective-permute-start.2
  4.3 8.5 %right_side.1 = (bf16[6,32,2,128,256]{4,3,2,1,0:T(8,128)(2,1)S(1)}, s32[28]{0:T(128)S(1)}) custom-call(s32[24]{0:T(128)} %left_qn_in.1, s32[24]{0:T(128)} %right_qn_in.1, bf16[24,128,128]{2,1,0:T(8,128)(2,1)} %psi_in.1, bf16[32,2,128,128]{3,2,1,0:T(8,128)(2,1)} %right_in.1), custom_call_target="tpu_custom_call" | custom-call | flops 12884901888 | bytes 4194304 | tf_op jit(solution)/shard_map/right_side/pallas_call | solution.py:236
  12.7 0.0 collective-permute-done
  12.7 2.0 %collective-permute-start.1 = (bf16[8,1,128,128]{3,2,0,1:T(8,128)(2,1)S(1)}, bf16[8,1,128,128]{3,2,0,1:T(8,128)(2,1)S(1)}, u32[]{:S(2)}, u32[]{:S(2)}) collective-permute-start(bf16[8,1,128,128]{3,2,0,1:T(8,128)(2,1)S(1)} %collective-permute-done), channel_id=1, source_target_pairs={{0,4},{4,0},{8,12},{12,8},{1,5},{5,1},{9,13},{13,9},{2,6},{6,2},{1... | collective-permute-start | bytes 786440 | tf_op jit(solution)/shard_map/ppermute | solution.py:257
  14.8 0.0 copy-done
  14.8 0.0 copy-done.1
  14.8 7.0 %own_left.1 = (f32[17,128,128]{2,1,0:T(8,128)S(1)}, f32[17,128,128]{2,1,0:T(8,128)S(1)}, f32[17,128,128]{2,1,0:T(8,128)S(1)}, f32[17,128,128]{2,1,0:T(8,128)S(1)}) custom-call(s32[28]{0:T(128)S(1)} %get-tuple-element.21.plan, s32[24,32]{1,0:T(8,128)S(1)} %bitcast.11, bf16[6,32,2,128,256]{4,3,2,1,0:T(8,128)(2,1)S(1)} %get-tuple-element.24.half, ...), custom_call_target="tpu_custom_call" | custom-call | flops 6442450944 | bytes 4194304 | tf_op jit(solution)/shard_map/own_left/pallas_call | solution.py:258
  21.8 0.0 collective-permute-done.2
  21.8 0.0 collective-permute-done.1
  21.8 0.0 copy-start.2
  21.8 5.1 %other_left.1 = (f32[17,128,128]{2,1,0:T(8,128)S(1)}, f32[17,128,128]{2,1,0:T(8,128)S(1)}, f32[17,128,128]{2,1,0:T(8,128)S(1)}, f32[17,128,128]{2,1,0:T(8,128)S(...) custom-call(s32[28]{0:T(128)S(1)} %get-tuple-element.21.plan, ...), custom_call_target="tpu_custom_call", output_to_operand_aliasing={{0}: (5, {}), {1}: (6, {}), {2}: (7, {}), {3}: (8, {})} | custom-call | flops 6442450944 | bytes 4194304 | tf_op jit(solution)/shard_map/other_left/pallas_call | solution.py:267
  26.9 0.1 collective-permute-start.3
  27.0 1.5 %collective-permute-done.3.taken = bf16[8,128,128]{2,1,0:T(8,128)(2,1)S(1)} collective-permute-done((bf16[8,128,128]{2,1,0:T(8,128)(2,1)S(1)}, bf16[8,128,128]{2,1,0:T(8,128)(2,1)S(1)}, u32[]{:S(2)}, u32[]{:S(2)}) %collective-permute-start.3) | collective-permute-done | bytes 262176 | tf_op jit(solution)/shard_map/ppermute | solution.py:281
  28.5 0.0 copy-done.2
  28.5 0.6 %combine.1 = (bf16[272,128]{1,0:T(8,128)(2,1)S(1)}, bf16[272,128]{1,0:T(8,128)(2,1)S(1)}, bf16[272,128]{1,0:T(8,128)(2,1)S(1)}, bf16[272,128]{1,0:T(8,128)(2,1)S(1)}) custom-call(s32[1,1,16]{2,1,0:T(1,128)S(1)} %copy-done.2, f32[8,128,128]{2,1,0:T(8,128)S(1)} %get-tuple-element.31.keep, bf16[8,128,128]{2,1,0:T(8,128)(2,1)S(1)} %collective-permute-done.3.taken), custom_call_target="tpu_custom_call" | custom-call | tf_op jit(solution)/shard_map/combine/pallas_call | solution.py:283
  29.1 1.8 %collective-permute-start.4 = (bf16[272,128]{1,0:T(8,128)(2,1)S(1)}, bf16[272,128]{1,0:T(8,128)(2,1)S(1)}, u32[]{:S(2)}, u32[]{:S(2)}) collective-permute-start(bf16[272,128]{1,0:T(8,128)(2,1)S(1)} %get-tuple-element.34), channel_id=1, source_target_pairs={{0,4},{4,8},{8,12},{12,0},{1,5},{5,9},{9,13},{13,1},{2,6},{6,10},{... | collective-permute-start | bytes 208904 | tf_op jit(solution)/shard_map/ppermute | solution.py:292
  30.9 1.1 %collective-permute-start.5 = (bf16[272,128]{1,0:T(8,128)(2,1)S(1)}, bf16[272,128]{1,0:T(8,128)(2,1)S(1)}, u32[]{:S(2)}, u32[]{:S(2)}) collective-permute-start(bf16[272,128]{1,0:T(8,128)(2,1)S(1)} %get-tuple-element.35), channel_id=1, source_target_pairs={{0,8},{4,12},{8,0},{12,4},{1,9},{5,13},{9,1},{13,5},{2,10},{6,14},... | collective-permute-start | bytes 208904 | tf_op jit(solution)/shard_map/ppermute | solution.py:292
  32.0 2.8 %collective-permute-start.6 = (bf16[272,128]{1,0:T(8,128)(2,1)S(1)}, bf16[272,128]{1,0:T(8,128)(2,1)S(1)}, u32[]{:S(2)}, u32[]{:S(2)}) collective-permute-start(bf16[272,128]{1,0:T(8,128)(2,1)S(1)} %get-tuple-element.36), channel_id=1, source_target_pairs={{0,12},{4,0},{8,4},{12,8},{1,13},{5,1},{9,5},{13,9},{2,14},{6,2},{... | collective-permute-start | bytes 208904 | tf_op jit(solution)/shard_map/ppermute | solution.py:292
  34.8 0.0 collective-permute-start.7
  34.8 0.6 %collective-permute-done.4.rest_1_ = bf16[272,128]{1,0:T(8,128)(2,1)S(1)} collective-permute-done((bf16[272,128]{1,0:T(8,128)(2,1)S(1)}, bf16[272,128]{1,0:T(8,128)(2,1)S(1)}, u32[]{:S(2)}, u32[]{:S(2)}) %collective-permute-start.4) | collective-permute-done | bytes 69664 | tf_op jit(solution)/shard_map/ppermute | solution.py:292
  35.4 0.0 collective-permute-start.8
  35.4 2.9 %collective-permute-done.5.rest_2_ = bf16[272,128]{1,0:T(8,128)(2,1)S(1)} collective-permute-done((bf16[272,128]{1,0:T(8,128)(2,1)S(1)}, bf16[272,128]{1,0:T(8,128)(2,1)S(1)}, u32[]{:S(2)}, u32[]{:S(2)}) %collective-permute-start.5) | collective-permute-done | bytes 69664 | tf_op jit(solution)/shard_map/ppermute | solution.py:292
  38.3 0.0 collective-permute-start.9
  38.3 0.0 collective-permute-done.6.rest_3_
  38.3 0.5 %collective-permute-start.10 = (bf16[272,128]{1,0:T(8,128)(2,1)S(1)}, bf16[272,128]{1,0:T(8,128)(2,1)S(1)}, u32[]{:S(2)}, u32[]{:S(2)}) collective-permute-start(bf16[272,128]{1,0:T(8,128)(2,1)S(1)} %collective-permute-done.6.rest_3_), channel_id=1, source_target_pairs={{0,1},{1,0},{2,3},{3,2},{4,5},{5,4},{6,7},{7,6},{8,9},{9,8},{10,11... | collective-permute-start | bytes 208904 | tf_op jit(solution)/shard_map/ppermute | solution.py:281
  38.8 0.0 collective-permute-done.7.rest_4_
  38.8 0.0 collective-permute-done.8.rest_5_
  38.8 0.7 %collective-permute-done.9.rest_6_ = bf16[272,128]{1,0:T(8,128)(2,1)S(1)} collective-permute-done((bf16[272,128]{1,0:T(8,128)(2,1)S(1)}, bf16[272,128]{1,0:T(8,128)(2,1)S(1)}, u32[]{:S(2)}, u32[]{:S(2)}) %collective-permute-start.9) | collective-permute-done | bytes 69664 | tf_op jit(solution)/shard_map/ppermute | solution.py:281
  39.5 0.2 collective-permute-done.10.rest_7_
  39.7 1.5 %assemble.1 = f32[24,128,128]{2,1,0:T(8,128)} custom-call(bf16[272,128]{1,0:T(8,128)(2,1)S(1)} %get-tuple-element.33.rest_0_, bf16[272,128]{1,0:T(8,128)(2,1)S(1)} %collective-permute-done.4.rest_1_, bf16[272,128]{1,0:T(8,128)(2,1)S(1)} %collective-permute-done.5.rest_2_, bf16[272,128]{1,0:T(8,128)(2,1)S(1)} %collective-permute-done.6.rest_3_, ...), custom_call_target="tpu_custom_call" | custom-call | tf_op jit(solution)/shard_map/assemble/pallas_call | solution.py:296
  (2 shorter events, 0.0 us)
Async XLA Ops:
  1.1 11.6 %collective-permute-start = (bf16[8,1,128,128]{3,2,0,1:T(8,128)(2,1)S(1)}, bf16[8,1,128,128]{3,2,0,1:T(8,128)(2,1)S(1)}, u32[]{:S(2)}, u32[]{:S(2)}) collective-permute-start(bf16[8,1,128,128]{3,2,0,1:T(8,128)(2,1)S(1)} %bitcast.14), channel_id=1, source_target_pairs={{2,0},{0,2},{3,1},{1,3},{6,4},{4,6},{7,5},{5,7},{10,8},{8,10},{11,... | collective-permute-start | bytes 786440 | tf_op jit(solution)/shard_map/ppermute | solution.py:220
  4.2 10.6 %copy-start = (bf16[32,1,128,128]{3,2,1,0:T(8,128)(2,1)S(1)}, bf16[32,1,128,128]{3,2,1,0:T(8,128)(2,1)}, u32[]{:S(2)}) copy-start(bf16[32,1,128,128]{3,2,1,0:T(8,128)(2,1)} %left.3) | copy-start | bytes 3145732
  4.2 10.6 %copy-start.1 = (s32[32,24]{0,1:T(8,128)S(1)}, s32[32,24]{0,1:T(8,128)}, u32[]{:S(2)}) copy-start(s32[32,24]{0,1:T(8,128)} %param.12) | copy-start | bytes 9220
  4.2 17.6 %collective-permute-start.2 = (bf16[16,1,128,128]{3,2,0,1:T(8,128)(2,1)S(1)}, bf16[16,1,128,128]{3,2,0,1:T(8,128)(2,1)S(1)}, u32[]{:S(2)}, u32[]{:S(2)}) collective-permute-start(bf16[16,1,128,128]{3,2,0,1:T(8,128)(2,1)S(1)} %bitcast.13), channel_id=1, source_target_pairs={{2,0},{0,2},{3,1},{1,3},{6,4},{4,6},{7,5},{5,7},{10,8},{8,10},{11,... | collective-permute-start | bytes 1572872 | tf_op jit(solution)/shard_map/ppermute | solution.py:220
  12.7 9.0 %collective-permute-start.1 = (bf16[8,1,128,128]{3,2,0,1:T(8,128)(2,1)S(1)}, bf16[8,1,128,128]{3,2,0,1:T(8,128)(2,1)S(1)}, u32[]{:S(2)}, u32[]{:S(2)}) collective-permute-start(bf16[8,1,128,128]{3,2,0,1:T(8,128)(2,1)S(1)} %collective-permute-done), channel_id=1, source_target_pairs={{0,4},{4,0},{8,12},{12,8},{1,5},{5,1},{9,13},{13,9},{2,6},{6,2},{1... | collective-permute-start | bytes 786440 | tf_op jit(solution)/shard_map/ppermute | solution.py:257
  21.8 6.7 %copy-start.2 = (s32[1,1,16]{2,1,0:T(1,128)S(1)}, s32[1,1,16]{2,1,0:T(1,128)}, u32[]{:S(2)}) copy-start(s32[1,1,16]{2,1,0:T(1,128)} %slot_target.1) | copy-start | bytes 196
  26.9 1.6 %collective-permute-start.3 = (bf16[8,128,128]{2,1,0:T(8,128)(2,1)S(1)}, bf16[8,128,128]{2,1,0:T(8,128)(2,1)S(1)}, u32[]{:S(2)}, u32[]{:S(2)}) collective-permute-start(bf16[8,128,128]{2,1,0:T(8,128)(2,1)S(1)} %get-tuple-element.32), channel_id=1, source_target_pairs={{0,1},{1,0},{2,3},{3,2},{4,5},{5,4},{6,7},{7,6},{8,9},{9,8},{10,11... | collective-permute-start | bytes 786440 | tf_op jit(solution)/shard_map/ppermute | solution.py:281
  29.1 6.3 %collective-permute-start.4 = (bf16[272,128]{1,0:T(8,128)(2,1)S(1)}, bf16[272,128]{1,0:T(8,128)(2,1)S(1)}, u32[]{:S(2)}, u32[]{:S(2)}) collective-permute-start(bf16[272,128]{1,0:T(8,128)(2,1)S(1)} %get-tuple-element.34), channel_id=1, source_target_pairs={{0,4},{4,8},{8,12},{12,0},{1,5},{5,9},{9,13},{13,1},{2,6},{6,10},{... | collective-permute-start | bytes 208904 | tf_op jit(solution)/shard_map/ppermute | solution.py:292
  30.9 7.4 %collective-permute-start.5 = (bf16[272,128]{1,0:T(8,128)(2,1)S(1)}, bf16[272,128]{1,0:T(8,128)(2,1)S(1)}, u32[]{:S(2)}, u32[]{:S(2)}) collective-permute-start(bf16[272,128]{1,0:T(8,128)(2,1)S(1)} %get-tuple-element.35), channel_id=1, source_target_pairs={{0,8},{4,12},{8,0},{12,4},{1,9},{5,13},{9,1},{13,5},{2,10},{6,14},... | collective-permute-start | bytes 208904 | tf_op jit(solution)/shard_map/ppermute | solution.py:292
  32.0 6.3 %collective-permute-start.6 = (bf16[272,128]{1,0:T(8,128)(2,1)S(1)}, bf16[272,128]{1,0:T(8,128)(2,1)S(1)}, u32[]{:S(2)}, u32[]{:S(2)}) collective-permute-start(bf16[272,128]{1,0:T(8,128)(2,1)S(1)} %get-tuple-element.36), channel_id=1, source_target_pairs={{0,12},{4,0},{8,4},{12,8},{1,13},{5,1},{9,5},{13,9},{2,14},{6,2},{... | collective-permute-start | bytes 208904 | tf_op jit(solution)/shard_map/ppermute | solution.py:292
  34.8 4.0 %collective-permute-start.7 = (bf16[272,128]{1,0:T(8,128)(2,1)S(1)}, bf16[272,128]{1,0:T(8,128)(2,1)S(1)}, u32[]{:S(2)}, u32[]{:S(2)}) collective-permute-start(bf16[272,128]{1,0:T(8,128)(2,1)S(1)} %get-tuple-element.33.rest_0_), channel_id=1, source_target_pairs={{0,1},{1,0},{2,3},{3,2},{4,5},{5,4},{6,7},{7,6},{8,9},{9,8},{10,11... | collective-permute-start | bytes 208904 | tf_op jit(solution)/shard_map/ppermute | solution.py:281
  35.4 3.4 %collective-permute-start.8 = (bf16[272,128]{1,0:T(8,128)(2,1)S(1)}, bf16[272,128]{1,0:T(8,128)(2,1)S(1)}, u32[]{:S(2)}, u32[]{:S(2)}) collective-permute-start(bf16[272,128]{1,0:T(8,128)(2,1)S(1)} %collective-permute-done.4.rest_1_), channel_id=1, source_target_pairs={{0,1},{1,0},{2,3},{3,2},{4,5},{5,4},{6,7},{7,6},{8,9},{9,8},{10,11... | collective-permute-start | bytes 208904 | tf_op jit(solution)/shard_map/ppermute | solution.py:281
  38.3 1.3 %collective-permute-start.9 = (bf16[272,128]{1,0:T(8,128)(2,1)S(1)}, bf16[272,128]{1,0:T(8,128)(2,1)S(1)}, u32[]{:S(2)}, u32[]{:S(2)}) collective-permute-start(bf16[272,128]{1,0:T(8,128)(2,1)S(1)} %collective-permute-done.5.rest_2_), channel_id=1, source_target_pairs={{0,1},{1,0},{2,3},{3,2},{4,5},{5,4},{6,7},{7,6},{8,9},{9,8},{10,11... | collective-permute-start | bytes 208904 | tf_op jit(solution)/shard_map/ppermute | solution.py:281
  38.3 1.4 %collective-permute-start.10 = (bf16[272,128]{1,0:T(8,128)(2,1)S(1)}, bf16[272,128]{1,0:T(8,128)(2,1)S(1)}, u32[]{:S(2)}, u32[]{:S(2)}) collective-permute-start(bf16[272,128]{1,0:T(8,128)(2,1)S(1)} %collective-permute-done.6.rest_3_), channel_id=1, source_target_pairs={{0,1},{1,0},{2,3},{3,2},{4,5},{5,4},{6,7},{7,6},{8,9},{9,8},{10,11... | collective-permute-start | bytes 208904 | tf_op jit(solution)/shard_map/ppermute | solution.py:281

commit v9 on v8

--- a/solution.py
+++ b/solution.py
@@ -100,8 +100,8 @@
     low, high = plan[sectors + 1 + code], plan[sectors + 2 + code]
     zero = jnp.zeros((width, width), jnp.bfloat16)
 
-    def one_group(g, unused):
-        places = [g * GROUP + j for j in range(GROUP)]
+    def terms(g, count):
+        places = [g * GROUP + j for j in range(count * GROUP)]
         members = [plan[at] for at in places]
         counts = [(low <= at) & (at < high) for at in places]
         for first, left in pieces:
@@ -112,19 +112,30 @@
                     [jnp.concatenate([block, zero], axis=1), jnp.concatenate([zero, block], axis=1)], axis=0
                 )
                 term = lax.dot_general(
-                    half[g, k].reshape(GROUP // 2 * width, 2 * width),
+                    half[pl.ds(g, count), k].reshape(count * GROUP // 2 * width, 2 * width),
                     weights,
                     NT,
                     preferred_element_type=jnp.float32,
                 )
-                for j in range(GROUP):
+                for j in range(count * GROUP):
                     p, e = j // 2, j % 2
                     slot = jnp.where(counts[j], slots[members[j], k], spare)
-                    totals[j % len(totals)][slot] += term[p * width : (p + 1) * width, e * width : (e + 1) * width]
-        return unused
-
-    groups = jnp.where(low < high, lax.div(high + GROUP - 1, jnp.int32(GROUP)), 0)
-    lax.fori_loop(lax.div(low, jnp.int32(GROUP)), groups, one_group, 0)
+                    totals[j % len(totals)][slot] += term[
+                        p * width : (p + 1) * width, e * width : (e + 1) * width
+                    ]
+
+    def two_groups(i, unused):
+        terms(start + 2 * i, 2)
+        return unused
+
+    def last_group(i, unused):
+        terms(start + groups - 1, 1)
+        return unused
+
+    start = lax.div(low, jnp.int32(GROUP))
+    groups = jnp.where(low < high, lax.div(high + GROUP - 1, jnp.int32(GROUP)) - start, 0)
+    lax.fori_loop(0, lax.div(groups, 2), two_groups, 0)
+    lax.fori_loop(0, lax.rem(groups, 2), last_group, 0)
 
 
 def own_kernel(plan, slots, half, left, direct, *totals):

time: 41.5 us -> 42.1 us (1.014); the launches traced: 41.2 us -> 41.3 us
  Pallas kernels: 23.8 us -> 23.3 us
  waiting for transfers between devices: 5.87 us -> 6.37 us
    pallas_call x1, Pallas kernels: 5.09 us -> 4 us  [shards(): pl.pallas_call(functools.partial(other_kernel, rows, sets), out_shape=[ja...]
    pallas_call x1, Pallas kernels: 7 us -> 7.55 us  [shards(): pl.pallas_call(own_kernel, out_shape=[jax.ShapeDtypeStruct(total_shape, j...]
  transfers between devices with their start and end apart: 11 -> 11, of which waited for: 5 -> 6; matrix products, arithmetic and copies ran while one was open for 0% -> 0% of each run, Pallas kernels for 38% -> 39%
where the time goes in v9:
time: 42.1 us; the launch traced here: 41.3 us
  Pallas kernels  23.3 us (55%)
  starting transfers between devices  11.6 us (28%)
  waiting for transfers between devices  6.37 us (15%)
    pallas_call x1, Pallas kernels, shards(): pl.pallas_call(functools.partial(right_kernel, blocks, left_local), out_s...  8.47 us
    pallas_call x1, Pallas kernels, shards(): pl.pallas_call(own_kernel, out_shape=[jax.ShapeDtypeStruct(total_shape, j...  7.55 us
    ppermute x3, starting transfers between devices, shards(): lax.ppermute(partial[d], 'sector', [(i, (i + d) % rows) for i in range(ro...  6.13 us
    pallas_call x1, Pallas kernels, shards(): pl.pallas_call(functools.partial(other_kernel, rows, sets), out_shape=[ja...  4 us
    ppermute x3, waiting for transfers between devices, shards(): lax.ppermute(partial[d], 'sector', [(i, (i + d) % rows) for i in range(ro...  3.85 us
    ppermute x2, starting transfers between devices, over_blocks(): lax.ppermute(part, 'blk', [((b + d) % blocks, b) for b in range(blocks)])  3.1 us
    ppermute x5, waiting for transfers between devices, over_cores(): lax.ppermute(block, 'op', [(h, halves - 1 - h) for h in range(halves)])  2.51 us
    ppermute x1, starting transfers between devices, shards(): swapped = [lax.ppermute(part, 'sector', swap) for part in direct]  2.01 us
  transfers between devices with their start and end apart: 11, of which 6 were waited for; matrix products, arithmetic and copies ran while one was open for 0% of the time, Pallas kernels for 39%

profile of v9, /device:TPU:0, one launch (start us, length us, event | category | flops | bytes accessed | tf_op | source)
XLA Modules:
  0.0 41.3 jit_solution(5784265726842041109)
XLA Ops:
  0.0 1.1 %cut_left.1 = (bf16[8,1,128,128]{3,2,1,0:T(8,128)(2,1)S(1)}, bf16[16,1,128,128]{3,2,1,0:T(8,128)(2,1)S(1)}) custom-call(bf16[32,1,128,128]{3,2,1,0:T(8,128)(2,1)} %left.3), custom_call_target="tpu_custom_call" | custom-call | tf_op jit(solution)/shard_map/cut_left/pallas_call | solution.py:233
  1.1 3.0 %collective-permute-start = (bf16[8,1,128,128]{3,2,0,1:T(8,128)(2,1)S(1)}, bf16[8,1,128,128]{3,2,0,1:T(8,128)(2,1)S(1)}, u32[]{:S(2)}, u32[]{:S(2)}) collective-permute-start(bf16[8,1,128,128]{3,2,0,1:T(8,128)(2,1)S(1)} %bitcast.14), channel_id=1, source_target_pairs={{2,0},{0,2},{3,1},{1,3},{6,4},{4,6},{7,5},{5,7},{10,8},{8,10},{11,... | collective-permute-start | bytes 786440 | tf_op jit(solution)/shard_map/ppermute | solution.py:231
  4.2 0.1 collective-permute-start.2
  4.3 8.5 %right_side.1 = (bf16[6,32,2,128,256]{4,3,2,1,0:T(8,128)(2,1)S(1)}, s32[28]{0:T(128)S(1)}) custom-call(s32[24]{0:T(128)} %left_qn_in.1, s32[24]{0:T(128)} %right_qn_in.1, bf16[24,128,128]{2,1,0:T(8,128)(2,1)} %psi_in.1, bf16[32,2,128,128]{3,2,1,0:T(8,128)(2,1)} %right_in.1), custom_call_target="tpu_custom_call" | custom-call | flops 12884901888 | bytes 4194304 | tf_op jit(solution)/shard_map/right_side/pallas_call | solution.py:247
  12.7 0.0 collective-permute-done
  12.7 2.0 %collective-permute-start.1 = (bf16[8,1,128,128]{3,2,0,1:T(8,128)(2,1)S(1)}, bf16[8,1,128,128]{3,2,0,1:T(8,128)(2,1)S(1)}, u32[]{:S(2)}, u32[]{:S(2)}) collective-permute-start(bf16[8,1,128,128]{3,2,0,1:T(8,128)(2,1)S(1)} %collective-permute-done), channel_id=1, source_target_pairs={{0,4},{4,0},{8,12},{12,8},{1,5},{5,1},{9,13},{13,9},{2,6},{6,2},{1... | collective-permute-start | bytes 786440 | tf_op jit(solution)/shard_map/ppermute | solution.py:268
  14.8 0.0 copy-done
  14.8 0.0 copy-done.1
  14.8 7.6 %own_left.1 = (f32[17,128,128]{2,1,0:T(8,128)S(1)}, f32[17,128,128]{2,1,0:T(8,128)S(1)}, f32[17,128,128]{2,1,0:T(8,128)S(1)}, f32[17,128,128]{2,1,0:T(8,128)S(1)}) custom-call(s32[28]{0:T(128)S(1)} %get-tuple-element.21.plan, s32[24,32]{1,0:T(8,128)S(1)} %bitcast.11, bf16[6,32,2,128,256]{4,3,2,1,0:T(8,128)(2,1)S(1)} %get-tuple-element.24.half, ...), custom_call_target="tpu_custom_call" | custom-call | flops 6442450944 | bytes 4194304 | tf_op jit(solution)/shard_map/own_left/pallas_call | solution.py:269
  22.3 0.0 collective-permute-done.2
  22.3 0.0 collective-permute-done.1
  22.3 0.0 copy-start.2
  22.4 4.0 %other_left.1 = (f32[17,128,128]{2,1,0:T(8,128)S(1)}, f32[17,128,128]{2,1,0:T(8,128)S(1)}, f32[17,128,128]{2,1,0:T(8,128)S(1)}, f32[17,128,128]{2,1,0:T(8,128)S(...) custom-call(s32[28]{0:T(128)S(1)} %get-tuple-element.21.plan, ...), custom_call_target="tpu_custom_call", output_to_operand_aliasing={{0}: (5, {}), {1}: (6, {}), {2}: (7, {}), {3}: (8, {})} | custom-call | flops 6442450944 | bytes 4194304 | tf_op jit(solution)/shard_map/other_left/pallas_call | solution.py:278
  26.4 0.1 collective-permute-start.3
  26.4 1.5 %collective-permute-done.3.taken = bf16[8,128,128]{2,1,0:T(8,128)(2,1)S(1)} collective-permute-done((bf16[8,128,128]{2,1,0:T(8,128)(2,1)S(1)}, bf16[8,128,128]{2,1,0:T(8,128)(2,1)S(1)}, u32[]{:S(2)}, u32[]{:S(2)}) %collective-permute-start.3) | collective-permute-done | bytes 262176 | tf_op jit(solution)/shard_map/ppermute | solution.py:292
  28.0 0.0 copy-done.2
  28.0 0.6 %combine.1 = (bf16[272,128]{1,0:T(8,128)(2,1)S(1)}, bf16[272,128]{1,0:T(8,128)(2,1)S(1)}, bf16[272,128]{1,0:T(8,128)(2,1)S(1)}, bf16[272,128]{1,0:T(8,128)(2,1)S(1)}) custom-call(s32[1,1,16]{2,1,0:T(1,128)S(1)} %copy-done.2, f32[8,128,128]{2,1,0:T(8,128)S(1)} %get-tuple-element.31.keep, bf16[8,128,128]{2,1,0:T(8,128)(2,1)S(1)} %collective-permute-done.3.taken), custom_call_target="tpu_custom_call" | custom-call | tf_op jit(solution)/shard_map/combine/pallas_call | solution.py:294
  28.6 1.2 %collective-permute-start.4 = (bf16[272,128]{1,0:T(8,128)(2,1)S(1)}, bf16[272,128]{1,0:T(8,128)(2,1)S(1)}, u32[]{:S(2)}, u32[]{:S(2)}) collective-permute-start(bf16[272,128]{1,0:T(8,128)(2,1)S(1)} %get-tuple-element.34), channel_id=1, source_target_pairs={{0,4},{4,8},{8,12},{12,0},{1,5},{5,9},{9,13},{13,1},{2,6},{6,10},{... | collective-permute-start | bytes 208904 | tf_op jit(solution)/shard_map/ppermute | solution.py:303
  29.8 3.5 %collective-permute-start.5 = (bf16[272,128]{1,0:T(8,128)(2,1)S(1)}, bf16[272,128]{1,0:T(8,128)(2,1)S(1)}, u32[]{:S(2)}, u32[]{:S(2)}) collective-permute-start(bf16[272,128]{1,0:T(8,128)(2,1)S(1)} %get-tuple-element.35), channel_id=1, source_target_pairs={{0,8},{4,12},{8,0},{12,4},{1,9},{5,13},{9,1},{13,5},{2,10},{6,14},... | collective-permute-start | bytes 208904 | tf_op jit(solution)/shard_map/ppermute | solution.py:303
  33.3 1.4 %collective-permute-start.6 = (bf16[272,128]{1,0:T(8,128)(2,1)S(1)}, bf16[272,128]{1,0:T(8,128)(2,1)S(1)}, u32[]{:S(2)}, u32[]{:S(2)}) collective-permute-start(bf16[272,128]{1,0:T(8,128)(2,1)S(1)} %get-tuple-element.36), channel_id=1, source_target_pairs={{0,12},{4,0},{8,4},{12,8},{1,13},{5,1},{9,5},{13,9},{2,14},{6,2},{... | collective-permute-start | bytes 208904 | tf_op jit(solution)/shard_map/ppermute | solution.py:303
  34.7 0.0 collective-permute-start.7
  34.7 0.8 %collective-permute-done.4.rest_1_ = bf16[272,128]{1,0:T(8,128)(2,1)S(1)} collective-permute-done((bf16[272,128]{1,0:T(8,128)(2,1)S(1)}, bf16[272,128]{1,0:T(8,128)(2,1)S(1)}, u32[]{:S(2)}, u32[]{:S(2)}) %collective-permute-start.4) | collective-permute-done | bytes 69664 | tf_op jit(solution)/shard_map/ppermute | solution.py:303
  35.5 0.0 collective-permute-start.8
  35.5 2.8 %collective-permute-done.5.rest_2_ = bf16[272,128]{1,0:T(8,128)(2,1)S(1)} collective-permute-done((bf16[272,128]{1,0:T(8,128)(2,1)S(1)}, bf16[272,128]{1,0:T(8,128)(2,1)S(1)}, u32[]{:S(2)}, u32[]{:S(2)}) %collective-permute-start.5) | collective-permute-done | bytes 69664 | tf_op jit(solution)/shard_map/ppermute | solution.py:303
  38.3 0.0 collective-permute-start.9
  38.3 0.2 collective-permute-done.6.rest_3_
  38.6 0.3 collective-permute-start.10
  38.8 0.0 collective-permute-done.7.rest_4_
  38.8 0.0 collective-permute-done.8.rest_5_
  38.8 0.7 %collective-permute-done.9.rest_6_ = bf16[272,128]{1,0:T(8,128)(2,1)S(1)} collective-permute-done((bf16[272,128]{1,0:T(8,128)(2,1)S(1)}, bf16[272,128]{1,0:T(8,128)(2,1)S(1)}, u32[]{:S(2)}, u32[]{:S(2)}) %collective-permute-start.9) | collective-permute-done | bytes 69664 | tf_op jit(solution)/shard_map/ppermute | solution.py:292
  39.6 0.2 collective-permute-done.10.rest_7_
  39.8 1.5 %assemble.1 = f32[24,128,128]{2,1,0:T(8,128)} custom-call(bf16[272,128]{1,0:T(8,128)(2,1)S(1)} %get-tuple-element.33.rest_0_, bf16[272,128]{1,0:T(8,128)(2,1)S(1)} %collective-permute-done.4.rest_1_, bf16[272,128]{1,0:T(8,128)(2,1)S(1)} %collective-permute-done.5.rest_2_, bf16[272,128]{1,0:T(8,128)(2,1)S(1)} %collective-permute-done.6.rest_3_, ...), custom_call_target="tpu_custom_call" | custom-call | tf_op jit(solution)/shard_map/assemble/pallas_call | solution.py:307
  (2 shorter events, 0.0 us)
Async XLA Ops:
  1.1 11.6 %collective-permute-start = (bf16[8,1,128,128]{3,2,0,1:T(8,128)(2,1)S(1)}, bf16[8,1,128,128]{3,2,0,1:T(8,128)(2,1)S(1)}, u32[]{:S(2)}, u32[]{:S(2)}) collective-permute-start(bf16[8,1,128,128]{3,2,0,1:T(8,128)(2,1)S(1)} %bitcast.14), channel_id=1, source_target_pairs={{2,0},{0,2},{3,1},{1,3},{6,4},{4,6},{7,5},{5,7},{10,8},{8,10},{11,... | collective-permute-start | bytes 786440 | tf_op jit(solution)/shard_map/ppermute | solution.py:231
  4.2 10.6 %copy-start = (bf16[32,1,128,128]{3,2,1,0:T(8,128)(2,1)S(1)}, bf16[32,1,128,128]{3,2,1,0:T(8,128)(2,1)}, u32[]{:S(2)}) copy-start(bf16[32,1,128,128]{3,2,1,0:T(8,128)(2,1)} %left.3) | copy-start | bytes 3145732
  4.2 10.6 %copy-start.1 = (s32[32,24]{0,1:T(8,128)S(1)}, s32[32,24]{0,1:T(8,128)}, u32[]{:S(2)}) copy-start(s32[32,24]{0,1:T(8,128)} %param.12) | copy-start | bytes 9220
  4.2 18.2 %collective-permute-start.2 = (bf16[16,1,128,128]{3,2,0,1:T(8,128)(2,1)S(1)}, bf16[16,1,128,128]{3,2,0,1:T(8,128)(2,1)S(1)}, u32[]{:S(2)}, u32[]{:S(2)}) collective-permute-start(bf16[16,1,128,128]{3,2,0,1:T(8,128)(2,1)S(1)} %bitcast.13), channel_id=1, source_target_pairs={{2,0},{0,2},{3,1},{1,3},{6,4},{4,6},{7,5},{5,7},{10,8},{8,10},{11,... | collective-permute-start | bytes 1572872 | tf_op jit(solution)/shard_map/ppermute | solution.py:231
  12.7 9.6 %collective-permute-start.1 = (bf16[8,1,128,128]{3,2,0,1:T(8,128)(2,1)S(1)}, bf16[8,1,128,128]{3,2,0,1:T(8,128)(2,1)S(1)}, u32[]{:S(2)}, u32[]{:S(2)}) collective-permute-start(bf16[8,1,128,128]{3,2,0,1:T(8,128)(2,1)S(1)} %collective-permute-done), channel_id=1, source_target_pairs={{0,4},{4,0},{8,12},{12,8},{1,5},{5,1},{9,13},{13,9},{2,6},{6,2},{1... | collective-permute-start | bytes 786440 | tf_op jit(solution)/shard_map/ppermute | solution.py:268
  22.3 5.6 %copy-start.2 = (s32[1,1,16]{2,1,0:T(1,128)S(1)}, s32[1,1,16]{2,1,0:T(1,128)}, u32[]{:S(2)}) copy-start(s32[1,1,16]{2,1,0:T(1,128)} %slot_target.1) | copy-start | bytes 196
  26.4 1.6 %collective-permute-start.3 = (bf16[8,128,128]{2,1,0:T(8,128)(2,1)S(1)}, bf16[8,128,128]{2,1,0:T(8,128)(2,1)S(1)}, u32[]{:S(2)}, u32[]{:S(2)}) collective-permute-start(bf16[8,128,128]{2,1,0:T(8,128)(2,1)S(1)} %get-tuple-element.32), channel_id=1, source_target_pairs={{0,1},{1,0},{2,3},{3,2},{4,5},{5,4},{6,7},{7,6},{8,9},{9,8},{10,11... | collective-permute-start | bytes 786440 | tf_op jit(solution)/shard_map/ppermute | solution.py:292
  28.6 6.9 %collective-permute-start.4 = (bf16[272,128]{1,0:T(8,128)(2,1)S(1)}, bf16[272,128]{1,0:T(8,128)(2,1)S(1)}, u32[]{:S(2)}, u32[]{:S(2)}) collective-permute-start(bf16[272,128]{1,0:T(8,128)(2,1)S(1)} %get-tuple-element.34), channel_id=1, source_target_pairs={{0,4},{4,8},{8,12},{12,0},{1,5},{5,9},{9,13},{13,1},{2,6},{6,10},{... | collective-permute-start | bytes 208904 | tf_op jit(solution)/shard_map/ppermute | solution.py:303
  29.8 8.5 %collective-permute-start.5 = (bf16[272,128]{1,0:T(8,128)(2,1)S(1)}, bf16[272,128]{1,0:T(8,128)(2,1)S(1)}, u32[]{:S(2)}, u32[]{:S(2)}) collective-permute-start(bf16[272,128]{1,0:T(8,128)(2,1)S(1)} %get-tuple-element.35), channel_id=1, source_target_pairs={{0,8},{4,12},{8,0},{12,4},{1,9},{5,13},{9,1},{13,5},{2,10},{6,14},... | collective-permute-start | bytes 208904 | tf_op jit(solution)/shard_map/ppermute | solution.py:303
  33.3 5.2 %collective-permute-start.6 = (bf16[272,128]{1,0:T(8,128)(2,1)S(1)}, bf16[272,128]{1,0:T(8,128)(2,1)S(1)}, u32[]{:S(2)}, u32[]{:S(2)}) collective-permute-start(bf16[272,128]{1,0:T(8,128)(2,1)S(1)} %get-tuple-element.36), channel_id=1, source_target_pairs={{0,12},{4,0},{8,4},{12,8},{1,13},{5,1},{9,5},{13,9},{2,14},{6,2},{... | collective-permute-start | bytes 208904 | tf_op jit(solution)/shard_map/ppermute | solution.py:303
  34.7 4.1 %collective-permute-start.7 = (bf16[272,128]{1,0:T(8,128)(2,1)S(1)}, bf16[272,128]{1,0:T(8,128)(2,1)S(1)}, u32[]{:S(2)}, u32[]{:S(2)}) collective-permute-start(bf16[272,128]{1,0:T(8,128)(2,1)S(1)} %get-tuple-element.33.rest_0_), channel_id=1, source_target_pairs={{0,1},{1,0},{2,3},{3,2},{4,5},{5,4},{6,7},{7,6},{8,9},{9,8},{10,11... | collective-permute-start | bytes 208904 | tf_op jit(solution)/shard_map/ppermute | solution.py:292
  35.5 3.3 %collective-permute-start.8 = (bf16[272,128]{1,0:T(8,128)(2,1)S(1)}, bf16[272,128]{1,0:T(8,128)(2,1)S(1)}, u32[]{:S(2)}, u32[]{:S(2)}) collective-permute-start(bf16[272,128]{1,0:T(8,128)(2,1)S(1)} %collective-permute-done.4.rest_1_), channel_id=1, source_target_pairs={{0,1},{1,0},{2,3},{3,2},{4,5},{5,4},{6,7},{7,6},{8,9},{9,8},{10,11... | collective-permute-start | bytes 208904 | tf_op jit(solution)/shard_map/ppermute | solution.py:292
  38.3 1.3 %collective-permute-start.9 = (bf16[272,128]{1,0:T(8,128)(2,1)S(1)}, bf16[272,128]{1,0:T(8,128)(2,1)S(1)}, u32[]{:S(2)}, u32[]{:S(2)}) collective-permute-start(bf16[272,128]{1,0:T(8,128)(2,1)S(1)} %collective-permute-done.5.rest_2_), channel_id=1, source_target_pairs={{0,1},{1,0},{2,3},{3,2},{4,5},{5,4},{6,7},{7,6},{8,9},{9,8},{10,11... | collective-permute-start | bytes 208904 | tf_op jit(solution)/shard_map/ppermute | solution.py:292
  38.6 1.3 %collective-permute-start.10 = (bf16[272,128]{1,0:T(8,128)(2,1)S(1)}, bf16[272,128]{1,0:T(8,128)(2,1)S(1)}, u32[]{:S(2)}, u32[]{:S(2)}) collective-permute-start(bf16[272,128]{1,0:T(8,128)(2,1)S(1)} %collective-permute-done.6.rest_3_), channel_id=1, source_target_pairs={{0,1},{1,0},{2,3},{3,2},{4,5},{5,4},{6,7},{7,6},{8,9},{9,8},{10,11... | collective-permute-start | bytes 208904 | tf_op jit(solution)/shard_map/ppermute | solution.py:292

commit v10 on v9

--- a/solution.py
+++ b/solution.py
@@ -82,16 +82,13 @@
                     right_qn[s] == r, block, zero
                 )
 
-    def one_step(i, unused):
+    for i in range(steps):
         right_copy(i).wait()
-        at = pl.ds(i * BLOCK_K, BLOCK_K)
-        stream = jnp.concatenate([right[at, r].reshape(BLOCK_K * width, width) for r in range(right_count)], axis=1)
-        for pair in range(sectors // 2):
-            product = jnp.dot(stream, sources[pair], preferred_element_type=jnp.float32)
-            half[pair // 2, at, pair % 2] = product.astype(jnp.bfloat16).reshape(BLOCK_K, width, 2 * width)
-        return unused
-
-    lax.fori_loop(0, steps, one_step, 0)
+    operators = right.shape[0]
+    stream = jnp.concatenate([right[:, r].reshape(operators * width, width) for r in range(right_count)], axis=1)
+    for pair in range(sectors // 2):
+        product = jnp.dot(stream, sources[pair], preferred_element_type=jnp.float32)
+        half[pair // 2, :, pair % 2] = product.astype(jnp.bfloat16).reshape(operators, width, 2 * width)
 
 
 def accumulate(code, pieces, plan, slots, half, totals):
@@ -201,9 +198,9 @@
             ids = jnp.where(side == h, mine[d][part * width :, :], theirs[d][part * width :, :]).astype(jnp.float32)
             for m in range(part):
                 at = pl.ds(m * width, width)
-                block = jnp.where(side == h, mine[d][at, :], theirs[d][at, :]).astype(jnp.float32)
+                block = jnp.where(side == h, mine[d][at, :], theirs[d][at, :])
                 target = jnp.max(ids[m : m + 1, :]).astype(jnp.int32)
-                out[target] += block.T
+                out[target] += block.T.astype(jnp.float32)
 
 
 def shards(sizes, psi, left_ops, right_ops, left_qn, right_qn, pair_slot, slot_target):

time: 42.1 us -> 41.6 us (0.988); the launches traced: 41.3 us -> 41.3 us
  Pallas kernels: 23.3 us -> 22.3 us
  starting transfers between devices: 11.6 us -> 12.2 us
    pallas_call x1, Pallas kernels: 7.55 us -> 6.46 us  [shards(): pl.pallas_call(own_kernel, out_shape=[jax.ShapeDtypeStruct(total_shape, j...]
    ppermute x3, starting transfers between devices: 6.13 us -> 6.77 us  [shards(): lax.ppermute(partial[d], 'sector', [(i, (i + d) % rows) for i in range(ro...]
  transfers between devices with their start and end apart: 11 -> 11, of which waited for: 6 -> 7; matrix products, arithmetic and copies ran while one was open for 0% -> 0% of each run, Pallas kernels for 39% -> 36%
where the time goes in v10:
time: 41.6 us; the launch traced here: 41.3 us
  Pallas kernels  22.3 us (54%)
  starting transfers between devices  12.2 us (29%)
  waiting for transfers between devices  6.74 us (16%)
    pallas_call x1, Pallas kernels, shards(): pl.pallas_call(functools.partial(right_kernel, blocks, left_local), out_s...  8.62 us
    ppermute x3, starting transfers between devices, shards(): lax.ppermute(partial[d], 'sector', [(i, (i + d) % rows) for i in range(ro...  6.77 us
    pallas_call x1, Pallas kernels, shards(): pl.pallas_call(own_kernel, out_shape=[jax.ShapeDtypeStruct(total_shape, j...  6.46 us
    pallas_call x1, Pallas kernels, shards(): pl.pallas_call(functools.partial(other_kernel, rows, sets), out_shape=[ja...  4 us
    ppermute x3, waiting for transfers between devices, shards(): lax.ppermute(partial[d], 'sector', [(i, (i + d) % rows) for i in range(ro...  3.9 us
    ppermute x2, starting transfers between devices, over_blocks(): lax.ppermute(part, 'blk', [((b + d) % blocks, b) for b in range(blocks)])  3.1 us
    ppermute x5, waiting for transfers between devices, over_cores(): lax.ppermute(block, 'op', [(h, halves - 1 - h) for h in range(halves)])  2.51 us
    ppermute x1, starting transfers between devices, shards(): swapped = [lax.ppermute(part, 'sector', swap) for part in direct]  2.01 us
  transfers between devices with their start and end apart: 11, of which 7 were waited for; matrix products, arithmetic and copies ran while one was open for 0% of the time, Pallas kernels for 36%

profile of v10, /device:TPU:0, one launch (start us, length us, event | category | flops | bytes accessed | tf_op | source)
XLA Modules:
  0.0 41.3 jit_solution(14886419321360965385)
XLA Ops:
  0.0 1.1 %cut_left.1 = (bf16[8,1,128,128]{3,2,1,0:T(8,128)(2,1)S(1)}, bf16[16,1,128,128]{3,2,1,0:T(8,128)(2,1)S(1)}) custom-call(bf16[32,1,128,128]{3,2,1,0:T(8,128)(2,1)} %left.3), custom_call_target="tpu_custom_call" | custom-call | tf_op jit(solution)/shard_map/cut_left/pallas_call | solution.py:230
  1.1 3.0 %collective-permute-start = (bf16[8,1,128,128]{3,2,0,1:T(8,128)(2,1)S(1)}, bf16[8,1,128,128]{3,2,0,1:T(8,128)(2,1)S(1)}, u32[]{:S(2)}, u32[]{:S(2)}) collective-permute-start(bf16[8,1,128,128]{3,2,0,1:T(8,128)(2,1)S(1)} %bitcast.14), channel_id=1, source_target_pairs={{2,0},{0,2},{3,1},{1,3},{6,4},{4,6},{7,5},{5,7},{10,8},{8,10},{11,... | collective-permute-start | bytes 786440 | tf_op jit(solution)/shard_map/ppermute | solution.py:228
  4.2 0.0 copy-start
  4.2 0.1 collective-permute-start.2
  4.3 8.6 %right_side.1 = (bf16[6,32,2,128,256]{4,3,2,1,0:T(8,128)(2,1)S(1)}, s32[28]{0:T(128)S(1)}) custom-call(s32[24]{0:T(128)} %left_qn_in.1, s32[24]{0:T(128)} %right_qn_in.1, bf16[24,128,128]{2,1,0:T(8,128)(2,1)} %psi_in.1, bf16[32,2,128,128]{3,2,1,0:T(8,128)(2,1)} %right_in.1), custom_call_target="tpu_custom_call" | custom-call | flops 12884901888 | bytes 4194304 | tf_op jit(solution)/shard_map/right_side/pallas_call | solution.py:244
  12.9 0.0 collective-permute-done
  12.9 2.0 %collective-permute-start.1 = (bf16[8,1,128,128]{3,2,0,1:T(8,128)(2,1)S(1)}, bf16[8,1,128,128]{3,2,0,1:T(8,128)(2,1)S(1)}, u32[]{:S(2)}, u32[]{:S(2)}) collective-permute-start(bf16[8,1,128,128]{3,2,0,1:T(8,128)(2,1)S(1)} %collective-permute-done), channel_id=1, source_target_pairs={{0,4},{4,0},{8,12},{12,8},{1,5},{5,1},{9,13},{13,9},{2,6},{6,2},{1... | collective-permute-start | bytes 786440 | tf_op jit(solution)/shard_map/ppermute | solution.py:265
  14.9 0.0 copy-done
  14.9 0.0 copy-done.1
  14.9 6.5 %own_left.1 = (f32[17,128,128]{2,1,0:T(8,128)S(1)}, f32[17,128,128]{2,1,0:T(8,128)S(1)}, f32[17,128,128]{2,1,0:T(8,128)S(1)}, f32[17,128,128]{2,1,0:T(8,128)S(1)}) custom-call(s32[28]{0:T(128)S(1)} %get-tuple-element.21.plan, s32[24,32]{1,0:T(8,128)S(1)} %bitcast.11, bf16[6,32,2,128,256]{4,3,2,1,0:T(8,128)(2,1)S(1)} %get-tuple-element.24.half, ...), custom_call_target="tpu_custom_call" | custom-call | flops 6442450944 | bytes 4194304 | tf_op jit(solution)/shard_map/own_left/pallas_call | solution.py:266
  21.4 0.3 collective-permute-done.2
  21.7 0.0 collective-permute-done.1
  21.7 4.0 %other_left.1 = (f32[17,128,128]{2,1,0:T(8,128)S(1)}, f32[17,128,128]{2,1,0:T(8,128)S(1)}, f32[17,128,128]{2,1,0:T(8,128)S(1)}, f32[17,128,128]{2,1,0:T(8,128)S(...) custom-call(s32[28]{0:T(128)S(1)} %get-tuple-element.21.plan, ...), custom_call_target="tpu_custom_call", output_to_operand_aliasing={{0}: (5, {}), {1}: (6, {}), {2}: (7, {}), {3}: (8, {})} | custom-call | flops 6442450944 | bytes 4194304 | tf_op jit(solution)/shard_map/other_left/pallas_call | solution.py:275
  25.7 0.1 collective-permute-start.3
  25.8 1.5 %collective-permute-done.3.taken = bf16[8,128,128]{2,1,0:T(8,128)(2,1)S(1)} collective-permute-done((bf16[8,128,128]{2,1,0:T(8,128)(2,1)S(1)}, bf16[8,128,128]{2,1,0:T(8,128)(2,1)S(1)}, u32[]{:S(2)}, u32[]{:S(2)}) %collective-permute-start.3) | collective-permute-done | bytes 262176 | tf_op jit(solution)/shard_map/ppermute | solution.py:289
  27.3 0.0 copy-done.2
  27.3 0.6 %combine.1 = (bf16[272,128]{1,0:T(8,128)(2,1)S(1)}, bf16[272,128]{1,0:T(8,128)(2,1)S(1)}, bf16[272,128]{1,0:T(8,128)(2,1)S(1)}, bf16[272,128]{1,0:T(8,128)(2,1)S(1)}) custom-call(s32[1,1,16]{2,1,0:T(1,128)S(1)} %copy-done.2, f32[8,128,128]{2,1,0:T(8,128)S(1)} %get-tuple-element.31.keep, bf16[8,128,128]{2,1,0:T(8,128)(2,1)S(1)} %collective-permute-done.3.taken), custom_call_target="tpu_custom_call" | custom-call | tf_op jit(solution)/shard_map/combine/pallas_call | solution.py:291
  27.9 2.8 %collective-permute-start.4 = (bf16[272,128]{1,0:T(8,128)(2,1)S(1)}, bf16[272,128]{1,0:T(8,128)(2,1)S(1)}, u32[]{:S(2)}, u32[]{:S(2)}) collective-permute-start(bf16[272,128]{1,0:T(8,128)(2,1)S(1)} %get-tuple-element.34), channel_id=1, source_target_pairs={{0,4},{4,8},{8,12},{12,0},{1,5},{5,9},{9,13},{13,1},{2,6},{6,10},{... | collective-permute-start | bytes 208904 | tf_op jit(solution)/shard_map/ppermute | solution.py:300
  30.8 2.6 %collective-permute-start.5 = (bf16[272,128]{1,0:T(8,128)(2,1)S(1)}, bf16[272,128]{1,0:T(8,128)(2,1)S(1)}, u32[]{:S(2)}, u32[]{:S(2)}) collective-permute-start(bf16[272,128]{1,0:T(8,128)(2,1)S(1)} %get-tuple-element.35), channel_id=1, source_target_pairs={{0,8},{4,12},{8,0},{12,4},{1,9},{5,13},{9,1},{13,5},{2,10},{6,14},... | collective-permute-start | bytes 208904 | tf_op jit(solution)/shard_map/ppermute | solution.py:300
  33.4 1.3 %collective-permute-start.6 = (bf16[272,128]{1,0:T(8,128)(2,1)S(1)}, bf16[272,128]{1,0:T(8,128)(2,1)S(1)}, u32[]{:S(2)}, u32[]{:S(2)}) collective-permute-start(bf16[272,128]{1,0:T(8,128)(2,1)S(1)} %get-tuple-element.36), channel_id=1, source_target_pairs={{0,12},{4,0},{8,4},{12,8},{1,13},{5,1},{9,5},{13,9},{2,14},{6,2},{... | collective-permute-start | bytes 208904 | tf_op jit(solution)/shard_map/ppermute | solution.py:300
  34.7 0.0 collective-permute-start.7
  34.7 0.9 %collective-permute-done.4.rest_1_ = bf16[272,128]{1,0:T(8,128)(2,1)S(1)} collective-permute-done((bf16[272,128]{1,0:T(8,128)(2,1)S(1)}, bf16[272,128]{1,0:T(8,128)(2,1)S(1)}, u32[]{:S(2)}, u32[]{:S(2)}) %collective-permute-start.4) | collective-permute-done | bytes 69664 | tf_op jit(solution)/shard_map/ppermute | solution.py:300
  35.6 0.0 collective-permute-start.8
  35.6 2.8 %collective-permute-done.5.rest_2_ = bf16[272,128]{1,0:T(8,128)(2,1)S(1)} collective-permute-done((bf16[272,128]{1,0:T(8,128)(2,1)S(1)}, bf16[272,128]{1,0:T(8,128)(2,1)S(1)}, u32[]{:S(2)}, u32[]{:S(2)}) %collective-permute-start.5) | collective-permute-done | bytes 69664 | tf_op jit(solution)/shard_map/ppermute | solution.py:300
  38.3 0.0 collective-permute-start.9
  38.4 0.2 collective-permute-done.6.rest_3_
  38.6 0.3 collective-permute-start.10
  38.9 0.0 collective-permute-done.7.rest_4_
  38.9 0.0 collective-permute-done.8.rest_5_
  38.9 0.7 %collective-permute-done.9.rest_6_ = bf16[272,128]{1,0:T(8,128)(2,1)S(1)} collective-permute-done((bf16[272,128]{1,0:T(8,128)(2,1)S(1)}, bf16[272,128]{1,0:T(8,128)(2,1)S(1)}, u32[]{:S(2)}, u32[]{:S(2)}) %collective-permute-start.9) | collective-permute-done | bytes 69664 | tf_op jit(solution)/shard_map/ppermute | solution.py:289
  39.6 0.2 collective-permute-done.10.rest_7_
  39.9 1.5 %assemble.1 = f32[24,128,128]{2,1,0:T(8,128)} custom-call(bf16[272,128]{1,0:T(8,128)(2,1)S(1)} %get-tuple-element.33.rest_0_, bf16[272,128]{1,0:T(8,128)(2,1)S(1)} %collective-permute-done.4.rest_1_, bf16[272,128]{1,0:T(8,128)(2,1)S(1)} %collective-permute-done.5.rest_2_, bf16[272,128]{1,0:T(8,128)(2,1)S(1)} %collective-permute-done.6.rest_3_, ...), custom_call_target="tpu_custom_call" | custom-call | tf_op jit(solution)/shard_map/assemble/pallas_call | solution.py:304
  (2 shorter events, 0.0 us)
Async XLA Ops:
  1.1 11.7 %collective-permute-start = (bf16[8,1,128,128]{3,2,0,1:T(8,128)(2,1)S(1)}, bf16[8,1,128,128]{3,2,0,1:T(8,128)(2,1)S(1)}, u32[]{:S(2)}, u32[]{:S(2)}) collective-permute-start(bf16[8,1,128,128]{3,2,0,1:T(8,128)(2,1)S(1)} %bitcast.14), channel_id=1, source_target_pairs={{2,0},{0,2},{3,1},{1,3},{6,4},{4,6},{7,5},{5,7},{10,8},{8,10},{11,... | collective-permute-start | bytes 786440 | tf_op jit(solution)/shard_map/ppermute | solution.py:228
  4.2 10.7 %copy-start = (bf16[32,1,128,128]{3,2,1,0:T(8,128)(2,1)S(1)}, bf16[32,1,128,128]{3,2,1,0:T(8,128)(2,1)}, u32[]{:S(2)}) copy-start(bf16[32,1,128,128]{3,2,1,0:T(8,128)(2,1)} %left.3) | copy-start | bytes 3145732
  4.2 10.7 %copy-start.1 = (s32[32,24]{0,1:T(8,128)S(1)}, s32[32,24]{0,1:T(8,128)}, u32[]{:S(2)}) copy-start(s32[32,24]{0,1:T(8,128)} %param.12) | copy-start | bytes 9220
  4.2 17.5 %collective-permute-start.2 = (bf16[16,1,128,128]{3,2,0,1:T(8,128)(2,1)S(1)}, bf16[16,1,128,128]{3,2,0,1:T(8,128)(2,1)S(1)}, u32[]{:S(2)}, u32[]{:S(2)}) collective-permute-start(bf16[16,1,128,128]{3,2,0,1:T(8,128)(2,1)S(1)} %bitcast.13), channel_id=1, source_target_pairs={{2,0},{0,2},{3,1},{1,3},{6,4},{4,6},{7,5},{5,7},{10,8},{8,10},{11,... | collective-permute-start | bytes 1572872 | tf_op jit(solution)/shard_map/ppermute | solution.py:228
  12.9 8.8 %collective-permute-start.1 = (bf16[8,1,128,128]{3,2,0,1:T(8,128)(2,1)S(1)}, bf16[8,1,128,128]{3,2,0,1:T(8,128)(2,1)S(1)}, u32[]{:S(2)}, u32[]{:S(2)}) collective-permute-start(bf16[8,1,128,128]{3,2,0,1:T(8,128)(2,1)S(1)} %collective-permute-done), channel_id=1, source_target_pairs={{0,4},{4,0},{8,12},{12,8},{1,5},{5,1},{9,13},{13,9},{2,6},{6,2},{1... | collective-permute-start | bytes 786440 | tf_op jit(solution)/shard_map/ppermute | solution.py:265
  21.7 5.6 %copy-start.2 = (s32[1,1,16]{2,1,0:T(1,128)S(1)}, s32[1,1,16]{2,1,0:T(1,128)}, u32[]{:S(2)}) copy-start(s32[1,1,16]{2,1,0:T(1,128)} %slot_target.1) | copy-start | bytes 196
  25.7 1.6 %collective-permute-start.3 = (bf16[8,128,128]{2,1,0:T(8,128)(2,1)S(1)}, bf16[8,128,128]{2,1,0:T(8,128)(2,1)S(1)}, u32[]{:S(2)}, u32[]{:S(2)}) collective-permute-start(bf16[8,128,128]{2,1,0:T(8,128)(2,1)S(1)} %get-tuple-element.32), channel_id=1, source_target_pairs={{0,1},{1,0},{2,3},{3,2},{4,5},{5,4},{6,7},{7,6},{8,9},{9,8},{10,11... | collective-permute-start | bytes 786440 | tf_op jit(solution)/shard_map/ppermute | solution.py:289
  27.9 7.6 %collective-permute-start.4 = (bf16[272,128]{1,0:T(8,128)(2,1)S(1)}, bf16[272,128]{1,0:T(8,128)(2,1)S(1)}, u32[]{:S(2)}, u32[]{:S(2)}) collective-permute-start(bf16[272,128]{1,0:T(8,128)(2,1)S(1)} %get-tuple-element.34), channel_id=1, source_target_pairs={{0,4},{4,8},{8,12},{12,0},{1,5},{5,9},{9,13},{13,1},{2,6},{6,10},{... | collective-permute-start | bytes 208904 | tf_op jit(solution)/shard_map/ppermute | solution.py:300
  30.8 7.6 %collective-permute-start.5 = (bf16[272,128]{1,0:T(8,128)(2,1)S(1)}, bf16[272,128]{1,0:T(8,128)(2,1)S(1)}, u32[]{:S(2)}, u32[]{:S(2)}) collective-permute-start(bf16[272,128]{1,0:T(8,128)(2,1)S(1)} %get-tuple-element.35), channel_id=1, source_target_pairs={{0,8},{4,12},{8,0},{12,4},{1,9},{5,13},{9,1},{13,5},{2,10},{6,14},... | collective-permute-start | bytes 208904 | tf_op jit(solution)/shard_map/ppermute | solution.py:300
  33.4 5.2 %collective-permute-start.6 = (bf16[272,128]{1,0:T(8,128)(2,1)S(1)}, bf16[272,128]{1,0:T(8,128)(2,1)S(1)}, u32[]{:S(2)}, u32[]{:S(2)}) collective-permute-start(bf16[272,128]{1,0:T(8,128)(2,1)S(1)} %get-tuple-element.36), channel_id=1, source_target_pairs={{0,12},{4,0},{8,4},{12,8},{1,13},{5,1},{9,5},{13,9},{2,14},{6,2},{... | collective-permute-start | bytes 208904 | tf_op jit(solution)/shard_map/ppermute | solution.py:300
  34.7 4.2 %collective-permute-start.7 = (bf16[272,128]{1,0:T(8,128)(2,1)S(1)}, bf16[272,128]{1,0:T(8,128)(2,1)S(1)}, u32[]{:S(2)}, u32[]{:S(2)}) collective-permute-start(bf16[272,128]{1,0:T(8,128)(2,1)S(1)} %get-tuple-element.33.rest_0_), channel_id=1, source_target_pairs={{0,1},{1,0},{2,3},{3,2},{4,5},{5,4},{6,7},{7,6},{8,9},{9,8},{10,11... | collective-permute-start | bytes 208904 | tf_op jit(solution)/shard_map/ppermute | solution.py:289
  35.6 3.3 %collective-permute-start.8 = (bf16[272,128]{1,0:T(8,128)(2,1)S(1)}, bf16[272,128]{1,0:T(8,128)(2,1)S(1)}, u32[]{:S(2)}, u32[]{:S(2)}) collective-permute-start(bf16[272,128]{1,0:T(8,128)(2,1)S(1)} %collective-permute-done.4.rest_1_), channel_id=1, source_target_pairs={{0,1},{1,0},{2,3},{3,2},{4,5},{5,4},{6,7},{7,6},{8,9},{9,8},{10,11... | collective-permute-start | bytes 208904 | tf_op jit(solution)/shard_map/ppermute | solution.py:289
  38.3 1.3 %collective-permute-start.9 = (bf16[272,128]{1,0:T(8,128)(2,1)S(1)}, bf16[272,128]{1,0:T(8,128)(2,1)S(1)}, u32[]{:S(2)}, u32[]{:S(2)}) collective-permute-start(bf16[272,128]{1,0:T(8,128)(2,1)S(1)} %collective-permute-done.5.rest_2_), channel_id=1, source_target_pairs={{0,1},{1,0},{2,3},{3,2},{4,5},{5,4},{6,7},{7,6},{8,9},{9,8},{10,11... | collective-permute-start | bytes 208904 | tf_op jit(solution)/shard_map/ppermute | solution.py:289
  38.6 1.3 %collective-permute-start.10 = (bf16[272,128]{1,0:T(8,128)(2,1)S(1)}, bf16[272,128]{1,0:T(8,128)(2,1)S(1)}, u32[]{:S(2)}, u32[]{:S(2)}) collective-permute-start(bf16[272,128]{1,0:T(8,128)(2,1)S(1)} %collective-permute-done.6.rest_3_), channel_id=1, source_target_pairs={{0,1},{1,0},{2,3},{3,2},{4,5},{5,4},{6,7},{7,6},{8,9},{9,8},{10,11... | collective-permute-start | bytes 208904 | tf_op jit(solution)/shard_map/ppermute | solution.py:289

commit v11 on v10

--- a/solution.py
+++ b/solution.py
@@ -25,11 +25,10 @@
         owner = lax.rem(mine + lax.div(code, jnp.int32(left_local)), jnp.int32(blocks))
         wanted = owner * left_local + lax.rem(code, jnp.int32(left_local))
 
-        def one_sector(s, n):
-            plan[n] = s
-            return n + (left_qn[s] == wanted).astype(jnp.int32)
-
-        return lax.fori_loop(0, count, one_sector, n)
+        for s in range(count):
+            plan[n] = jnp.int32(s)
+            n = n + (left_qn[s] == wanted).astype(jnp.int32)
+        return n
 
     plan[count + 1 + blocks * left_local] = lax.fori_loop(0, blocks * left_local, one_code, jnp.int32(0))
 
@@ -165,40 +164,41 @@
         return unused
 
     lax.fori_loop(0, shifts, one_shift, 0)
-    part = CAP // 2
-    for owner in range(rows):
-        for m in range(part):
-            at = owner * CAP + side * part + m
-            keep[owner * part + m] = sum(total[at] for total in totals)
-            at = owner * CAP + (1 - side) * part + m
-            give[owner * part + m] = sum(total[at] for total in totals).astype(jnp.bfloat16)
+    for j in range(rows // 2):
+        mine = lax.bitwise_xor(row, j + (1 - side) * (rows // 2)) * CAP
+        other = lax.bitwise_xor(row, j + side * (rows // 2)) * CAP
+        for m in range(CAP):
+            keep[j * CAP + m] = sum(total[mine + m] for total in totals)
+            give[j * CAP + m] = sum(total[other + m] for total in totals).astype(jnp.bfloat16)
 
 
 def combine_kernel(slot_target, keep, taken, *outs):
-    part, width = CAP // 2, keep.shape[1]
+    width = keep.shape[1]
     row, side = lax.axis_index("sector"), lax.axis_index("op")
     line = lax.broadcasted_iota(jnp.int32, (TAIL, width), 0)
-    for d, out in enumerate(outs):
-        owner = lax.rem(row + d, jnp.int32(len(outs)))
+    for j, out in enumerate(outs):
+        owner = lax.bitwise_xor(row, j + (1 - side) * len(outs))
         ids = jnp.zeros((TAIL, width), jnp.int32)
-        for m in range(part):
-            block = keep[owner * part + m] + taken[owner * part + m].astype(jnp.float32)
+        for m in range(CAP):
+            block = keep[j * CAP + m] + taken[j * CAP + m].astype(jnp.float32)
             out[m * width : (m + 1) * width, :] = block.astype(jnp.bfloat16)
-            ids = jnp.where(line == m, slot_target[0, 0, owner * CAP + side * part + m], ids)
-        out[part * width :, :] = ids.astype(jnp.float32).astype(jnp.bfloat16)
-
-
-def assemble_kernel(rows, *rest):
-    mine, theirs, out = rest[:rows], rest[rows : 2 * rows], rest[-1]
-    part, width = CAP // 2, out.shape[1]
+            ids = jnp.where(line == m, slot_target[0, 0, owner * CAP + m], ids)
+        out[CAP * width :, :] = ids.astype(jnp.float32).astype(jnp.bfloat16)
+
+
+def assemble_kernel(*refs):
+    count = len(refs) // 2
+    mine, theirs, out = refs[:count], refs[count : 2 * count], refs[-1]
+    width = out.shape[1]
     side = lax.axis_index("op")
     out[...] = jnp.zeros_like(out)
-    for d in range(rows):
+    for j in range(count):
         for h in range(2):
-            ids = jnp.where(side == h, mine[d][part * width :, :], theirs[d][part * width :, :]).astype(jnp.float32)
-            for m in range(part):
+            tail = pl.ds(CAP * width, TAIL)
+            ids = jnp.where(side == h, mine[j][tail, :], theirs[j][tail, :]).astype(jnp.float32)
+            for m in range(CAP):
                 at = pl.ds(m * width, width)
-                block = jnp.where(side == h, mine[d][at, :], theirs[d][at, :])
+                block = jnp.where(side == h, mine[j][at, :], theirs[j][at, :])
                 target = jnp.max(ids[m : m + 1, :]).astype(jnp.int32)
                 out[target] += block.T.astype(jnp.float32)
 
@@ -220,7 +220,7 @@
         flops = int(16 * operators * sectors * width**3 * share)
         return pl.CostEstimate(flops=flops, bytes_accessed=4 * 2**20, transcendentals=0)
 
-    assert rows % 2 == 0
+    assert rows % 2 == 0 and rows & (rows - 1) == 0 and halves == 2
     quarter = operators // 4
     swap = [(i, i ^ 1) for i in range(rows)]
 
@@ -290,21 +290,22 @@
 
     partial = pl.pallas_call(
         combine_kernel,
-        out_shape=[jax.ShapeDtypeStruct((CAP // 2 * width + TAIL, width), jnp.bfloat16)] * rows,
+        out_shape=[jax.ShapeDtypeStruct((CAP * width + TAIL, width), jnp.bfloat16)] * (rows // 2),
         in_specs=[smem] + [vmem] * 2,
-        out_specs=[vmem] * rows,
+        out_specs=[vmem] * (rows // 2),
         compiler_params=params,
         name="combine",
     )(slot_target, keep, over_cores(give))
-    crossed = {
-        d: lax.ppermute(partial[d], "sector", [(i, (i + d) % rows) for i in range(rows)]) for d in range(1, rows)
-    }
-    mine = [partial[0]] + [crossed[d] for d in range(1, rows)]
+    def over_rows(block, j):
+        goals = [(i, h, i ^ (j + (1 - h) * (rows // 2))) for i in range(rows) for h in range(halves)]
+        return lax.ppermute(block, ("sector", "op"), [(i * halves + h, goal * halves + h) for i, h, goal in goals])
+
+    mine = [over_rows(block, j) for j, block in enumerate(partial)]
     theirs = [over_cores(block) for block in mine]
     return pl.pallas_call(
-        functools.partial(assemble_kernel, rows),
+        assemble_kernel,
         out_shape=jax.ShapeDtypeStruct((sectors, width, width), jnp.float32),
-        in_specs=[vmem] * (2 * rows),
+        in_specs=[vmem] * rows,
         out_specs=vmem,
         compiler_params=params,
         name="assemble",

time: 41.6 us -> 43.5 us (1.046); the launches traced: 41.3 us -> 42.6 us
  waiting for transfers between devices: 6.74 us -> 8.07 us
  Pallas kernels: 22.3 us -> 23.6 us
  starting transfers between devices: 12.2 us -> 10.9 us
    ppermute x3 -> x2, waiting for transfers between devices: 3.9 us -> 5.51 us  [over_rows(): lax.ppermute(block, ('sector', 'op'), [(i * halves + h, goal * halves + h...]
    ppermute x3 -> x2, starting transfers between devices: 6.77 us -> 5.19 us  [over_rows(): lax.ppermute(block, ('sector', 'op'), [(i * halves + h, goal * halves + h...]
    pallas_call x1, Pallas kernels: 6.46 us -> 7.73 us  [shards(): pl.pallas_call(own_kernel, out_shape=[jax.ShapeDtypeStruct(total_shape, j...]
    ppermute x5 -> x3, waiting for transfers between devices: 2.51 us -> 2.55 us  [over_cores(): lax.ppermute(block, 'op', [(h, halves - 1 - h) for h in range(halves)])]
  transfers between devices with their start and end apart: 11 -> 8, of which waited for: 7 -> 4; matrix products, arithmetic and copies ran while one was open for 0% -> 0% of each run, Pallas kernels for 36% -> 38%
where the time goes in v11:
time: 43.5 us; the launch traced here: 42.6 us
  Pallas kernels  23.6 us (54%)
  starting transfers between devices  10.9 us (25%)
  waiting for transfers between devices  8.07 us (19%)
    pallas_call x1, Pallas kernels, shards(): pl.pallas_call(functools.partial(right_kernel, blocks, left_local), out_s...  8.62 us
    pallas_call x1, Pallas kernels, shards(): pl.pallas_call(own_kernel, out_shape=[jax.ShapeDtypeStruct(total_shape, j...  7.73 us
    ppermute x2, waiting for transfers between devices, over_rows(): lax.ppermute(block, ('sector', 'op'), [(i * halves + h, goal * halves + h...  5.51 us
    ppermute x2, starting transfers between devices, over_rows(): lax.ppermute(block, ('sector', 'op'), [(i * halves + h, goal * halves + h...  5.19 us
    pallas_call x1, Pallas kernels, shards(): pl.pallas_call(functools.partial(other_kernel, rows, sets), out_shape=[ja...  4 us
    ppermute x2, starting transfers between devices, over_blocks(): lax.ppermute(part, 'blk', [((b + d) % blocks, b) for b in range(blocks)])  3.1 us
    ppermute x3, waiting for transfers between devices, over_cores(): lax.ppermute(block, 'op', [(h, halves - 1 - h) for h in range(halves)])  2.55 us
    ppermute x1, starting transfers between devices, shards(): swapped = [lax.ppermute(part, 'sector', swap) for part in direct]  2.01 us
  transfers between devices with their start and end apart: 8, of which 4 were waited for; matrix products, arithmetic and copies ran while one was open for 0% of the time, Pallas kernels for 38%

profile of v11, /device:TPU:0, one launch (start us, length us, event | category | flops | bytes accessed | tf_op | source)
XLA Modules:
  0.0 42.6 jit_solution(14329993578611981303)
XLA Ops:
  0.0 1.1 %cut_left.1 = (bf16[8,1,128,128]{3,2,1,0:T(8,128)(2,1)S(1)}, bf16[16,1,128,128]{3,2,1,0:T(8,128)(2,1)S(1)}) custom-call(bf16[32,1,128,128]{3,2,1,0:T(8,128)(2,1)} %left.3), custom_call_target="tpu_custom_call" | custom-call | tf_op jit(solution)/shard_map/cut_left/pallas_call | solution.py:230
  1.1 3.0 %collective-permute-start = (bf16[8,1,128,128]{3,2,0,1:T(8,128)(2,1)S(1)}, bf16[8,1,128,128]{3,2,0,1:T(8,128)(2,1)S(1)}, u32[]{:S(2)}, u32[]{:S(2)}) collective-permute-start(bf16[8,1,128,128]{3,2,0,1:T(8,128)(2,1)S(1)} %bitcast.14), channel_id=1, source_target_pairs={{2,0},{0,2},{3,1},{1,3},{6,4},{4,6},{7,5},{5,7},{10,8},{8,10},{11,... | collective-permute-start | bytes 786440 | tf_op jit(solution)/shard_map/ppermute | solution.py:228
  4.2 0.0 copy-start
  4.2 0.0 copy-start.1
  4.2 0.1 collective-permute-start.2
  4.3 8.6 %right_side.1 = (bf16[6,32,2,128,256]{4,3,2,1,0:T(8,128)(2,1)S(1)}, s32[28]{0:T(128)S(1)}) custom-call(s32[24]{0:T(128)} %left_qn_in.1, s32[24]{0:T(128)} %right_qn_in.1, bf16[24,128,128]{2,1,0:T(8,128)(2,1)} %psi_in.1, bf16[32,2,128,128]{3,2,1,0:T(8,128)(2,1)} %right_in.1), custom_call_target="tpu_custom_call" | custom-call | flops 12884901888 | bytes 4194304 | tf_op jit(solution)/shard_map/right_side/pallas_call | solution.py:244
  12.9 0.0 collective-permute-done
  12.9 2.0 %collective-permute-start.1 = (bf16[8,1,128,128]{3,2,0,1:T(8,128)(2,1)S(1)}, bf16[8,1,128,128]{3,2,0,1:T(8,128)(2,1)S(1)}, u32[]{:S(2)}, u32[]{:S(2)}) collective-permute-start(bf16[8,1,128,128]{3,2,0,1:T(8,128)(2,1)S(1)} %collective-permute-done), channel_id=1, source_target_pairs={{0,4},{4,0},{8,12},{12,8},{1,5},{5,1},{9,13},{13,9},{2,6},{6,2},{1... | collective-permute-start | bytes 786440 | tf_op jit(solution)/shard_map/ppermute | solution.py:265
  14.9 0.0 copy-done
  14.9 0.0 copy-done.1
  14.9 7.7 %own_left.1 = (f32[17,128,128]{2,1,0:T(8,128)S(1)}, f32[17,128,128]{2,1,0:T(8,128)S(1)}, f32[17,128,128]{2,1,0:T(8,128)S(1)}, f32[17,128,128]{2,1,0:T(8,128)S(1)}) custom-call(s32[28]{0:T(128)S(1)} %get-tuple-element.19.plan, s32[24,32]{1,0:T(8,128)S(1)} %bitcast.11, bf16[6,32,2,128,256]{4,3,2,1,0:T(8,128)(2,1)S(1)} %get-tuple-element.22.half, ...), custom_call_target="tpu_custom_call" | custom-call | flops 6442450944 | bytes 4194304 | tf_op jit(solution)/shard_map/own_left/pallas_call | solution.py:266
  22.6 0.0 collective-permute-done.2
  22.7 0.0 collective-permute-done.1
  22.7 0.0 copy-start.2
  22.7 4.0 %other_left.1 = (f32[17,128,128]{2,1,0:T(8,128)S(1)}, f32[17,128,128]{2,1,0:T(8,128)S(1)}, f32[17,128,128]{2,1,0:T(8,128)S(1)}, f32[17,128,128]{2,1,0:T(8,128)S(...) custom-call(s32[28]{0:T(128)S(1)} %get-tuple-element.19.plan, ...), custom_call_target="tpu_custom_call", output_to_operand_aliasing={{0}: (5, {}), {1}: (6, {}), {2}: (7, {}), {3}: (8, {})} | custom-call | flops 6442450944 | bytes 4194304 | tf_op jit(solution)/shard_map/other_left/pallas_call | solution.py:275
  26.7 0.1 collective-permute-start.3
  26.8 1.5 %collective-permute-done.3.taken = bf16[8,128,128]{2,1,0:T(8,128)(2,1)S(1)} collective-permute-done((bf16[8,128,128]{2,1,0:T(8,128)(2,1)S(1)}, bf16[8,128,128]{2,1,0:T(8,128)(2,1)S(1)}, u32[]{:S(2)}, u32[]{:S(2)}) %collective-permute-start.3) | collective-permute-done | bytes 262176 | tf_op jit(solution)/shard_map/ppermute | solution.py:289
  28.3 0.0 copy-done.2
  28.3 0.6 %combine.1 = (bf16[528,128]{1,0:T(8,128)(2,1)S(1)}, bf16[528,128]{1,0:T(8,128)(2,1)S(1)}) custom-call(s32[1,1,16]{2,1,0:T(1,128)S(1)} %copy-done.2, f32[8,128,128]{2,1,0:T(8,128)S(1)} %get-tuple-element.29.keep, bf16[8,128,128]{2,1,0:T(8,128)(2,1)S(1)} %collective-permute-done.3.taken), custom_call_target="tpu_custom_call" | custom-call | tf_op jit(solution)/shard_map/combine/pallas_call | solution.py:291
  28.9 3.0 %collective-permute-start.4 = (bf16[528,128]{1,0:T(8,128)(2,1)S(1)}, bf16[528,128]{1,0:T(8,128)(2,1)S(1)}, u32[]{:S(2)}, u32[]{:S(2)}) collective-permute-start(bf16[528,128]{1,0:T(8,128)(2,1)S(1)} %get-tuple-element.31), channel_id=1, source_target_pairs={{0,8},{1,1},{4,12},{5,5},{8,0},{9,9},{12,4},{13,13},{2,10},{3,3},{... | collective-permute-start | bytes 405512 | tf_op jit(solution)/shard_map/ppermute | solution.py:301
  31.9 2.2 %collective-permute-start.5 = (bf16[528,128]{1,0:T(8,128)(2,1)S(1)}, bf16[528,128]{1,0:T(8,128)(2,1)S(1)}, u32[]{:S(2)}, u32[]{:S(2)}) collective-permute-start(bf16[528,128]{1,0:T(8,128)(2,1)S(1)} %get-tuple-element.32), channel_id=1, source_target_pairs={{0,12},{1,5},{4,8},{5,1},{8,4},{9,13},{12,0},{13,9},{2,14},{3,7},{... | collective-permute-start | bytes 405512 | tf_op jit(solution)/shard_map/ppermute | solution.py:301
  34.1 5.5 %collective-permute-done.4.refs_0_ = bf16[528,128]{1,0:T(8,128)(2,1)S(1)} collective-permute-done((bf16[528,128]{1,0:T(8,128)(2,1)S(1)}, bf16[528,128]{1,0:T(8,128)(2,1)S(1)}, u32[]{:S(2)}, u32[]{:S(2)}) %collective-permute-start.4) | collective-permute-done | bytes 135200 | tf_op jit(solution)/shard_map/ppermute | solution.py:301
  39.6 0.0 collective-permute-start.6
  39.6 0.0 collective-permute-done.5.refs_1_
  39.6 0.5 %collective-permute-start.7 = (bf16[528,128]{1,0:T(8,128)(2,1)S(1)}, bf16[528,128]{1,0:T(8,128)(2,1)S(1)}, u32[]{:S(2)}, u32[]{:S(2)}) collective-permute-start(bf16[528,128]{1,0:T(8,128)(2,1)S(1)} %collective-permute-done.5.refs_1_), channel_id=1, source_target_pairs={{0,1},{1,0},{2,3},{3,2},{4,5},{5,4},{6,7},{7,6},{8,9},{9,8},{10,11... | collective-permute-start | bytes 405512 | tf_op jit(solution)/shard_map/ppermute | solution.py:289
  40.1 0.8 %collective-permute-done.6.refs_2_ = bf16[528,128]{1,0:T(8,128)(2,1)S(1)} collective-permute-done((bf16[528,128]{1,0:T(8,128)(2,1)S(1)}, bf16[528,128]{1,0:T(8,128)(2,1)S(1)}, u32[]{:S(2)}, u32[]{:S(2)}) %collective-permute-start.6) | collective-permute-done | bytes 135200 | tf_op jit(solution)/shard_map/ppermute | solution.py:289
  40.9 0.2 collective-permute-done.7.refs_3_
  41.1 1.5 %assemble.1 = f32[24,128,128]{2,1,0:T(8,128)} custom-call(bf16[528,128]{1,0:T(8,128)(2,1)S(1)} %collective-permute-done.4.refs_0_, bf16[528,128]{1,0:T(8,128)(2,1)S(1)} %collective-permute-done.5.refs_1_, bf16[528,128]{1,0:T(8,128)(2,1)S(1)} %collective-permute-done.6.refs_2_, bf16[528,128]{1,0:T(8,128)(2,1)S(1)} %collective-permute-done.7.refs_3_), custom_call_target="tpu_custom_call" | custom-call | tf_op jit(solution)/shard_map/assemble/pallas_call | solution.py:305
Async XLA Ops:
  1.1 11.7 %collective-permute-start = (bf16[8,1,128,128]{3,2,0,1:T(8,128)(2,1)S(1)}, bf16[8,1,128,128]{3,2,0,1:T(8,128)(2,1)S(1)}, u32[]{:S(2)}, u32[]{:S(2)}) collective-permute-start(bf16[8,1,128,128]{3,2,0,1:T(8,128)(2,1)S(1)} %bitcast.14), channel_id=1, source_target_pairs={{2,0},{0,2},{3,1},{1,3},{6,4},{4,6},{7,5},{5,7},{10,8},{8,10},{11,... | collective-permute-start | bytes 786440 | tf_op jit(solution)/shard_map/ppermute | solution.py:228
  4.2 10.7 %copy-start = (bf16[32,1,128,128]{3,2,1,0:T(8,128)(2,1)S(1)}, bf16[32,1,128,128]{3,2,1,0:T(8,128)(2,1)}, u32[]{:S(2)}) copy-start(bf16[32,1,128,128]{3,2,1,0:T(8,128)(2,1)} %left.3) | copy-start | bytes 3145732
  4.2 10.7 %copy-start.1 = (s32[32,24]{0,1:T(8,128)S(1)}, s32[32,24]{0,1:T(8,128)}, u32[]{:S(2)}) copy-start(s32[32,24]{0,1:T(8,128)} %param.12) | copy-start | bytes 9220
  4.2 18.5 %collective-permute-start.2 = (bf16[16,1,128,128]{3,2,0,1:T(8,128)(2,1)S(1)}, bf16[16,1,128,128]{3,2,0,1:T(8,128)(2,1)S(1)}, u32[]{:S(2)}, u32[]{:S(2)}) collective-permute-start(bf16[16,1,128,128]{3,2,0,1:T(8,128)(2,1)S(1)} %bitcast.13), channel_id=1, source_target_pairs={{2,0},{0,2},{3,1},{1,3},{6,4},{4,6},{7,5},{5,7},{10,8},{8,10},{11,... | collective-permute-start | bytes 1572872 | tf_op jit(solution)/shard_map/ppermute | solution.py:228
  12.9 9.8 %collective-permute-start.1 = (bf16[8,1,128,128]{3,2,0,1:T(8,128)(2,1)S(1)}, bf16[8,1,128,128]{3,2,0,1:T(8,128)(2,1)S(1)}, u32[]{:S(2)}, u32[]{:S(2)}) collective-permute-start(bf16[8,1,128,128]{3,2,0,1:T(8,128)(2,1)S(1)} %collective-permute-done), channel_id=1, source_target_pairs={{0,4},{4,0},{8,12},{12,8},{1,5},{5,1},{9,13},{13,9},{2,6},{6,2},{1... | collective-permute-start | bytes 786440 | tf_op jit(solution)/shard_map/ppermute | solution.py:265
  22.7 5.6 %copy-start.2 = (s32[1,1,16]{2,1,0:T(1,128)S(1)}, s32[1,1,16]{2,1,0:T(1,128)}, u32[]{:S(2)}) copy-start(s32[1,1,16]{2,1,0:T(1,128)} %slot_target.1) | copy-start | bytes 196
  26.7 1.6 %collective-permute-start.3 = (bf16[8,128,128]{2,1,0:T(8,128)(2,1)S(1)}, bf16[8,128,128]{2,1,0:T(8,128)(2,1)S(1)}, u32[]{:S(2)}, u32[]{:S(2)}) collective-permute-start(bf16[8,128,128]{2,1,0:T(8,128)(2,1)S(1)} %get-tuple-element.30), channel_id=1, source_target_pairs={{0,1},{1,0},{2,3},{3,2},{4,5},{5,4},{6,7},{7,6},{8,9},{9,8},{10,11... | collective-permute-start | bytes 786440 | tf_op jit(solution)/shard_map/ppermute | solution.py:289
  28.9 10.7 %collective-permute-start.4 = (bf16[528,128]{1,0:T(8,128)(2,1)S(1)}, bf16[528,128]{1,0:T(8,128)(2,1)S(1)}, u32[]{:S(2)}, u32[]{:S(2)}) collective-permute-start(bf16[528,128]{1,0:T(8,128)(2,1)S(1)} %get-tuple-element.31), channel_id=1, source_target_pairs={{0,8},{1,1},{4,12},{5,5},{8,0},{9,9},{12,4},{13,13},{2,10},{3,3},{... | collective-permute-start | bytes 405512 | tf_op jit(solution)/shard_map/ppermute | solution.py:301
  31.9 7.7 %collective-permute-start.5 = (bf16[528,128]{1,0:T(8,128)(2,1)S(1)}, bf16[528,128]{1,0:T(8,128)(2,1)S(1)}, u32[]{:S(2)}, u32[]{:S(2)}) collective-permute-start(bf16[528,128]{1,0:T(8,128)(2,1)S(1)} %get-tuple-element.32), channel_id=1, source_target_pairs={{0,12},{1,5},{4,8},{5,1},{8,4},{9,13},{12,0},{13,9},{2,14},{3,7},{... | collective-permute-start | bytes 405512 | tf_op jit(solution)/shard_map/ppermute | solution.py:301
  39.6 1.4 %collective-permute-start.6 = (bf16[528,128]{1,0:T(8,128)(2,1)S(1)}, bf16[528,128]{1,0:T(8,128)(2,1)S(1)}, u32[]{:S(2)}, u32[]{:S(2)}) collective-permute-start(bf16[528,128]{1,0:T(8,128)(2,1)S(1)} %collective-permute-done.4.refs_0_), channel_id=1, source_target_pairs={{0,1},{1,0},{2,3},{3,2},{4,5},{5,4},{6,7},{7,6},{8,9},{9,8},{10,11... | collective-permute-start | bytes 405512 | tf_op jit(solution)/shard_map/ppermute | solution.py:289
  39.6 1.5 %collective-permute-start.7 = (bf16[528,128]{1,0:T(8,128)(2,1)S(1)}, bf16[528,128]{1,0:T(8,128)(2,1)S(1)}, u32[]{:S(2)}, u32[]{:S(2)}) collective-permute-start(bf16[528,128]{1,0:T(8,128)(2,1)S(1)} %collective-permute-done.5.refs_1_), channel_id=1, source_target_pairs={{0,1},{1,0},{2,3},{3,2},{4,5},{5,4},{6,7},{7,6},{8,9},{9,8},{10,11... | collective-permute-start | bytes 405512 | tf_op jit(solution)/shard_map/ppermute | solution.py:289

commit v12 on v10

--- a/solution.py
+++ b/solution.py
@@ -25,11 +25,10 @@
         owner = lax.rem(mine + lax.div(code, jnp.int32(left_local)), jnp.int32(blocks))
         wanted = owner * left_local + lax.rem(code, jnp.int32(left_local))
 
-        def one_sector(s, n):
-            plan[n] = s
-            return n + (left_qn[s] == wanted).astype(jnp.int32)
-
-        return lax.fori_loop(0, count, one_sector, n)
+        for s in range(count):
+            plan[n] = jnp.int32(s)
+            n = n + (left_qn[s] == wanted).astype(jnp.int32)
+        return n
 
     plan[count + 1 + blocks * left_local] = lax.fori_loop(0, blocks * left_local, one_code, jnp.int32(0))
 
@@ -174,11 +173,11 @@
             give[owner * part + m] = sum(total[at] for total in totals).astype(jnp.bfloat16)
 
 
-def combine_kernel(slot_target, keep, taken, *outs):
+def combine_kernel(shifts, slot_target, keep, taken, *outs):
     part, width = CAP // 2, keep.shape[1]
     row, side = lax.axis_index("sector"), lax.axis_index("op")
     line = lax.broadcasted_iota(jnp.int32, (TAIL, width), 0)
-    for d, out in enumerate(outs):
+    for d, out in zip(shifts, outs):
         owner = lax.rem(row + d, jnp.int32(len(outs)))
         ids = jnp.zeros((TAIL, width), jnp.int32)
         for m in range(part):
@@ -288,18 +287,19 @@
     def over_cores(block):
         return lax.ppermute(block, "op", [(h, halves - 1 - h) for h in range(halves)])
 
+    shifts = sorted(range(1, rows), key=lambda d: (abs(d - rows // 2), d)) + [0]
     partial = pl.pallas_call(
-        combine_kernel,
+        functools.partial(combine_kernel, shifts),
         out_shape=[jax.ShapeDtypeStruct((CAP // 2 * width + TAIL, width), jnp.bfloat16)] * rows,
         in_specs=[smem] + [vmem] * 2,
         out_specs=[vmem] * rows,
         compiler_params=params,
         name="combine",
     )(slot_target, keep, over_cores(give))
-    crossed = {
-        d: lax.ppermute(partial[d], "sector", [(i, (i + d) % rows) for i in range(rows)]) for d in range(1, rows)
-    }
-    mine = [partial[0]] + [crossed[d] for d in range(1, rows)]
+    mine = [
+        lax.ppermute(block, "sector", [(i, (i + d) % rows) for i in range(rows)]) if d else block
+        for d, block in zip(shifts, partial)
+    ]
     theirs = [over_cores(block) for block in mine]
     return pl.pallas_call(
         functools.partial(assemble_kernel, rows),

time: 41.6 us -> 41.7 us (level); the launches traced: 41.3 us -> 41 us
  waiting for transfers between devices: 6.74 us -> 5.15 us
  Pallas kernels: 22.3 us -> 23.6 us
    pallas_call x1, Pallas kernels: 6.46 us -> 7.73 us  [shards(): pl.pallas_call(own_kernel, out_shape=[jax.ShapeDtypeStruct(total_shape, j...]
    ppermute x3, waiting for transfers between devices: 3.9 us -> 2.72 us  [shards(): lax.ppermute(block, 'sector', [(i, (i + d) % rows) for i in range(rows)])]
  transfers between devices with their start and end apart: 11 -> 11, of which waited for: 7 -> 5; matrix products, arithmetic and copies ran while one was open for 0% -> 0% of each run, Pallas kernels for 36% -> 40%
where the time goes in v12:
time: 41.7 us; the launch traced here: 41 us
  Pallas kernels  23.6 us (57%)
  starting transfers between devices  12.2 us (29%)
  waiting for transfers between devices  5.15 us (12%)
    pallas_call x1, Pallas kernels, shards(): pl.pallas_call(functools.partial(right_kernel, blocks, left_local), out_s...  8.62 us
    pallas_call x1, Pallas kernels, shards(): pl.pallas_call(own_kernel, out_shape=[jax.ShapeDtypeStruct(total_shape, j...  7.73 us
    ppermute x3, starting transfers between devices, shards(): lax.ppermute(block, 'sector', [(i, (i + d) % rows) for i in range(rows)])  6.48 us
    pallas_call x1, Pallas kernels, shards(): pl.pallas_call(functools.partial(other_kernel, rows, sets), out_shape=[ja...  4 us
    ppermute x2, starting transfers between devices, over_blocks(): lax.ppermute(part, 'blk', [((b + d) % blocks, b) for b in range(blocks)])  3.1 us
    ppermute x3, waiting for transfers between devices, shards(): lax.ppermute(block, 'sector', [(i, (i + d) % rows) for i in range(rows)])  2.72 us
    ppermute x5, waiting for transfers between devices, over_cores(): lax.ppermute(block, 'op', [(h, halves - 1 - h) for h in range(halves)])  2.43 us
    ppermute x1, starting transfers between devices, shards(): swapped = [lax.ppermute(part, 'sector', swap) for part in direct]  2.01 us
  transfers between devices with their start and end apart: 11, of which 5 were waited for; matrix products, arithmetic and copies ran while one was open for 0% of the time, Pallas kernels for 40%

profile of v12, /device:TPU:0, one launch (start us, length us, event | category | flops | bytes accessed | tf_op | source)
XLA Modules:
  0.0 41.0 jit_solution(363418626199955501)
XLA Ops:
  0.0 1.1 %cut_left.1 = (bf16[8,1,128,128]{3,2,1,0:T(8,128)(2,1)S(1)}, bf16[16,1,128,128]{3,2,1,0:T(8,128)(2,1)S(1)}) custom-call(bf16[32,1,128,128]{3,2,1,0:T(8,128)(2,1)} %left.3), custom_call_target="tpu_custom_call" | custom-call | tf_op jit(solution)/shard_map/cut_left/pallas_call | solution.py:229
  1.1 3.0 %collective-permute-start = (bf16[8,1,128,128]{3,2,0,1:T(8,128)(2,1)S(1)}, bf16[8,1,128,128]{3,2,0,1:T(8,128)(2,1)S(1)}, u32[]{:S(2)}, u32[]{:S(2)}) collective-permute-start(bf16[8,1,128,128]{3,2,0,1:T(8,128)(2,1)S(1)} %bitcast.14), channel_id=1, source_target_pairs={{2,0},{0,2},{3,1},{1,3},{6,4},{4,6},{7,5},{5,7},{10,8},{8,10},{11,... | collective-permute-start | bytes 786440 | tf_op jit(solution)/shard_map/ppermute | solution.py:227
  4.2 0.1 collective-permute-start.2
  4.3 8.6 %right_side.1 = (bf16[6,32,2,128,256]{4,3,2,1,0:T(8,128)(2,1)S(1)}, s32[28]{0:T(128)S(1)}) custom-call(s32[24]{0:T(128)} %left_qn_in.1, s32[24]{0:T(128)} %right_qn_in.1, bf16[24,128,128]{2,1,0:T(8,128)(2,1)} %psi_in.1, bf16[32,2,128,128]{3,2,1,0:T(8,128)(2,1)} %right_in.1), custom_call_target="tpu_custom_call" | custom-call | flops 12884901888 | bytes 4194304 | tf_op jit(solution)/shard_map/right_side/pallas_call | solution.py:243
  12.9 0.0 collective-permute-done
  12.9 2.0 %collective-permute-start.1 = (bf16[8,1,128,128]{3,2,0,1:T(8,128)(2,1)S(1)}, bf16[8,1,128,128]{3,2,0,1:T(8,128)(2,1)S(1)}, u32[]{:S(2)}, u32[]{:S(2)}) collective-permute-start(bf16[8,1,128,128]{3,2,0,1:T(8,128)(2,1)S(1)} %collective-permute-done), channel_id=1, source_target_pairs={{0,4},{4,0},{8,12},{12,8},{1,5},{5,1},{9,13},{13,9},{2,6},{6,2},{1... | collective-permute-start | bytes 786440 | tf_op jit(solution)/shard_map/ppermute | solution.py:264
  14.9 0.0 copy-done
  14.9 0.0 copy-done.1
  14.9 7.7 %own_left.1 = (f32[17,128,128]{2,1,0:T(8,128)S(1)}, f32[17,128,128]{2,1,0:T(8,128)S(1)}, f32[17,128,128]{2,1,0:T(8,128)S(1)}, f32[17,128,128]{2,1,0:T(8,128)S(1)}) custom-call(s32[28]{0:T(128)S(1)} %get-tuple-element.21.plan, s32[24,32]{1,0:T(8,128)S(1)} %bitcast.11, bf16[6,32,2,128,256]{4,3,2,1,0:T(8,128)(2,1)S(1)} %get-tuple-element.24.half, ...), custom_call_target="tpu_custom_call" | custom-call | flops 6442450944 | bytes 4194304 | tf_op jit(solution)/shard_map/own_left/pallas_call | solution.py:265
  22.6 0.0 collective-permute-done.2
  22.6 0.0 collective-permute-done.1
  22.7 0.0 copy-start.2
  22.7 4.0 %other_left.1 = (f32[17,128,128]{2,1,0:T(8,128)S(1)}, f32[17,128,128]{2,1,0:T(8,128)S(1)}, f32[17,128,128]{2,1,0:T(8,128)S(1)}, f32[17,128,128]{2,1,0:T(8,128)S(...) custom-call(s32[28]{0:T(128)S(1)} %get-tuple-element.21.plan, ...), custom_call_target="tpu_custom_call", output_to_operand_aliasing={{0}: (5, {}), {1}: (6, {}), {2}: (7, {}), {3}: (8, {})} | custom-call | flops 6442450944 | bytes 4194304 | tf_op jit(solution)/shard_map/other_left/pallas_call | solution.py:274
  26.7 0.1 collective-permute-start.3
  26.8 1.5 %collective-permute-done.3.taken = bf16[8,128,128]{2,1,0:T(8,128)(2,1)S(1)} collective-permute-done((bf16[8,128,128]{2,1,0:T(8,128)(2,1)S(1)}, bf16[8,128,128]{2,1,0:T(8,128)(2,1)S(1)}, u32[]{:S(2)}, u32[]{:S(2)}) %collective-permute-start.3) | collective-permute-done | bytes 262176 | tf_op jit(solution)/shard_map/ppermute | solution.py:288
  28.3 0.0 copy-done.2
  28.3 0.6 %combine.1 = (bf16[272,128]{1,0:T(8,128)(2,1)S(1)}, bf16[272,128]{1,0:T(8,128)(2,1)S(1)}, bf16[272,128]{1,0:T(8,128)(2,1)S(1)}, bf16[272,128]{1,0:T(8,128)(2,1)S(1)}) custom-call(s32[1,1,16]{2,1,0:T(1,128)S(1)} %copy-done.2, f32[8,128,128]{2,1,0:T(8,128)S(1)} %get-tuple-element.31.keep, bf16[8,128,128]{2,1,0:T(8,128)(2,1)S(1)} %collective-permute-done.3.taken), custom_call_target="tpu_custom_call" | custom-call | tf_op jit(solution)/shard_map/combine/pallas_call | solution.py:291
  28.9 2.7 %collective-permute-start.4 = (bf16[272,128]{1,0:T(8,128)(2,1)S(1)}, bf16[272,128]{1,0:T(8,128)(2,1)S(1)}, u32[]{:S(2)}, u32[]{:S(2)}) collective-permute-start(bf16[272,128]{1,0:T(8,128)(2,1)S(1)} %get-tuple-element.33), channel_id=1, source_target_pairs={{0,8},{4,12},{8,0},{12,4},{1,9},{5,13},{9,1},{13,5},{2,10},{6,14},... | collective-permute-start | bytes 208904 | tf_op jit(solution)/shard_map/ppermute | solution.py:300
  31.6 0.0 collective-permute-start.5
  31.6 3.8 %collective-permute-start.6 = (bf16[272,128]{1,0:T(8,128)(2,1)S(1)}, bf16[272,128]{1,0:T(8,128)(2,1)S(1)}, u32[]{:S(2)}, u32[]{:S(2)}) collective-permute-start(bf16[272,128]{1,0:T(8,128)(2,1)S(1)} %get-tuple-element.35), channel_id=1, source_target_pairs={{0,12},{4,0},{8,4},{12,8},{1,13},{5,1},{9,5},{13,9},{2,14},{6,2},{... | collective-permute-start | bytes 208904 | tf_op jit(solution)/shard_map/ppermute | solution.py:300
  35.4 0.0 collective-permute-start.10
  35.4 1.3 %collective-permute-done.4.rest_0_ = bf16[272,128]{1,0:T(8,128)(2,1)S(1)} collective-permute-done((bf16[272,128]{1,0:T(8,128)(2,1)S(1)}, bf16[272,128]{1,0:T(8,128)(2,1)S(1)}, u32[]{:S(2)}, u32[]{:S(2)}) %collective-permute-start.4) | collective-permute-done | bytes 69664 | tf_op jit(solution)/shard_map/ppermute | solution.py:300
  36.7 0.0 collective-permute-start.7
  36.7 1.4 %collective-permute-done.5.rest_1_ = bf16[272,128]{1,0:T(8,128)(2,1)S(1)} collective-permute-done((bf16[272,128]{1,0:T(8,128)(2,1)S(1)}, bf16[272,128]{1,0:T(8,128)(2,1)S(1)}, u32[]{:S(2)}, u32[]{:S(2)}) %collective-permute-start.5) | collective-permute-done | bytes 69664 | tf_op jit(solution)/shard_map/ppermute | solution.py:300
  38.1 0.0 collective-permute-start.8
  38.1 0.0 collective-permute-done.6.rest_2_
  38.1 0.5 %collective-permute-start.9 = (bf16[272,128]{1,0:T(8,128)(2,1)S(1)}, bf16[272,128]{1,0:T(8,128)(2,1)S(1)}, u32[]{:S(2)}, u32[]{:S(2)}) collective-permute-start(bf16[272,128]{1,0:T(8,128)(2,1)S(1)} %collective-permute-done.6.rest_2_), channel_id=1, source_target_pairs={{0,1},{1,0},{2,3},{3,2},{4,5},{5,4},{6,7},{7,6},{8,9},{9,8},{10,11... | collective-permute-start | bytes 208904 | tf_op jit(solution)/shard_map/ppermute | solution.py:288
  38.6 0.0 collective-permute-done.10.rest_7_
  38.6 0.0 collective-permute-done.7.rest_4_
  38.6 0.7 %collective-permute-done.8.rest_5_ = bf16[272,128]{1,0:T(8,128)(2,1)S(1)} collective-permute-done((bf16[272,128]{1,0:T(8,128)(2,1)S(1)}, bf16[272,128]{1,0:T(8,128)(2,1)S(1)}, u32[]{:S(2)}, u32[]{:S(2)}) %collective-permute-start.8) | collective-permute-done | bytes 69664 | tf_op jit(solution)/shard_map/ppermute | solution.py:288
  39.3 0.2 collective-permute-done.9.rest_6_
  39.5 1.5 %assemble.1 = f32[24,128,128]{2,1,0:T(8,128)} custom-call(bf16[272,128]{1,0:T(8,128)(2,1)S(1)} %collective-permute-done.4.rest_0_, bf16[272,128]{1,0:T(8,128)(2,1)S(1)} %collective-permute-done.5.rest_1_, bf16[272,128]{1,0:T(8,128)(2,1)S(1)} %collective-permute-done.6.rest_2_, bf16[272,128]{1,0:T(8,128)(2,1)S(1)} %get-tuple-element.36.rest_3_, ...), custom_call_target="tpu_custom_call" | custom-call | tf_op jit(solution)/shard_map/assemble/pallas_call | solution.py:304
  (2 shorter events, 0.0 us)
Async XLA Ops:
  1.1 11.7 %collective-permute-start = (bf16[8,1,128,128]{3,2,0,1:T(8,128)(2,1)S(1)}, bf16[8,1,128,128]{3,2,0,1:T(8,128)(2,1)S(1)}, u32[]{:S(2)}, u32[]{:S(2)}) collective-permute-start(bf16[8,1,128,128]{3,2,0,1:T(8,128)(2,1)S(1)} %bitcast.14), channel_id=1, source_target_pairs={{2,0},{0,2},{3,1},{1,3},{6,4},{4,6},{7,5},{5,7},{10,8},{8,10},{11,... | collective-permute-start | bytes 786440 | tf_op jit(solution)/shard_map/ppermute | solution.py:227
  4.2 10.7 %copy-start = (bf16[32,1,128,128]{3,2,1,0:T(8,128)(2,1)S(1)}, bf16[32,1,128,128]{3,2,1,0:T(8,128)(2,1)}, u32[]{:S(2)}) copy-start(bf16[32,1,128,128]{3,2,1,0:T(8,128)(2,1)} %left.3) | copy-start | bytes 3145732
  4.2 10.7 %copy-start.1 = (s32[32,24]{0,1:T(8,128)S(1)}, s32[32,24]{0,1:T(8,128)}, u32[]{:S(2)}) copy-start(s32[32,24]{0,1:T(8,128)} %param.12) | copy-start | bytes 9220
  4.2 18.5 %collective-permute-start.2 = (bf16[16,1,128,128]{3,2,0,1:T(8,128)(2,1)S(1)}, bf16[16,1,128,128]{3,2,0,1:T(8,128)(2,1)S(1)}, u32[]{:S(2)}, u32[]{:S(2)}) collective-permute-start(bf16[16,1,128,128]{3,2,0,1:T(8,128)(2,1)S(1)} %bitcast.13), channel_id=1, source_target_pairs={{2,0},{0,2},{3,1},{1,3},{6,4},{4,6},{7,5},{5,7},{10,8},{8,10},{11,... | collective-permute-start | bytes 1572872 | tf_op jit(solution)/shard_map/ppermute | solution.py:227
  12.9 9.8 %collective-permute-start.1 = (bf16[8,1,128,128]{3,2,0,1:T(8,128)(2,1)S(1)}, bf16[8,1,128,128]{3,2,0,1:T(8,128)(2,1)S(1)}, u32[]{:S(2)}, u32[]{:S(2)}) collective-permute-start(bf16[8,1,128,128]{3,2,0,1:T(8,128)(2,1)S(1)} %collective-permute-done), channel_id=1, source_target_pairs={{0,4},{4,0},{8,12},{12,8},{1,5},{5,1},{9,13},{13,9},{2,6},{6,2},{1... | collective-permute-start | bytes 786440 | tf_op jit(solution)/shard_map/ppermute | solution.py:264
  22.7 5.6 %copy-start.2 = (s32[1,1,16]{2,1,0:T(1,128)S(1)}, s32[1,1,16]{2,1,0:T(1,128)}, u32[]{:S(2)}) copy-start(s32[1,1,16]{2,1,0:T(1,128)} %slot_target.1) | copy-start | bytes 196
  26.7 1.6 %collective-permute-start.3 = (bf16[8,128,128]{2,1,0:T(8,128)(2,1)S(1)}, bf16[8,128,128]{2,1,0:T(8,128)(2,1)S(1)}, u32[]{:S(2)}, u32[]{:S(2)}) collective-permute-start(bf16[8,128,128]{2,1,0:T(8,128)(2,1)S(1)} %get-tuple-element.32), channel_id=1, source_target_pairs={{0,1},{1,0},{2,3},{3,2},{4,5},{5,4},{6,7},{7,6},{8,9},{9,8},{10,11... | collective-permute-start | bytes 786440 | tf_op jit(solution)/shard_map/ppermute | solution.py:288
  28.9 7.8 %collective-permute-start.4 = (bf16[272,128]{1,0:T(8,128)(2,1)S(1)}, bf16[272,128]{1,0:T(8,128)(2,1)S(1)}, u32[]{:S(2)}, u32[]{:S(2)}) collective-permute-start(bf16[272,128]{1,0:T(8,128)(2,1)S(1)} %get-tuple-element.33), channel_id=1, source_target_pairs={{0,8},{4,12},{8,0},{12,4},{1,9},{5,13},{9,1},{13,5},{2,10},{6,14},... | collective-permute-start | bytes 208904 | tf_op jit(solution)/shard_map/ppermute | solution.py:300
  31.6 6.5 %collective-permute-start.5 = (bf16[272,128]{1,0:T(8,128)(2,1)S(1)}, bf16[272,128]{1,0:T(8,128)(2,1)S(1)}, u32[]{:S(2)}, u32[]{:S(2)}) collective-permute-start(bf16[272,128]{1,0:T(8,128)(2,1)S(1)} %get-tuple-element.34), channel_id=1, source_target_pairs={{0,4},{4,8},{8,12},{12,0},{1,5},{5,9},{9,13},{13,1},{2,6},{6,10},{... | collective-permute-start | bytes 208904 | tf_op jit(solution)/shard_map/ppermute | solution.py:300
  31.6 6.5 %collective-permute-start.6 = (bf16[272,128]{1,0:T(8,128)(2,1)S(1)}, bf16[272,128]{1,0:T(8,128)(2,1)S(1)}, u32[]{:S(2)}, u32[]{:S(2)}) collective-permute-start(bf16[272,128]{1,0:T(8,128)(2,1)S(1)} %get-tuple-element.35), channel_id=1, source_target_pairs={{0,12},{4,0},{8,4},{12,8},{1,13},{5,1},{9,5},{13,9},{2,14},{6,2},{... | collective-permute-start | bytes 208904 | tf_op jit(solution)/shard_map/ppermute | solution.py:300
  35.4 3.2 %collective-permute-start.10 = (bf16[272,128]{1,0:T(8,128)(2,1)S(1)}, bf16[272,128]{1,0:T(8,128)(2,1)S(1)}, u32[]{:S(2)}, u32[]{:S(2)}) collective-permute-start(bf16[272,128]{1,0:T(8,128)(2,1)S(1)} %get-tuple-element.36.rest_3_), channel_id=1, source_target_pairs={{0,1},{1,0},{2,3},{3,2},{4,5},{5,4},{6,7},{7,6},{8,9},{9,8},{10,11... | collective-permute-start | bytes 208904 | tf_op jit(solution)/shard_map/ppermute | solution.py:288
  36.7 1.9 %collective-permute-start.7 = (bf16[272,128]{1,0:T(8,128)(2,1)S(1)}, bf16[272,128]{1,0:T(8,128)(2,1)S(1)}, u32[]{:S(2)}, u32[]{:S(2)}) collective-permute-start(bf16[272,128]{1,0:T(8,128)(2,1)S(1)} %collective-permute-done.4.rest_0_), channel_id=1, source_target_pairs={{0,1},{1,0},{2,3},{3,2},{4,5},{5,4},{6,7},{7,6},{8,9},{9,8},{10,11... | collective-permute-start | bytes 208904 | tf_op jit(solution)/shard_map/ppermute | solution.py:288
  38.1 1.3 %collective-permute-start.8 = (bf16[272,128]{1,0:T(8,128)(2,1)S(1)}, bf16[272,128]{1,0:T(8,128)(2,1)S(1)}, u32[]{:S(2)}, u32[]{:S(2)}) collective-permute-start(bf16[272,128]{1,0:T(8,128)(2,1)S(1)} %collective-permute-done.5.rest_1_), channel_id=1, source_target_pairs={{0,1},{1,0},{2,3},{3,2},{4,5},{5,4},{6,7},{7,6},{8,9},{9,8},{10,11... | collective-permute-start | bytes 208904 | tf_op jit(solution)/shard_map/ppermute | solution.py:288
  38.1 1.4 %collective-permute-start.9 = (bf16[272,128]{1,0:T(8,128)(2,1)S(1)}, bf16[272,128]{1,0:T(8,128)(2,1)S(1)}, u32[]{:S(2)}, u32[]{:S(2)}) collective-permute-start(bf16[272,128]{1,0:T(8,128)(2,1)S(1)} %collective-permute-done.6.rest_2_), channel_id=1, source_target_pairs={{0,1},{1,0},{2,3},{3,2},{4,5},{5,4},{6,7},{7,6},{8,9},{9,8},{10,11... | collective-permute-start | bytes 208904 | tf_op jit(solution)/shard_map/ppermute | solution.py:288

commit v13 on v12

--- a/solution.py
+++ b/solution.py
@@ -81,13 +81,16 @@
                     right_qn[s] == r, block, zero
                 )
 
-    for i in range(steps):
+    def one_step(i, unused):
         right_copy(i).wait()
-    operators = right.shape[0]
-    stream = jnp.concatenate([right[:, r].reshape(operators * width, width) for r in range(right_count)], axis=1)
-    for pair in range(sectors // 2):
-        product = jnp.dot(stream, sources[pair], preferred_element_type=jnp.float32)
-        half[pair // 2, :, pair % 2] = product.astype(jnp.bfloat16).reshape(operators, width, 2 * width)
+        at = pl.ds(i * BLOCK_K, BLOCK_K)
+        stream = jnp.concatenate([right[at, r].reshape(BLOCK_K * width, width) for r in range(right_count)], axis=1)
+        for pair in range(sectors // 2):
+            product = jnp.dot(stream, sources[pair], preferred_element_type=jnp.float32)
+            half[pair // 2, at, pair % 2] = product.astype(jnp.bfloat16).reshape(BLOCK_K, width, 2 * width)
+        return unused
+
+    lax.fori_loop(0, steps, one_step, 0)
 
 
 def accumulate(code, pieces, plan, slots, half, totals):

time: 41.7 us -> 42.1 us (level); the launches traced: 41 us -> 42.5 us
  starting transfers between devices: 12.2 us -> 13.7 us
    ppermute x3, starting transfers between devices: 6.48 us -> 8.07 us  [shards(): lax.ppermute(block, 'sector', [(i, (i + d) % rows) for i in range(rows)])]
  transfers between devices with their start and end apart: 11 -> 11, of which waited for: 5 -> 6; matrix products, arithmetic and copies ran while one was open for 0% -> 0% of each run, Pallas kernels for 40% -> 38%
where the time goes in v13:
time: 42.1 us; the launch traced here: 42.5 us
  Pallas kernels  23.3 us (55%)
  starting transfers between devices  13.7 us (33%)
  waiting for transfers between devices  5.45 us (13%)
    pallas_call x1, Pallas kernels, shards(): pl.pallas_call(functools.partial(right_kernel, blocks, left_local), out_s...  8.47 us
    ppermute x3, starting transfers between devices, shards(): lax.ppermute(block, 'sector', [(i, (i + d) % rows) for i in range(rows)])  8.07 us
    pallas_call x1, Pallas kernels, shards(): pl.pallas_call(own_kernel, out_shape=[jax.ShapeDtypeStruct(total_shape, j...  7.55 us
    pallas_call x1, Pallas kernels, shards(): pl.pallas_call(functools.partial(other_kernel, rows, sets), out_shape=[ja...  4 us
    ppermute x2, starting transfers between devices, over_blocks(): lax.ppermute(part, 'blk', [((b + d) % blocks, b) for b in range(blocks)])  3.1 us
    ppermute x3, waiting for transfers between devices, shards(): lax.ppermute(block, 'sector', [(i, (i + d) % rows) for i in range(rows)])  2.78 us
    ppermute x5, waiting for transfers between devices, over_cores(): lax.ppermute(block, 'op', [(h, halves - 1 - h) for h in range(halves)])  2.66 us
    ppermute x1, starting transfers between devices, shards(): swapped = [lax.ppermute(part, 'sector', swap) for part in direct]  2.01 us
  transfers between devices with their start and end apart: 11, of which 6 were waited for; matrix products, arithmetic and copies ran while one was open for 0% of the time, Pallas kernels for 38%

profile of v13, /device:TPU:0, one launch (start us, length us, event | category | flops | bytes accessed | tf_op | source)
XLA Modules:
  0.0 42.5 jit_solution(17894152519788001176)
XLA Ops:
  0.0 1.1 %cut_left.1 = (bf16[8,1,128,128]{3,2,1,0:T(8,128)(2,1)S(1)}, bf16[16,1,128,128]{3,2,1,0:T(8,128)(2,1)S(1)}) custom-call(bf16[32,1,128,128]{3,2,1,0:T(8,128)(2,1)} %left.3), custom_call_target="tpu_custom_call" | custom-call | tf_op jit(solution)/shard_map/cut_left/pallas_call | solution.py:232
  1.1 3.0 %collective-permute-start = (bf16[8,1,128,128]{3,2,0,1:T(8,128)(2,1)S(1)}, bf16[8,1,128,128]{3,2,0,1:T(8,128)(2,1)S(1)}, u32[]{:S(2)}, u32[]{:S(2)}) collective-permute-start(bf16[8,1,128,128]{3,2,0,1:T(8,128)(2,1)S(1)} %bitcast.14), channel_id=1, source_target_pairs={{2,0},{0,2},{3,1},{1,3},{6,4},{4,6},{7,5},{5,7},{10,8},{8,10},{11,... | collective-permute-start | bytes 786440 | tf_op jit(solution)/shard_map/ppermute | solution.py:230
  4.2 0.1 collective-permute-start.2
  4.3 8.5 %right_side.1 = (bf16[6,32,2,128,256]{4,3,2,1,0:T(8,128)(2,1)S(1)}, s32[28]{0:T(128)S(1)}) custom-call(s32[24]{0:T(128)} %left_qn_in.1, s32[24]{0:T(128)} %right_qn_in.1, bf16[24,128,128]{2,1,0:T(8,128)(2,1)} %psi_in.1, bf16[32,2,128,128]{3,2,1,0:T(8,128)(2,1)} %right_in.1), custom_call_target="tpu_custom_call" | custom-call | flops 12884901888 | bytes 4194304 | tf_op jit(solution)/shard_map/right_side/pallas_call | solution.py:246
  12.7 0.0 collective-permute-done
  12.7 2.0 %collective-permute-start.1 = (bf16[8,1,128,128]{3,2,0,1:T(8,128)(2,1)S(1)}, bf16[8,1,128,128]{3,2,0,1:T(8,128)(2,1)S(1)}, u32[]{:S(2)}, u32[]{:S(2)}) collective-permute-start(bf16[8,1,128,128]{3,2,0,1:T(8,128)(2,1)S(1)} %collective-permute-done), channel_id=1, source_target_pairs={{0,4},{4,0},{8,12},{12,8},{1,5},{5,1},{9,13},{13,9},{2,6},{6,2},{1... | collective-permute-start | bytes 786440 | tf_op jit(solution)/shard_map/ppermute | solution.py:267
  14.8 0.0 copy-done
  14.8 0.0 copy-done.1
  14.8 7.6 %own_left.1 = (f32[17,128,128]{2,1,0:T(8,128)S(1)}, f32[17,128,128]{2,1,0:T(8,128)S(1)}, f32[17,128,128]{2,1,0:T(8,128)S(1)}, f32[17,128,128]{2,1,0:T(8,128)S(1)}) custom-call(s32[28]{0:T(128)S(1)} %get-tuple-element.21.plan, s32[24,32]{1,0:T(8,128)S(1)} %bitcast.11, bf16[6,32,2,128,256]{4,3,2,1,0:T(8,128)(2,1)S(1)} %get-tuple-element.24.half, ...), custom_call_target="tpu_custom_call" | custom-call | flops 6442450944 | bytes 4194304 | tf_op jit(solution)/shard_map/own_left/pallas_call | solution.py:268
  22.3 0.0 collective-permute-done.2
  22.3 0.0 collective-permute-done.1
  22.3 0.0 copy-start.2
  22.4 4.0 %other_left.1 = (f32[17,128,128]{2,1,0:T(8,128)S(1)}, f32[17,128,128]{2,1,0:T(8,128)S(1)}, f32[17,128,128]{2,1,0:T(8,128)S(1)}, f32[17,128,128]{2,1,0:T(8,128)S(...) custom-call(s32[28]{0:T(128)S(1)} %get-tuple-element.21.plan, ...), custom_call_target="tpu_custom_call", output_to_operand_aliasing={{0}: (5, {}), {1}: (6, {}), {2}: (7, {}), {3}: (8, {})} | custom-call | flops 6442450944 | bytes 4194304 | tf_op jit(solution)/shard_map/other_left/pallas_call | solution.py:277
  26.4 0.1 collective-permute-start.3
  26.4 1.5 %collective-permute-done.3.taken = bf16[8,128,128]{2,1,0:T(8,128)(2,1)S(1)} collective-permute-done((bf16[8,128,128]{2,1,0:T(8,128)(2,1)S(1)}, bf16[8,128,128]{2,1,0:T(8,128)(2,1)S(1)}, u32[]{:S(2)}, u32[]{:S(2)}) %collective-permute-start.3) | collective-permute-done | bytes 262176 | tf_op jit(solution)/shard_map/ppermute | solution.py:291
  28.0 0.0 copy-done.2
  28.0 0.6 %combine.1 = (bf16[272,128]{1,0:T(8,128)(2,1)S(1)}, bf16[272,128]{1,0:T(8,128)(2,1)S(1)}, bf16[272,128]{1,0:T(8,128)(2,1)S(1)}, bf16[272,128]{1,0:T(8,128)(2,1)S(1)}) custom-call(s32[1,1,16]{2,1,0:T(1,128)S(1)} %copy-done.2, f32[8,128,128]{2,1,0:T(8,128)S(1)} %get-tuple-element.31.keep, bf16[8,128,128]{2,1,0:T(8,128)(2,1)S(1)} %collective-permute-done.3.taken), custom_call_target="tpu_custom_call" | custom-call | tf_op jit(solution)/shard_map/combine/pallas_call | solution.py:294
  28.6 4.3 %collective-permute-start.4 = (bf16[272,128]{1,0:T(8,128)(2,1)S(1)}, bf16[272,128]{1,0:T(8,128)(2,1)S(1)}, u32[]{:S(2)}, u32[]{:S(2)}) collective-permute-start(bf16[272,128]{1,0:T(8,128)(2,1)S(1)} %get-tuple-element.33), channel_id=1, source_target_pairs={{0,8},{4,12},{8,0},{12,4},{1,9},{5,13},{9,1},{13,5},{2,10},{6,14},... | collective-permute-start | bytes 208904 | tf_op jit(solution)/shard_map/ppermute | solution.py:303
  32.8 0.5 %collective-permute-start.5 = (bf16[272,128]{1,0:T(8,128)(2,1)S(1)}, bf16[272,128]{1,0:T(8,128)(2,1)S(1)}, u32[]{:S(2)}, u32[]{:S(2)}) collective-permute-start(bf16[272,128]{1,0:T(8,128)(2,1)S(1)} %get-tuple-element.34), channel_id=1, source_target_pairs={{0,4},{4,8},{8,12},{12,0},{1,5},{5,9},{9,13},{13,1},{2,6},{6,10},{... | collective-permute-start | bytes 208904 | tf_op jit(solution)/shard_map/ppermute | solution.py:303
  33.3 3.3 %collective-permute-start.6 = (bf16[272,128]{1,0:T(8,128)(2,1)S(1)}, bf16[272,128]{1,0:T(8,128)(2,1)S(1)}, u32[]{:S(2)}, u32[]{:S(2)}) collective-permute-start(bf16[272,128]{1,0:T(8,128)(2,1)S(1)} %get-tuple-element.35), channel_id=1, source_target_pairs={{0,12},{4,0},{8,4},{12,8},{1,13},{5,1},{9,5},{13,9},{2,14},{6,2},{... | collective-permute-start | bytes 208904 | tf_op jit(solution)/shard_map/ppermute | solution.py:303
  36.6 0.0 collective-permute-start.10
  36.7 0.2 collective-permute-done.4.rest_0_
  36.9 0.3 collective-permute-start.7
  37.2 2.2 %collective-permute-done.5.rest_1_ = bf16[272,128]{1,0:T(8,128)(2,1)S(1)} collective-permute-done((bf16[272,128]{1,0:T(8,128)(2,1)S(1)}, bf16[272,128]{1,0:T(8,128)(2,1)S(1)}, u32[]{:S(2)}, u32[]{:S(2)}) %collective-permute-start.5) | collective-permute-done | bytes 69664 | tf_op jit(solution)/shard_map/ppermute | solution.py:303
  39.4 0.0 collective-permute-start.8
  39.4 0.4 collective-permute-done.6.rest_2_
  39.7 0.1 collective-permute-start.9
  39.9 0.0 collective-permute-done.10.rest_7_
  39.9 0.0 collective-permute-done.7.rest_4_
  39.9 0.7 %collective-permute-done.8.rest_5_ = bf16[272,128]{1,0:T(8,128)(2,1)S(1)} collective-permute-done((bf16[272,128]{1,0:T(8,128)(2,1)S(1)}, bf16[272,128]{1,0:T(8,128)(2,1)S(1)}, u32[]{:S(2)}, u32[]{:S(2)}) %collective-permute-start.8) | collective-permute-done | bytes 69664 | tf_op jit(solution)/shard_map/ppermute | solution.py:291
  40.6 0.4 collective-permute-done.9.rest_6_
  41.0 1.5 %assemble.1 = f32[24,128,128]{2,1,0:T(8,128)} custom-call(bf16[272,128]{1,0:T(8,128)(2,1)S(1)} %collective-permute-done.4.rest_0_, bf16[272,128]{1,0:T(8,128)(2,1)S(1)} %collective-permute-done.5.rest_1_, bf16[272,128]{1,0:T(8,128)(2,1)S(1)} %collective-permute-done.6.rest_2_, bf16[272,128]{1,0:T(8,128)(2,1)S(1)} %get-tuple-element.36.rest_3_, ...), custom_call_target="tpu_custom_call" | custom-call | tf_op jit(solution)/shard_map/assemble/pallas_call | solution.py:307
  (2 shorter events, 0.0 us)
Async XLA Ops:
  1.1 11.6 %collective-permute-start = (bf16[8,1,128,128]{3,2,0,1:T(8,128)(2,1)S(1)}, bf16[8,1,128,128]{3,2,0,1:T(8,128)(2,1)S(1)}, u32[]{:S(2)}, u32[]{:S(2)}) collective-permute-start(bf16[8,1,128,128]{3,2,0,1:T(8,128)(2,1)S(1)} %bitcast.14), channel_id=1, source_target_pairs={{2,0},{0,2},{3,1},{1,3},{6,4},{4,6},{7,5},{5,7},{10,8},{8,10},{11,... | collective-permute-start | bytes 786440 | tf_op jit(solution)/shard_map/ppermute | solution.py:230
  4.2 10.6 %copy-start = (bf16[32,1,128,128]{3,2,1,0:T(8,128)(2,1)S(1)}, bf16[32,1,128,128]{3,2,1,0:T(8,128)(2,1)}, u32[]{:S(2)}) copy-start(bf16[32,1,128,128]{3,2,1,0:T(8,128)(2,1)} %left.3) | copy-start | bytes 3145732
  4.2 10.6 %copy-start.1 = (s32[32,24]{0,1:T(8,128)S(1)}, s32[32,24]{0,1:T(8,128)}, u32[]{:S(2)}) copy-start(s32[32,24]{0,1:T(8,128)} %param.12) | copy-start | bytes 9220
  4.2 18.2 %collective-permute-start.2 = (bf16[16,1,128,128]{3,2,0,1:T(8,128)(2,1)S(1)}, bf16[16,1,128,128]{3,2,0,1:T(8,128)(2,1)S(1)}, u32[]{:S(2)}, u32[]{:S(2)}) collective-permute-start(bf16[16,1,128,128]{3,2,0,1:T(8,128)(2,1)S(1)} %bitcast.13), channel_id=1, source_target_pairs={{2,0},{0,2},{3,1},{1,3},{6,4},{4,6},{7,5},{5,7},{10,8},{8,10},{11,... | collective-permute-start | bytes 1572872 | tf_op jit(solution)/shard_map/ppermute | solution.py:230
  12.7 9.6 %collective-permute-start.1 = (bf16[8,1,128,128]{3,2,0,1:T(8,128)(2,1)S(1)}, bf16[8,1,128,128]{3,2,0,1:T(8,128)(2,1)S(1)}, u32[]{:S(2)}, u32[]{:S(2)}) collective-permute-start(bf16[8,1,128,128]{3,2,0,1:T(8,128)(2,1)S(1)} %collective-permute-done), channel_id=1, source_target_pairs={{0,4},{4,0},{8,12},{12,8},{1,5},{5,1},{9,13},{13,9},{2,6},{6,2},{1... | collective-permute-start | bytes 786440 | tf_op jit(solution)/shard_map/ppermute | solution.py:267
  22.3 5.6 %copy-start.2 = (s32[1,1,16]{2,1,0:T(1,128)S(1)}, s32[1,1,16]{2,1,0:T(1,128)}, u32[]{:S(2)}) copy-start(s32[1,1,16]{2,1,0:T(1,128)} %slot_target.1) | copy-start | bytes 196
  26.4 1.6 %collective-permute-start.3 = (bf16[8,128,128]{2,1,0:T(8,128)(2,1)S(1)}, bf16[8,128,128]{2,1,0:T(8,128)(2,1)S(1)}, u32[]{:S(2)}, u32[]{:S(2)}) collective-permute-start(bf16[8,128,128]{2,1,0:T(8,128)(2,1)S(1)} %get-tuple-element.32), channel_id=1, source_target_pairs={{0,1},{1,0},{2,3},{3,2},{4,5},{5,4},{6,7},{7,6},{8,9},{9,8},{10,11... | collective-permute-start | bytes 786440 | tf_op jit(solution)/shard_map/ppermute | solution.py:291
  28.6 8.3 %collective-permute-start.4 = (bf16[272,128]{1,0:T(8,128)(2,1)S(1)}, bf16[272,128]{1,0:T(8,128)(2,1)S(1)}, u32[]{:S(2)}, u32[]{:S(2)}) collective-permute-start(bf16[272,128]{1,0:T(8,128)(2,1)S(1)} %get-tuple-element.33), channel_id=1, source_target_pairs={{0,8},{4,12},{8,0},{12,4},{1,9},{5,13},{9,1},{13,5},{2,10},{6,14},... | collective-permute-start | bytes 208904 | tf_op jit(solution)/shard_map/ppermute | solution.py:303
  32.8 6.5 %collective-permute-start.5 = (bf16[272,128]{1,0:T(8,128)(2,1)S(1)}, bf16[272,128]{1,0:T(8,128)(2,1)S(1)}, u32[]{:S(2)}, u32[]{:S(2)}) collective-permute-start(bf16[272,128]{1,0:T(8,128)(2,1)S(1)} %get-tuple-element.34), channel_id=1, source_target_pairs={{0,4},{4,8},{8,12},{12,0},{1,5},{5,9},{9,13},{13,1},{2,6},{6,10},{... | collective-permute-start | bytes 208904 | tf_op jit(solution)/shard_map/ppermute | solution.py:303
  33.3 6.4 %collective-permute-start.6 = (bf16[272,128]{1,0:T(8,128)(2,1)S(1)}, bf16[272,128]{1,0:T(8,128)(2,1)S(1)}, u32[]{:S(2)}, u32[]{:S(2)}) collective-permute-start(bf16[272,128]{1,0:T(8,128)(2,1)S(1)} %get-tuple-element.35), channel_id=1, source_target_pairs={{0,12},{4,0},{8,4},{12,8},{1,13},{5,1},{9,5},{13,9},{2,14},{6,2},{... | collective-permute-start | bytes 208904 | tf_op jit(solution)/shard_map/ppermute | solution.py:303
  36.6 3.2 %collective-permute-start.10 = (bf16[272,128]{1,0:T(8,128)(2,1)S(1)}, bf16[272,128]{1,0:T(8,128)(2,1)S(1)}, u32[]{:S(2)}, u32[]{:S(2)}) collective-permute-start(bf16[272,128]{1,0:T(8,128)(2,1)S(1)} %get-tuple-element.36.rest_3_), channel_id=1, source_target_pairs={{0,1},{1,0},{2,3},{3,2},{4,5},{5,4},{6,7},{7,6},{8,9},{9,8},{10,11... | collective-permute-start | bytes 208904 | tf_op jit(solution)/shard_map/ppermute | solution.py:291
  36.9 3.0 %collective-permute-start.7 = (bf16[272,128]{1,0:T(8,128)(2,1)S(1)}, bf16[272,128]{1,0:T(8,128)(2,1)S(1)}, u32[]{:S(2)}, u32[]{:S(2)}) collective-permute-start(bf16[272,128]{1,0:T(8,128)(2,1)S(1)} %collective-permute-done.4.rest_0_), channel_id=1, source_target_pairs={{0,1},{1,0},{2,3},{3,2},{4,5},{5,4},{6,7},{7,6},{8,9},{9,8},{10,11... | collective-permute-start | bytes 208904 | tf_op jit(solution)/shard_map/ppermute | solution.py:291
  39.4 1.3 %collective-permute-start.8 = (bf16[272,128]{1,0:T(8,128)(2,1)S(1)}, bf16[272,128]{1,0:T(8,128)(2,1)S(1)}, u32[]{:S(2)}, u32[]{:S(2)}) collective-permute-start(bf16[272,128]{1,0:T(8,128)(2,1)S(1)} %collective-permute-done.5.rest_1_), channel_id=1, source_target_pairs={{0,1},{1,0},{2,3},{3,2},{4,5},{5,4},{6,7},{7,6},{8,9},{9,8},{10,11... | collective-permute-start | bytes 208904 | tf_op jit(solution)/shard_map/ppermute | solution.py:291
  39.7 1.3 %collective-permute-start.9 = (bf16[272,128]{1,0:T(8,128)(2,1)S(1)}, bf16[272,128]{1,0:T(8,128)(2,1)S(1)}, u32[]{:S(2)}, u32[]{:S(2)}) collective-permute-start(bf16[272,128]{1,0:T(8,128)(2,1)S(1)} %collective-permute-done.6.rest_2_), channel_id=1, source_target_pairs={{0,1},{1,0},{2,3},{3,2},{4,5},{5,4},{6,7},{7,6},{8,9},{9,8},{10,11... | collective-permute-start | bytes 208904 | tf_op jit(solution)/shard_map/ppermute | solution.py:291

commit v14 on v13

--- a/solution.py
+++ b/solution.py
@@ -223,7 +223,7 @@
         return pl.CostEstimate(flops=flops, bytes_accessed=4 * 2**20, transcendentals=0)
 
     assert rows % 2 == 0
-    quarter = operators // 4
+    quarter = operators * 9 // 32
     swap = [(i, i ^ 1) for i in range(rows)]
 
     def over_blocks(part):

time: 42.1 us -> 40.8 us (0.969); the launches traced: 42.5 us -> 40.6 us
  starting transfers between devices: 13.7 us -> 11.7 us
    ppermute x3, starting transfers between devices: 8.07 us -> 6.3 us  [shards(): lax.ppermute(block, 'sector', [(i, (i + d) % rows) for i in range(rows)])]
    pallas_call x1, Pallas kernels: 7.55 us -> 6.74 us  [shards(): pl.pallas_call(own_kernel, out_shape=[jax.ShapeDtypeStruct(total_shape, j...]
    pallas_call x1, Pallas kernels: 4 us -> 4.8 us  [shards(): pl.pallas_call(functools.partial(other_kernel, rows, sets), out_shape=[ja...]
  transfers between devices with their start and end apart: 11 -> 11, of which waited for: 6 -> 6; matrix products, arithmetic and copies ran while one was open for 0% -> 0% of each run, Pallas kernels for 38% -> 37%
where the time goes in v14:
time: 40.8 us; the launch traced here: 40.6 us
  Pallas kernels  23.2 us (57%)
  starting transfers between devices  11.7 us (29%)
  waiting for transfers between devices  5.52 us (14%)
    pallas_call x1, Pallas kernels, shards(): pl.pallas_call(functools.partial(right_kernel, blocks, left_local), out_s...  8.47 us
    pallas_call x1, Pallas kernels, shards(): pl.pallas_call(own_kernel, out_shape=[jax.ShapeDtypeStruct(total_shape, j...  6.74 us
    ppermute x3, starting transfers between devices, shards(): lax.ppermute(block, 'sector', [(i, (i + d) % rows) for i in range(rows)])  6.3 us
    pallas_call x1, Pallas kernels, shards(): pl.pallas_call(functools.partial(other_kernel, rows, sets), out_shape=[ja...  4.8 us
    ppermute x2, starting transfers between devices, over_blocks(): lax.ppermute(part, 'blk', [((b + d) % blocks, b) for b in range(blocks)])  3.1 us
    ppermute x3, waiting for transfers between devices, shards(): lax.ppermute(block, 'sector', [(i, (i + d) % rows) for i in range(rows)])  2.97 us
    ppermute x5, waiting for transfers between devices, over_cores(): lax.ppermute(block, 'op', [(h, halves - 1 - h) for h in range(halves)])  2.54 us
    ppermute x1, starting transfers between devices, shards(): swapped = [lax.ppermute(part, 'sector', swap) for part in direct]  2.01 us
  transfers between devices with their start and end apart: 11, of which 6 were waited for; matrix products, arithmetic and copies ran while one was open for 0% of the time, Pallas kernels for 37%

profile of v14, /device:TPU:0, one launch (start us, length us, event | category | flops | bytes accessed | tf_op | source)
XLA Modules:
  0.0 40.6 jit_solution(17734866121613663103)
XLA Ops:
  0.0 1.1 %cut_left.1 = (bf16[9,1,128,128]{3,2,1,0:T(8,128)(2,1)S(1)}, bf16[14,1,128,128]{3,2,1,0:T(8,128)(2,1)S(1)}) custom-call(bf16[32,1,128,128]{3,2,1,0:T(8,128)(2,1)} %left.3), custom_call_target="tpu_custom_call" | custom-call | tf_op jit(solution)/shard_map/cut_left/pallas_call | solution.py:232
  1.1 3.0 %collective-permute-start = (bf16[9,1,128,128]{3,2,0,1:T(8,128)(2,1)S(1)}, bf16[9,1,128,128]{3,2,0,1:T(8,128)(2,1)S(1)}, u32[]{:S(2)}, u32[]{:S(2)}) collective-permute-start(bf16[9,1,128,128]{3,2,0,1:T(8,128)(2,1)S(1)} %bitcast.14), channel_id=1, source_target_pairs={{2,0},{0,2},{3,1},{1,3},{6,4},{4,6},{7,5},{5,7},{10,8},{8,10},{11,... | collective-permute-start | bytes 884744 | tf_op jit(solution)/shard_map/ppermute | solution.py:230
  4.1 0.1 collective-permute-start.2
  4.2 8.5 %right_side.1 = (bf16[6,32,2,128,256]{4,3,2,1,0:T(8,128)(2,1)S(1)}, s32[28]{0:T(128)S(1)}) custom-call(s32[24]{0:T(128)} %left_qn_in.1, s32[24]{0:T(128)} %right_qn_in.1, bf16[24,128,128]{2,1,0:T(8,128)(2,1)} %psi_in.1, bf16[32,2,128,128]{3,2,1,0:T(8,128)(2,1)} %right_in.1), custom_call_target="tpu_custom_call" | custom-call | flops 12884901888 | bytes 4194304 | tf_op jit(solution)/shard_map/right_side/pallas_call | solution.py:246
  12.7 0.0 collective-permute-done
  12.7 2.0 %collective-permute-start.1 = (bf16[9,1,128,128]{3,2,0,1:T(8,128)(2,1)S(1)}, bf16[9,1,128,128]{3,2,0,1:T(8,128)(2,1)S(1)}, u32[]{:S(2)}, u32[]{:S(2)}) collective-permute-start(bf16[9,1,128,128]{3,2,0,1:T(8,128)(2,1)S(1)} %collective-permute-done), channel_id=1, source_target_pairs={{0,4},{4,0},{8,12},{12,8},{1,5},{5,1},{9,13},{13,9},{2,6},{6,2},{1... | collective-permute-start | bytes 884744 | tf_op jit(solution)/shard_map/ppermute | solution.py:267
  14.7 0.0 copy-done
  14.7 0.0 copy-done.1
  14.7 6.7 %own_left.1 = (f32[17,128,128]{2,1,0:T(8,128)S(1)}, f32[17,128,128]{2,1,0:T(8,128)S(1)}, f32[17,128,128]{2,1,0:T(8,128)S(1)}, f32[17,128,128]{2,1,0:T(8,128)S(1)}) custom-call(s32[28]{0:T(128)S(1)} %get-tuple-element.21.plan, s32[24,32]{1,0:T(8,128)S(1)} %bitcast.11, bf16[6,32,2,128,256]{4,3,2,1,0:T(8,128)(2,1)S(1)} %get-tuple-element.24.half, ...), custom_call_target="tpu_custom_call" | custom-call | flops 6442450944 | bytes 4194304 | tf_op jit(solution)/shard_map/own_left/pallas_call | solution.py:268
  21.5 0.0 collective-permute-done.2
  21.5 0.0 collective-permute-done.1
  21.5 0.0 copy-start.2
  21.5 4.8 %other_left.1 = (f32[17,128,128]{2,1,0:T(8,128)S(1)}, f32[17,128,128]{2,1,0:T(8,128)S(1)}, f32[17,128,128]{2,1,0:T(8,128)S(1)}, f32[17,128,128]{2,1,0:T(8,128)S(...) custom-call(s32[28]{0:T(128)S(1)} %get-tuple-element.21.plan, ...), custom_call_target="tpu_custom_call", output_to_operand_aliasing={{0}: (5, {}), {1}: (6, {}), {2}: (7, {}), {3}: (8, {})} | custom-call | flops 6442450944 | bytes 4194304 | tf_op jit(solution)/shard_map/other_left/pallas_call | solution.py:277
  26.3 0.1 collective-permute-start.3
  26.4 1.5 %collective-permute-done.3.taken = bf16[8,128,128]{2,1,0:T(8,128)(2,1)S(1)} collective-permute-done((bf16[8,128,128]{2,1,0:T(8,128)(2,1)S(1)}, bf16[8,128,128]{2,1,0:T(8,128)(2,1)S(1)}, u32[]{:S(2)}, u32[]{:S(2)}) %collective-permute-start.3) | collective-permute-done | bytes 262176 | tf_op jit(solution)/shard_map/ppermute | solution.py:291
  27.9 0.0 copy-done.2
  27.9 0.6 %combine.1 = (bf16[272,128]{1,0:T(8,128)(2,1)S(1)}, bf16[272,128]{1,0:T(8,128)(2,1)S(1)}, bf16[272,128]{1,0:T(8,128)(2,1)S(1)}, bf16[272,128]{1,0:T(8,128)(2,1)S(1)}) custom-call(s32[1,1,16]{2,1,0:T(1,128)S(1)} %copy-done.2, f32[8,128,128]{2,1,0:T(8,128)S(1)} %get-tuple-element.31.keep, bf16[8,128,128]{2,1,0:T(8,128)(2,1)S(1)} %collective-permute-done.3.taken), custom_call_target="tpu_custom_call" | custom-call | tf_op jit(solution)/shard_map/combine/pallas_call | solution.py:294
  28.6 2.5 %collective-permute-start.4 = (bf16[272,128]{1,0:T(8,128)(2,1)S(1)}, bf16[272,128]{1,0:T(8,128)(2,1)S(1)}, u32[]{:S(2)}, u32[]{:S(2)}) collective-permute-start(bf16[272,128]{1,0:T(8,128)(2,1)S(1)} %get-tuple-element.33), channel_id=1, source_target_pairs={{0,8},{4,12},{8,0},{12,4},{1,9},{5,13},{9,1},{13,5},{2,10},{6,14},... | collective-permute-start | bytes 208904 | tf_op jit(solution)/shard_map/ppermute | solution.py:303
  31.0 0.7 %collective-permute-start.5 = (bf16[272,128]{1,0:T(8,128)(2,1)S(1)}, bf16[272,128]{1,0:T(8,128)(2,1)S(1)}, u32[]{:S(2)}, u32[]{:S(2)}) collective-permute-start(bf16[272,128]{1,0:T(8,128)(2,1)S(1)} %get-tuple-element.34), channel_id=1, source_target_pairs={{0,4},{4,8},{8,12},{12,0},{1,5},{5,9},{9,13},{13,1},{2,6},{6,10},{... | collective-permute-start | bytes 208904 | tf_op jit(solution)/shard_map/ppermute | solution.py:303
  31.7 3.1 %collective-permute-start.6 = (bf16[272,128]{1,0:T(8,128)(2,1)S(1)}, bf16[272,128]{1,0:T(8,128)(2,1)S(1)}, u32[]{:S(2)}, u32[]{:S(2)}) collective-permute-start(bf16[272,128]{1,0:T(8,128)(2,1)S(1)} %get-tuple-element.35), channel_id=1, source_target_pairs={{0,12},{4,0},{8,4},{12,8},{1,13},{5,1},{9,5},{13,9},{2,14},{6,2},{... | collective-permute-start | bytes 208904 | tf_op jit(solution)/shard_map/ppermute | solution.py:303
  34.9 0.0 collective-permute-start.10
  34.9 2.0 %collective-permute-done.4.rest_0_ = bf16[272,128]{1,0:T(8,128)(2,1)S(1)} collective-permute-done((bf16[272,128]{1,0:T(8,128)(2,1)S(1)}, bf16[272,128]{1,0:T(8,128)(2,1)S(1)}, u32[]{:S(2)}, u32[]{:S(2)}) %collective-permute-start.4) | collective-permute-done | bytes 69664 | tf_op jit(solution)/shard_map/ppermute | solution.py:303
  36.9 0.0 collective-permute-start.7
  36.9 0.7 %collective-permute-done.5.rest_1_ = bf16[272,128]{1,0:T(8,128)(2,1)S(1)} collective-permute-done((bf16[272,128]{1,0:T(8,128)(2,1)S(1)}, bf16[272,128]{1,0:T(8,128)(2,1)S(1)}, u32[]{:S(2)}, u32[]{:S(2)}) %collective-permute-start.5) | collective-permute-done | bytes 69664 | tf_op jit(solution)/shard_map/ppermute | solution.py:303
  37.6 0.0 collective-permute-start.8
  37.6 0.3 collective-permute-done.6.rest_2_
  37.8 0.2 collective-permute-start.9
  38.1 0.0 collective-permute-done.10.rest_7_
  38.1 0.0 collective-permute-done.7.rest_4_
  38.1 0.7 %collective-permute-done.8.rest_5_ = bf16[272,128]{1,0:T(8,128)(2,1)S(1)} collective-permute-done((bf16[272,128]{1,0:T(8,128)(2,1)S(1)}, bf16[272,128]{1,0:T(8,128)(2,1)S(1)}, u32[]{:S(2)}, u32[]{:S(2)}) %collective-permute-start.8) | collective-permute-done | bytes 69664 | tf_op jit(solution)/shard_map/ppermute | solution.py:291
  38.8 0.3 collective-permute-done.9.rest_6_
  39.1 1.5 %assemble.1 = f32[24,128,128]{2,1,0:T(8,128)} custom-call(bf16[272,128]{1,0:T(8,128)(2,1)S(1)} %collective-permute-done.4.rest_0_, bf16[272,128]{1,0:T(8,128)(2,1)S(1)} %collective-permute-done.5.rest_1_, bf16[272,128]{1,0:T(8,128)(2,1)S(1)} %collective-permute-done.6.rest_2_, bf16[272,128]{1,0:T(8,128)(2,1)S(1)} %get-tuple-element.36.rest_3_, ...), custom_call_target="tpu_custom_call" | custom-call | tf_op jit(solution)/shard_map/assemble/pallas_call | solution.py:307
  (2 shorter events, 0.0 us)
Async XLA Ops:
  1.1 11.6 %collective-permute-start = (bf16[9,1,128,128]{3,2,0,1:T(8,128)(2,1)S(1)}, bf16[9,1,128,128]{3,2,0,1:T(8,128)(2,1)S(1)}, u32[]{:S(2)}, u32[]{:S(2)}) collective-permute-start(bf16[9,1,128,128]{3,2,0,1:T(8,128)(2,1)S(1)} %bitcast.14), channel_id=1, source_target_pairs={{2,0},{0,2},{3,1},{1,3},{6,4},{4,6},{7,5},{5,7},{10,8},{8,10},{11,... | collective-permute-start | bytes 884744 | tf_op jit(solution)/shard_map/ppermute | solution.py:230
  4.1 10.6 %copy-start = (bf16[32,1,128,128]{3,2,1,0:T(8,128)(2,1)S(1)}, bf16[32,1,128,128]{3,2,1,0:T(8,128)(2,1)}, u32[]{:S(2)}) copy-start(bf16[32,1,128,128]{3,2,1,0:T(8,128)(2,1)} %left.3) | copy-start | bytes 3145732
  4.1 10.6 %copy-start.1 = (s32[32,24]{0,1:T(8,128)S(1)}, s32[32,24]{0,1:T(8,128)}, u32[]{:S(2)}) copy-start(s32[32,24]{0,1:T(8,128)} %param.12) | copy-start | bytes 9220
  4.1 17.4 %collective-permute-start.2 = (bf16[14,1,128,128]{3,2,0,1:T(8,128)(2,1)S(1)}, bf16[14,1,128,128]{3,2,0,1:T(8,128)(2,1)S(1)}, u32[]{:S(2)}, u32[]{:S(2)}) collective-permute-start(bf16[14,1,128,128]{3,2,0,1:T(8,128)(2,1)S(1)} %bitcast.13), channel_id=1, source_target_pairs={{2,0},{0,2},{3,1},{1,3},{6,4},{4,6},{7,5},{5,7},{10,8},{8,10},{11,... | collective-permute-start | bytes 1376264 | tf_op jit(solution)/shard_map/ppermute | solution.py:230
  12.7 8.8 %collective-permute-start.1 = (bf16[9,1,128,128]{3,2,0,1:T(8,128)(2,1)S(1)}, bf16[9,1,128,128]{3,2,0,1:T(8,128)(2,1)S(1)}, u32[]{:S(2)}, u32[]{:S(2)}) collective-permute-start(bf16[9,1,128,128]{3,2,0,1:T(8,128)(2,1)S(1)} %collective-permute-done), channel_id=1, source_target_pairs={{0,4},{4,0},{8,12},{12,8},{1,5},{5,1},{9,13},{13,9},{2,6},{6,2},{1... | collective-permute-start | bytes 884744 | tf_op jit(solution)/shard_map/ppermute | solution.py:267
  21.5 6.4 %copy-start.2 = (s32[1,1,16]{2,1,0:T(1,128)S(1)}, s32[1,1,16]{2,1,0:T(1,128)}, u32[]{:S(2)}) copy-start(s32[1,1,16]{2,1,0:T(1,128)} %slot_target.1) | copy-start | bytes 196
  26.3 1.6 %collective-permute-start.3 = (bf16[8,128,128]{2,1,0:T(8,128)(2,1)S(1)}, bf16[8,128,128]{2,1,0:T(8,128)(2,1)S(1)}, u32[]{:S(2)}, u32[]{:S(2)}) collective-permute-start(bf16[8,128,128]{2,1,0:T(8,128)(2,1)S(1)} %get-tuple-element.32), channel_id=1, source_target_pairs={{0,1},{1,0},{2,3},{3,2},{4,5},{5,4},{6,7},{7,6},{8,9},{9,8},{10,11... | collective-permute-start | bytes 786440 | tf_op jit(solution)/shard_map/ppermute | solution.py:291
  28.6 8.3 %collective-permute-start.4 = (bf16[272,128]{1,0:T(8,128)(2,1)S(1)}, bf16[272,128]{1,0:T(8,128)(2,1)S(1)}, u32[]{:S(2)}, u32[]{:S(2)}) collective-permute-start(bf16[272,128]{1,0:T(8,128)(2,1)S(1)} %get-tuple-element.33), channel_id=1, source_target_pairs={{0,8},{4,12},{8,0},{12,4},{1,9},{5,13},{9,1},{13,5},{2,10},{6,14},... | collective-permute-start | bytes 208904 | tf_op jit(solution)/shard_map/ppermute | solution.py:303
  31.0 6.5 %collective-permute-start.5 = (bf16[272,128]{1,0:T(8,128)(2,1)S(1)}, bf16[272,128]{1,0:T(8,128)(2,1)S(1)}, u32[]{:S(2)}, u32[]{:S(2)}) collective-permute-start(bf16[272,128]{1,0:T(8,128)(2,1)S(1)} %get-tuple-element.34), channel_id=1, source_target_pairs={{0,4},{4,8},{8,12},{12,0},{1,5},{5,9},{9,13},{13,1},{2,6},{6,10},{... | collective-permute-start | bytes 208904 | tf_op jit(solution)/shard_map/ppermute | solution.py:303
  31.7 6.1 %collective-permute-start.6 = (bf16[272,128]{1,0:T(8,128)(2,1)S(1)}, bf16[272,128]{1,0:T(8,128)(2,1)S(1)}, u32[]{:S(2)}, u32[]{:S(2)}) collective-permute-start(bf16[272,128]{1,0:T(8,128)(2,1)S(1)} %get-tuple-element.35), channel_id=1, source_target_pairs={{0,12},{4,0},{8,4},{12,8},{1,13},{5,1},{9,5},{13,9},{2,14},{6,2},{... | collective-permute-start | bytes 208904 | tf_op jit(solution)/shard_map/ppermute | solution.py:303
  34.9 3.2 %collective-permute-start.10 = (bf16[272,128]{1,0:T(8,128)(2,1)S(1)}, bf16[272,128]{1,0:T(8,128)(2,1)S(1)}, u32[]{:S(2)}, u32[]{:S(2)}) collective-permute-start(bf16[272,128]{1,0:T(8,128)(2,1)S(1)} %get-tuple-element.36.rest_3_), channel_id=1, source_target_pairs={{0,1},{1,0},{2,3},{3,2},{4,5},{5,4},{6,7},{7,6},{8,9},{9,8},{10,11... | collective-permute-start | bytes 208904 | tf_op jit(solution)/shard_map/ppermute | solution.py:291
  36.9 1.3 %collective-permute-start.7 = (bf16[272,128]{1,0:T(8,128)(2,1)S(1)}, bf16[272,128]{1,0:T(8,128)(2,1)S(1)}, u32[]{:S(2)}, u32[]{:S(2)}) collective-permute-start(bf16[272,128]{1,0:T(8,128)(2,1)S(1)} %collective-permute-done.4.rest_0_), channel_id=1, source_target_pairs={{0,1},{1,0},{2,3},{3,2},{4,5},{5,4},{6,7},{7,6},{8,9},{9,8},{10,11... | collective-permute-start | bytes 208904 | tf_op jit(solution)/shard_map/ppermute | solution.py:291
  37.6 1.3 %collective-permute-start.8 = (bf16[272,128]{1,0:T(8,128)(2,1)S(1)}, bf16[272,128]{1,0:T(8,128)(2,1)S(1)}, u32[]{:S(2)}, u32[]{:S(2)}) collective-permute-start(bf16[272,128]{1,0:T(8,128)(2,1)S(1)} %collective-permute-done.5.rest_1_), channel_id=1, source_target_pairs={{0,1},{1,0},{2,3},{3,2},{4,5},{5,4},{6,7},{7,6},{8,9},{9,8},{10,11... | collective-permute-start | bytes 208904 | tf_op jit(solution)/shard_map/ppermute | solution.py:291
  37.8 1.3 %collective-permute-start.9 = (bf16[272,128]{1,0:T(8,128)(2,1)S(1)}, bf16[272,128]{1,0:T(8,128)(2,1)S(1)}, u32[]{:S(2)}, u32[]{:S(2)}) collective-permute-start(bf16[272,128]{1,0:T(8,128)(2,1)S(1)} %collective-permute-done.6.rest_2_), channel_id=1, source_target_pairs={{0,1},{1,0},{2,3},{3,2},{4,5},{5,4},{6,7},{7,6},{8,9},{9,8},{10,11... | collective-permute-start | bytes 208904 | tf_op jit(solution)/shard_map/ppermute | solution.py:291
